TPU v7x, 32 devices: a whole 2x2x4 slice. The times are simulated.
32 devices in a mesh: member: 2 (over y), lat: 4 (over z), lon: 2 (over x), lev: 2 (over core).
Axes of the slice: x: 2, y: 2, z: 4, core: 2. Of those that a mesh axis runs over, the one named last changes fastest.
Arguments:
- control: float32 [4, 448, 1024], P('lev', ('member', 'lat'), 'lon'), parts along dimension 1, may hold values from -6 to 6
- vertical: float32 [4, 4], replicated, may hold values from -3 to 3
- spread: float32 [4, 224, 1024], P('lev', 'lat', 'lon'), may hold values from 0.4 to 1
- error_scale: float32 [4, 224, 1024], P('lev', 'lat', 'lon'), may hold values from 0.3 to 6
- wind_lon: float32 [4, 448, 1024], P('lev', ('member', 'lat'), 'lon'), parts along dimension 1, may hold values from -0.6 to 0.6
- wind_lat: float32 [4, 448, 1024], P('lev', ('member', 'lat'), 'lon'), parts along dimension 1, may hold values from -0.6 to 0.6
- obs_block: int32 [2, 4, 2, 8, 2], P('lev', 'lat', 'lon'), may hold values from 0 to 447
- obs_platform: int32 [2, 4, 2, 8, 2], P('lev', 'lat', 'lon'), may hold values from 0 to 7
- obs_count: int32 [2, 4, 2, 8], P('lev', 'lat', 'lon'), may hold values from 1 to 2, as said below
- interp: float32 [2, 4, 2, 8, 2, 128, 128], P('lev', 'lat', 'lon'), may hold values from -0.5 to 0.5
- innovation: float32 [2, 8, 2, 8, 2, 128], P('lev', ('member', 'lat'), 'lon'), parts along dimension 1, may hold values from -6 to 6
- error_inverse: float32 [4, 2, 8, 128, 128], P('lat', 'lon'), may hold values from -0.8 to 4.8
- previous_direction: float32 [4, 448, 1024], P('lev', ('member', 'lat'), 'lon'), parts along dimension 1, may hold values from -6 to 6
- previous_square: float32 [2], P('member'), parts along dimension 0, may hold values from 0.5 to 2
Outputs:
- gradient: float32 [4, 448, 1024], P('lev', ('member', 'lat'), 'lon'), parts along dimension 1
- direction: float32 [4, 448, 1024], P('lev', ('member', 'lat'), 'lon'), parts along dimension 1
There are 2 independent parts, one for each index of `member`. A program takes and returns all parts, laid end to end along the dimension named above; an argument that names none is the same for every part. Nothing has to cross between parts.
Inputs may be any that keep to these rules, and one draw needn't show every extreme that they name: The first obs_count slots toward an owner are used; at most 2 go from one tile to one owner.
All inputs are finite; a program needn't handle non-finite values.
Results may differ from a plain program's by a relative error of at most 0.00013.
Values sent between devices are 32-bit elements; how exact they have to be, the bound alone decides.
No kernel may reach another device: no remote copies, remote signals or barrier semaphores. Data moves between devices by JAX's collectives and lax.ppermute only.
A program may use at most 64 MiB of HBM per device.

v0:
```python
import jax
import jax.numpy as jnp
from jax import lax
from jax.sharding import PartitionSpec as P

FILTER = 2


highest = lax.Precision.HIGHEST
smoothing = 0.1
diffusion = 0.15


def padded_2(cells, sides, width, closed):
    for axis, dim in sides:
        count = lax.axis_size(axis)
        ends = count if closed else count - 1
        head = lax.slice_in_dim(cells, 0, width, axis=dim)
        tail = lax.slice_in_dim(cells, cells.shape[dim] - width, cells.shape[dim], axis=dim)
        cells = jnp.concatenate(
            [
                lax.ppermute(tail, axis, [(i, (i + 1) % count) for i in range(ends)]),
                cells,
                lax.ppermute(head, axis, [((i + 1) % count, i) for i in range(ends)]),
            ],
            axis=dim,
        )
    return cells


def with_rim(stacked, rim_width):
    wide = padded_2(stacked, (("lon", 3),), rim_width, True)
    return padded_2(wide, (("lat", 2),), rim_width, False)


def beside_all(padded, north, east):
    height = padded.shape[-2]
    breadth = padded.shape[-1]
    return padded[..., 1 + north : height - 1 + north, 1 + east : breadth - 1 + east]


def laplace(padded):
    return (
        beside_all(padded, 1, 0)
        + beside_all(padded, -1, 0)
        + beside_all(padded, 0, 1)
        + beside_all(padded, 0, -1)
        - 4.0 * beside_all(padded, 0, 0)
    )


def smooth(field_now, spread):
    for repeat in range(FILTER):
        padded = with_rim((spread * field_now)[None], 1)[0]
        field_now = field_now + smoothing * spread * laplace(padded)
    return field_now


def advance(padded, centre, wind_e, wind_n):
    return (
        centre
        - 0.5 * wind_e * (beside_all(padded, 0, 1) - beside_all(padded, 0, -1))
        - 0.5 * wind_n * (beside_all(padded, 1, 0) - beside_all(padded, -1, 0))
        + diffusion * laplace(padded)
    )


def retreat(field_now, wind_e, wind_n):
    padded = with_rim(jnp.stack([wind_e * field_now, wind_n * field_now, field_now]), 1)
    east_part = beside_all(padded[0], 0, 1) - beside_all(padded[0], 0, -1)
    north_part = beside_all(padded[1], 1, 0) - beside_all(padded[1], -1, 0)
    return field_now + 0.5 * east_part + 0.5 * north_part + diffusion * laplace(padded[2])


def all_layers(field_now):
    return lax.all_gather(field_now, "lev", axis=0, tiled=True)


def weigh_obs(arrived, platforms, error_inverse):
    matrices = error_inverse.reshape(error_inverse.shape[-3:])
    plat_count = matrices.shape[0]
    products = jnp.einsum("pij,osj->posi", matrices, arrived, precision=highest)
    selector = (platforms[None] == jnp.arange(plat_count, dtype=jnp.int32)[:, None, None]).astype(
        jnp.float32
    )
    return jnp.sum(selector[..., None] * products, axis=0)


def local(
    control,
    vertical,
    spread,
    error_scale,
    wind_lon,
    wind_lat,
    obs_block,
    obs_platform,
    obs_count,
    interp,
    innovation,
    error_inverse,
    previous_direction,
    previous_square,
):
    layer_count = control.shape[0]
    offset = lax.axis_index("lev") * layer_count
    own_rows = lax.dynamic_slice_in_dim(vertical, offset, layer_count, 0)
    blended = jnp.einsum("lm,mij->lij", own_rows, all_layers(control), precision=highest)
    field_now = error_scale * smooth(blended, spread)
    for repeat in range(2):
        padded = with_rim(field_now[None], 1)[0]
        field_now = advance(padded, field_now, wind_lon, wind_lat)
    owners = obs_count.shape[-1]
    slot_count = obs_block.shape[-1]
    obs_width = interp.shape[-1]
    cell_rows = field_now.reshape(-1, obs_width)
    block_index = obs_block.reshape(owners * slot_count)
    weights = interp.reshape(owners * slot_count, obs_width, obs_width)
    evolved = jnp.einsum("bij,bj->bi", weights, cell_rows[block_index], precision=highest)
    is_live = jnp.arange(slot_count, dtype=jnp.int32)[None, :] < obs_count.reshape(owners)[:, None]
    departure = jnp.where(
        is_live[:, :, None],
        evolved.reshape(owners, slot_count, obs_width)
        - innovation.reshape(owners, slot_count, obs_width),
        jnp.float32(0.0),
    )
    platforms = obs_platform.reshape(owners, slot_count)
    arrived, arrived_platforms = (
        lax.all_to_all(departure, ("lat", "lon"), split_axis=0, concat_axis=0, tiled=True),
        lax.all_to_all(platforms, ("lat", "lon"), split_axis=0, concat_axis=0, tiled=True),
    )
    result = weigh_obs(arrived, arrived_platforms, error_inverse)
    returned = lax.all_to_all(result, ("lat", "lon"), split_axis=0, concat_axis=0, tiled=True)
    adjoint_obs = jnp.einsum(
        "bij,bi->bj", weights, returned.reshape(owners * slot_count, obs_width), precision=highest
    )
    adjoint = jnp.zeros_like(cell_rows).at[block_index].add(adjoint_obs).reshape(field_now.shape)
    for repeat in range(2):
        adjoint = retreat(adjoint, wind_lon, wind_lat)
    filtered = smooth(error_scale * adjoint, spread)
    own_columns = lax.dynamic_slice_in_dim(vertical, offset, layer_count, 1)
    gradient = control + jnp.einsum(
        "lm,lij->mij", own_columns, all_layers(filtered), precision=highest
    )
    sum_squares = lax.psum(jnp.sum(gradient * gradient), ("lat", "lon", "lev"))
    cell_count = gradient.size * lax.axis_size("lat") * lax.axis_size("lon") * lax.axis_size("lev")
    square = sum_squares / cell_count
    direction = -gradient + square / previous_square[0] * previous_direction
    return (gradient, direction)


def solution(mesh):
    placed = (
        P("lev", ("member", "lat"), "lon"),
        P(),
        P("lev", "lat", "lon"),
        P("lev", "lat", "lon"),
        P("lev", ("member", "lat"), "lon"),
        P("lev", ("member", "lat"), "lon"),
        P("lev", "lat", "lon", None, None),
        P("lev", "lat", "lon", None, None),
        P("lev", "lat", "lon", None),
        P("lev", "lat", "lon", None, None, None, None),
        P("lev", ("member", "lat"), "lon", None, None, None),
        P("lat", "lon", None, None, None),
        P("lev", ("member", "lat"), "lon"),
        P("member"),
    )
    return jax.shard_map(
        local,
        mesh=mesh,
        in_specs=placed,
        out_specs=(P("lev", ("member", "lat"), "lon"), P("lev", ("member", "lat"), "lon")),
        check_vma=False,
    )
```

profile of v0, /device:TPU:0, one launch (start us, length us, event | category | flops | bytes accessed | tf_op | source)
XLA Modules:
  0.0 193.1 jit_solution(1540834913772240107)
XLA Ops:
  0.6 2.6 %all_gather.6 = f32[4,56,512]{2,1,0:T(8,128)S(1)} all-gather(f32[2,56,512]{2,1,0:T(8,128)} %param.14), channel_id=1, replica_groups=mesh['member'=2,'lat'=4,'lon'=2,'lev'=2] {'lev'}, dimensions={0}, use_global_device_ids=true | all-gather | bytes 688128 | tf_op jit(solution)/shard_map/all_gather | solution.py:76
  5.1 2.9 %collective-permute-start = (f32[1,2,56,1]{3,2,1,0:T(8,128)S(1)}, f32[1,2,56,1]{3,2,1,0:T(8,128)S(1)}, u32[]{:S(2)}, u32[]{:S(2)}) collective-permute-start(f32[1,2,56,1]{3,2,1,0:T(8,128)S(1)} %get-tuple-element.60), channel_id=1, source_target_pairs={{0,2},{2,0},{1,3},{3,1},{4,6},{6,4},{5,7},{7,5},{8,10},{10,8},{9,1... | collective-permute-start | bytes 1352 | tf_op jit(solution)/shard_map/ppermute | solution.py:22
  12.3 3.5 %collective-permute-start.2 = (f32[1,2,1,514]{3,2,1,0:T(1,128)S(1)}, f32[1,2,1,514]{3,2,1,0:T(1,128)S(1)}, u32[]{:S(2)}, u32[]{:S(2)}) collective-permute-start(f32[1,2,1,514]{3,2,1,0:T(1,128)S(1)} %get-tuple-element.46), channel_id=1, source_target_pairs={{0,4},{4,8},{8,12},{1,5},{5,9},{9,13},{2,6},{6,10},{10,14},{3,7},{... | collective-permute-start | bytes 12344 | tf_op jit(solution)/shard_map/ppermute | solution.py:22
  17.1 4.2 %collective-permute-done.3 = f32[1,2,1,514]{3,2,1,0:T(1,128)S(1)} collective-permute-done((f32[1,2,1,514]{3,2,1,0:T(1,128)S(1)}, f32[1,2,1,514]{3,2,1,0:T(1,128)S(1)}, u32[]{:S(2)}, u32[]{:S(2)}) %collective-permute-start.3) | collective-permute-done | bytes 4144 | tf_op jit(solution)/shard_map/ppermute | solution.py:24
  27.2 3.5 %collective-permute-start.6 = (f32[1,2,1,514]{3,2,1,0:T(1,128)S(1)}, f32[1,2,1,514]{3,2,1,0:T(1,128)S(1)}, u32[]{:S(2)}, u32[]{:S(2)}) collective-permute-start(f32[1,2,1,514]{3,2,1,0:T(1,128)S(1)} %get-tuple-element.44), channel_id=1, source_target_pairs={{0,4},{4,8},{8,12},{1,5},{5,9},{9,13},{2,6},{6,10},{10,14},{3,7},{... | collective-permute-start | bytes 12344 | tf_op jit(solution)/shard_map/ppermute | solution.py:22
  32.1 4.2 %collective-permute-done.7 = f32[1,2,1,514]{3,2,1,0:T(1,128)S(1)} collective-permute-done((f32[1,2,1,514]{3,2,1,0:T(1,128)S(1)}, f32[1,2,1,514]{3,2,1,0:T(1,128)S(1)}, u32[]{:S(2)}, u32[]{:S(2)}) %collective-permute-start.7) | collective-permute-done | bytes 4144 | tf_op jit(solution)/shard_map/ppermute | solution.py:24
  39.6 3.3 %all-to-all-start = ((s32[8,1,2]{2,1,0:T(1,128)}), s32[8,1,2]{2,1,0:T(1,128)S(1)}, u32[]{:S(2)}, u32[]{:S(2)}) async-start(s32[8,1,2]{2,1,0:T(1,128)} %copy.158), calls=%async_computation | async-start | bytes 8192 | tf_op jit(solution)/shard_map/all_to_all | solution.py:130
  43.1 3.9 %collective-permute-start.10 = (f32[1,2,1,514]{3,2,1,0:T(1,128)S(1)}, f32[1,2,1,514]{3,2,1,0:T(1,128)S(1)}, u32[]{:S(2)}, u32[]{:S(2)}) collective-permute-start(f32[1,2,1,514]{3,2,1,0:T(1,128)S(1)} %get-tuple-element.42), channel_id=1, source_target_pairs={{0,4},{4,8},{8,12},{1,5},{5,9},{9,13},{2,6},{6,10},{10,14},{3,7},{... | collective-permute-start | bytes 12344 | tf_op jit(solution)/shard_map/ppermute | solution.py:22
  49.2 3.3 %collective-permute-done.11 = f32[1,2,1,514]{3,2,1,0:T(1,128)S(1)} collective-permute-done((f32[1,2,1,514]{3,2,1,0:T(1,128)S(1)}, f32[1,2,1,514]{3,2,1,0:T(1,128)S(1)}, u32[]{:S(2)}, u32[]{:S(2)}) %collective-permute-start.11) | collective-permute-done | bytes 4144 | tf_op jit(solution)/shard_map/ppermute | solution.py:24
  58.9 3.4 %collective-permute-start.14 = (f32[1,2,1,514]{3,2,1,0:T(1,128)S(1)}, f32[1,2,1,514]{3,2,1,0:T(1,128)S(1)}, u32[]{:S(2)}, u32[]{:S(2)}) collective-permute-start(f32[1,2,1,514]{3,2,1,0:T(1,128)S(1)} %get-tuple-element.40), channel_id=1, source_target_pairs={{0,4},{4,8},{8,12},{1,5},{5,9},{9,13},{2,6},{6,10},{10,14},{3,7},{... | collective-permute-start | bytes 12344 | tf_op jit(solution)/shard_map/ppermute | solution.py:22
  63.6 4.1 %collective-permute-done.15 = f32[1,2,1,514]{3,2,1,0:T(1,128)S(1)} collective-permute-done((f32[1,2,1,514]{3,2,1,0:T(1,128)S(1)}, f32[1,2,1,514]{3,2,1,0:T(1,128)S(1)}, u32[]{:S(2)}, u32[]{:S(2)}) %collective-permute-start.15) | collective-permute-done | bytes 4144 | tf_op jit(solution)/shard_map/ppermute | solution.py:24
  71.3 3.3 %all-to-all-start.1 = ((f32[8,2,128]{2,1,0:T(2,128)}), f32[8,2,128]{2,1,0:T(2,128)S(1)}, u32[]{:S(2)}, u32[]{:S(2)}) async-start(f32[8,2,128]{2,1,0:T(2,128)} %fusion.44), calls=%async_computation.1 | async-start | bytes 16384 | tf_op jit(solution)/shard_map/all_to_all | solution.py:129
  74.6 6.4 %all-to-all-done.1 = f32[8,2,128]{2,1,0:T(2,128)S(1)} async-done(((f32[8,2,128]{2,1,0:T(2,128)}), f32[8,2,128]{2,1,0:T(2,128)S(1)}, u32[]{:S(2)}, u32[]{:S(2)}) %all-to-all-start.1) | async-done | bytes 8224 | tf_op jit(solution)/shard_map/all_to_all | solution.py:129
  81.6 8.9 %all_to_all.19 = f32[8,2,128]{2,1,0:T(2,128)S(1)} all-to-all(f32[8,2,128]{2,1,0:T(2,128)S(1)} %copy.164), channel_id=1, replica_groups=mesh['member'=2,'lat'=4,'lon'=2,'lev'=2] {'lat','lon'}, dimensions={0} | all-to-all | bytes 16384 | tf_op jit(solution)/shard_map/all_to_all | solution.py:133
  94.6 4.1 %collective-permute-done.16 = f32[3,2,56,1]{3,2,1,0:T(8,128)S(1)} collective-permute-done((f32[3,2,56,1]{3,2,1,0:T(8,128)S(1)}, f32[3,2,56,1]{3,2,1,0:T(8,128)S(1)}, u32[]{:S(2)}, u32[]{:S(2)}) %collective-permute-start.16) | collective-permute-done | bytes 1376 | tf_op jit(solution)/shard_map/ppermute | solution.py:22
  98.7 3.7 %collective-permute-done.17 = f32[3,2,56,1]{3,2,1,0:T(8,128)S(1)} collective-permute-done((f32[3,2,56,1]{3,2,1,0:T(8,128)S(1)}, f32[3,2,56,1]{3,2,1,0:T(8,128)S(1)}, u32[]{:S(2)}, u32[]{:S(2)}) %collective-permute-start.17) | collective-permute-done | bytes 1376 | tf_op jit(solution)/shard_map/ppermute | solution.py:24
  106.3 4.2 %collective-permute-done.19 = f32[3,2,1,514]{3,2,1,0:T(1,128)S(1)} collective-permute-done((f32[3,2,1,514]{3,2,1,0:T(1,128)S(1)}, f32[3,2,1,514]{3,2,1,0:T(1,128)S(1)}, u32[]{:S(2)}, u32[]{:S(2)}) %collective-permute-start.19) | collective-permute-done | bytes 12368 | tf_op jit(solution)/shard_map/ppermute | solution.py:24
  113.7 3.4 %collective-permute-done.20 = f32[3,2,56,1]{3,2,1,0:T(8,128)S(1)} collective-permute-done((f32[3,2,56,1]{3,2,1,0:T(8,128)S(1)}, f32[3,2,56,1]{3,2,1,0:T(8,128)S(1)}, u32[]{:S(2)}, u32[]{:S(2)}) %collective-permute-start.20) | collective-permute-done | bytes 1376 | tf_op jit(solution)/shard_map/ppermute | solution.py:22
  119.1 2.5 %collective-permute-start.22 = (f32[3,2,1,514]{3,2,1,0:T(1,128)S(1)}, f32[3,2,1,514]{3,2,1,0:T(1,128)S(1)}, u32[]{:S(2)}, u32[]{:S(2)}) collective-permute-start(f32[3,2,1,514]{3,2,1,0:T(1,128)S(1)} %get-tuple-element.22), channel_id=1, source_target_pairs={{0,4},{4,8},{8,12},{1,5},{5,9},{9,13},{2,6},{6,10},{10,14},{3,7},{... | collective-permute-start | bytes 37016 | tf_op jit(solution)/shard_map/ppermute | solution.py:22
  123.0 4.2 %collective-permute-done.23 = f32[3,2,1,514]{3,2,1,0:T(1,128)S(1)} collective-permute-done((f32[3,2,1,514]{3,2,1,0:T(1,128)S(1)}, f32[3,2,1,514]{3,2,1,0:T(1,128)S(1)}, u32[]{:S(2)}, u32[]{:S(2)}) %collective-permute-start.23) | collective-permute-done | bytes 12368 | tf_op jit(solution)/shard_map/ppermute | solution.py:24
  133.4 2.9 %collective-permute-start.26 = (f32[1,2,1,514]{3,2,1,0:T(1,128)S(1)}, f32[1,2,1,514]{3,2,1,0:T(1,128)S(1)}, u32[]{:S(2)}, u32[]{:S(2)}) collective-permute-start(f32[1,2,1,514]{3,2,1,0:T(1,128)S(1)} %get-tuple-element.38), channel_id=1, source_target_pairs={{0,4},{4,8},{8,12},{1,5},{5,9},{9,13},{2,6},{6,10},{10,14},{3,7},{... | collective-permute-start | bytes 12344 | tf_op jit(solution)/shard_map/ppermute | solution.py:22
  137.8 4.0 %collective-permute-done.27 = f32[1,2,1,514]{3,2,1,0:T(1,128)S(1)} collective-permute-done((f32[1,2,1,514]{3,2,1,0:T(1,128)S(1)}, f32[1,2,1,514]{3,2,1,0:T(1,128)S(1)}, u32[]{:S(2)}, u32[]{:S(2)}) %collective-permute-start.27) | collective-permute-done | bytes 4144 | tf_op jit(solution)/shard_map/ppermute | solution.py:24
  152.0 3.6 %collective-permute-done.31 = f32[1,2,1,514]{3,2,1,0:T(1,128)S(1)} collective-permute-done((f32[1,2,1,514]{3,2,1,0:T(1,128)S(1)}, f32[1,2,1,514]{3,2,1,0:T(1,128)S(1)}, u32[]{:S(2)}, u32[]{:S(2)}) %collective-permute-start.31) | collective-permute-done | bytes 4144 | tf_op jit(solution)/shard_map/ppermute | solution.py:24
  160.5 30.2 %psum.7 = f32[]{:T(128)} all-reduce(f32[]{:T(128)} %get-tuple-element.62), channel_id=1, replica_groups=mesh['member'=2,'lat'=4,'lon'=2,'lev'=2] {'lat','lon','lev'}, use_global_device_ids=true, to_apply=%region_3.4 | all-reduce | flops 1 | bytes 8 | tf_op jit(solution)/shard_map/psum | solution.py:145
  (134 shorter events, 70.2 us)
Async XLA Ops:
  5.1 5.1 %collective-permute-start = (f32[1,2,56,1]{3,2,1,0:T(8,128)S(1)}, f32[1,2,56,1]{3,2,1,0:T(8,128)S(1)}, u32[]{:S(2)}, u32[]{:S(2)}) collective-permute-start(f32[1,2,56,1]{3,2,1,0:T(8,128)S(1)} %get-tuple-element.60), channel_id=1, source_target_pairs={{0,2},{2,0},{1,3},{3,1},{4,6},{6,4},{5,7},{7,5},{8,10},{10,8},{9,1... | collective-permute-start | bytes 1352 | tf_op jit(solution)/shard_map/ppermute | solution.py:22
  12.3 4.8 %collective-permute-start.2 = (f32[1,2,1,514]{3,2,1,0:T(1,128)S(1)}, f32[1,2,1,514]{3,2,1,0:T(1,128)S(1)}, u32[]{:S(2)}, u32[]{:S(2)}) collective-permute-start(f32[1,2,1,514]{3,2,1,0:T(1,128)S(1)} %get-tuple-element.46), channel_id=1, source_target_pairs={{0,4},{4,8},{8,12},{1,5},{5,9},{9,13},{2,6},{6,10},{10,14},{3,7},{... | collective-permute-start | bytes 12344 | tf_op jit(solution)/shard_map/ppermute | solution.py:22
  15.8 5.5 %collective-permute-start.3 = (f32[1,2,1,514]{3,2,1,0:T(1,128)S(1)}, f32[1,2,1,514]{3,2,1,0:T(1,128)S(1)}, u32[]{:S(2)}, u32[]{:S(2)}) collective-permute-start(f32[1,2,1,514]{3,2,1,0:T(1,128)S(1)} %get-tuple-element.47), channel_id=1, source_target_pairs={{4,0},{8,4},{12,8},{5,1},{9,5},{13,9},{6,2},{10,6},{14,10},{7,3},{... | collective-permute-start | bytes 12344 | tf_op jit(solution)/shard_map/ppermute | solution.py:24
  21.9 4.2 %collective-permute-start.4 = (f32[1,2,56,1]{3,2,1,0:T(8,128)S(1)}, f32[1,2,56,1]{3,2,1,0:T(8,128)S(1)}, u32[]{:S(2)}, u32[]{:S(2)}) collective-permute-start(f32[1,2,56,1]{3,2,1,0:T(8,128)S(1)} %get-tuple-element.58), channel_id=1, source_target_pairs={{0,2},{2,0},{1,3},{3,1},{4,6},{6,4},{5,7},{7,5},{8,10},{10,8},{9,1... | collective-permute-start | bytes 1352 | tf_op jit(solution)/shard_map/ppermute | solution.py:22
  27.2 4.9 %collective-permute-start.6 = (f32[1,2,1,514]{3,2,1,0:T(1,128)S(1)}, f32[1,2,1,514]{3,2,1,0:T(1,128)S(1)}, u32[]{:S(2)}, u32[]{:S(2)}) collective-permute-start(f32[1,2,1,514]{3,2,1,0:T(1,128)S(1)} %get-tuple-element.44), channel_id=1, source_target_pairs={{0,4},{4,8},{8,12},{1,5},{5,9},{9,13},{2,6},{6,10},{10,14},{3,7},{... | collective-permute-start | bytes 12344 | tf_op jit(solution)/shard_map/ppermute | solution.py:22
  30.7 5.6 %collective-permute-start.7 = (f32[1,2,1,514]{3,2,1,0:T(1,128)S(1)}, f32[1,2,1,514]{3,2,1,0:T(1,128)S(1)}, u32[]{:S(2)}, u32[]{:S(2)}) collective-permute-start(f32[1,2,1,514]{3,2,1,0:T(1,128)S(1)} %get-tuple-element.45), channel_id=1, source_target_pairs={{4,0},{8,4},{12,8},{5,1},{9,5},{13,9},{6,2},{10,6},{14,10},{7,3},{... | collective-permute-start | bytes 12344 | tf_op jit(solution)/shard_map/ppermute | solution.py:24
  36.9 6.1 %collective-permute-start.8 = (f32[1,2,56,1]{3,2,1,0:T(8,128)S(1)}, f32[1,2,56,1]{3,2,1,0:T(8,128)S(1)}, u32[]{:S(2)}, u32[]{:S(2)}) collective-permute-start(f32[1,2,56,1]{3,2,1,0:T(8,128)S(1)} %get-tuple-element.56), channel_id=1, source_target_pairs={{0,2},{2,0},{1,3},{3,1},{4,6},{6,4},{5,7},{7,5},{8,10},{10,8},{9,1... | collective-permute-start | bytes 1352 | tf_op jit(solution)/shard_map/ppermute | solution.py:22
  38.0 5.0 %collective-permute-start.9 = (f32[1,2,56,1]{3,2,1,0:T(8,128)S(1)}, f32[1,2,56,1]{3,2,1,0:T(8,128)S(1)}, u32[]{:S(2)}, u32[]{:S(2)}) collective-permute-start(f32[1,2,56,1]{3,2,1,0:T(8,128)S(1)} %get-tuple-element.57), channel_id=1, source_target_pairs={{2,0},{0,2},{3,1},{1,3},{6,4},{4,6},{7,5},{5,7},{10,8},{8,10},{11,... | collective-permute-start | bytes 1352 | tf_op jit(solution)/shard_map/ppermute | solution.py:24
  39.6 23.9 %all-to-all-start = ((s32[8,1,2]{2,1,0:T(1,128)}), s32[8,1,2]{2,1,0:T(1,128)S(1)}, u32[]{:S(2)}, u32[]{:S(2)}) async-start(s32[8,1,2]{2,1,0:T(1,128)} %copy.158), calls=%async_computation | async-start | bytes 8192 | tf_op jit(solution)/shard_map/all_to_all | solution.py:130
  43.1 6.1 %collective-permute-start.10 = (f32[1,2,1,514]{3,2,1,0:T(1,128)S(1)}, f32[1,2,1,514]{3,2,1,0:T(1,128)S(1)}, u32[]{:S(2)}, u32[]{:S(2)}) collective-permute-start(f32[1,2,1,514]{3,2,1,0:T(1,128)S(1)} %get-tuple-element.42), channel_id=1, source_target_pairs={{0,4},{4,8},{8,12},{1,5},{5,9},{9,13},{2,6},{6,10},{10,14},{3,7},{... | collective-permute-start | bytes 12344 | tf_op jit(solution)/shard_map/ppermute | solution.py:22
  47.0 5.5 %collective-permute-start.11 = (f32[1,2,1,514]{3,2,1,0:T(1,128)S(1)}, f32[1,2,1,514]{3,2,1,0:T(1,128)S(1)}, u32[]{:S(2)}, u32[]{:S(2)}) collective-permute-start(f32[1,2,1,514]{3,2,1,0:T(1,128)S(1)} %get-tuple-element.43), channel_id=1, source_target_pairs={{4,0},{8,4},{12,8},{5,1},{9,5},{13,9},{6,2},{10,6},{14,10},{7,3},{... | collective-permute-start | bytes 12344 | tf_op jit(solution)/shard_map/ppermute | solution.py:24
  53.1 4.2 %collective-permute-start.12 = (f32[1,2,56,1]{3,2,1,0:T(8,128)S(1)}, f32[1,2,56,1]{3,2,1,0:T(8,128)S(1)}, u32[]{:S(2)}, u32[]{:S(2)}) collective-permute-start(f32[1,2,56,1]{3,2,1,0:T(8,128)S(1)} %get-tuple-element.54), channel_id=1, source_target_pairs={{0,2},{2,0},{1,3},{3,1},{4,6},{6,4},{5,7},{7,5},{8,10},{10,8},{9,1... | collective-permute-start | bytes 1352 | tf_op jit(solution)/shard_map/ppermute | solution.py:22
  58.9 4.8 %collective-permute-start.14 = (f32[1,2,1,514]{3,2,1,0:T(1,128)S(1)}, f32[1,2,1,514]{3,2,1,0:T(1,128)S(1)}, u32[]{:S(2)}, u32[]{:S(2)}) collective-permute-start(f32[1,2,1,514]{3,2,1,0:T(1,128)S(1)} %get-tuple-element.40), channel_id=1, source_target_pairs={{0,4},{4,8},{8,12},{1,5},{5,9},{9,13},{2,6},{6,10},{10,14},{3,7},{... | collective-permute-start | bytes 12344 | tf_op jit(solution)/shard_map/ppermute | solution.py:22
  62.2 5.5 %collective-permute-start.15 = (f32[1,2,1,514]{3,2,1,0:T(1,128)S(1)}, f32[1,2,1,514]{3,2,1,0:T(1,128)S(1)}, u32[]{:S(2)}, u32[]{:S(2)}) collective-permute-start(f32[1,2,1,514]{3,2,1,0:T(1,128)S(1)} %get-tuple-element.41), channel_id=1, source_target_pairs={{4,0},{8,4},{12,8},{5,1},{9,5},{13,9},{6,2},{10,6},{14,10},{7,3},{... | collective-permute-start | bytes 12344 | tf_op jit(solution)/shard_map/ppermute | solution.py:24
  71.3 9.8 %all-to-all-start.1 = ((f32[8,2,128]{2,1,0:T(2,128)}), f32[8,2,128]{2,1,0:T(2,128)S(1)}, u32[]{:S(2)}, u32[]{:S(2)}) async-start(f32[8,2,128]{2,1,0:T(2,128)} %fusion.44), calls=%async_computation.1 | async-start | bytes 16384 | tf_op jit(solution)/shard_map/all_to_all | solution.py:129
  92.5 6.2 %collective-permute-start.16 = (f32[3,2,56,1]{3,2,1,0:T(8,128)S(1)}, f32[3,2,56,1]{3,2,1,0:T(8,128)S(1)}, u32[]{:S(2)}, u32[]{:S(2)}) collective-permute-start(f32[3,2,56,1]{3,2,1,0:T(8,128)S(1)} %get-tuple-element.34), channel_id=1, source_target_pairs={{0,2},{2,0},{1,3},{3,1},{4,6},{6,4},{5,7},{7,5},{8,10},{10,8},{9,1... | collective-permute-start | bytes 4040 | tf_op jit(solution)/shard_map/ppermute | solution.py:22
  93.1 9.3 %collective-permute-start.17 = (f32[3,2,56,1]{3,2,1,0:T(8,128)S(1)}, f32[3,2,56,1]{3,2,1,0:T(8,128)S(1)}, u32[]{:S(2)}, u32[]{:S(2)}) collective-permute-start(f32[3,2,56,1]{3,2,1,0:T(8,128)S(1)} %get-tuple-element.35), channel_id=1, source_target_pairs={{2,0},{0,2},{3,1},{1,3},{6,4},{4,6},{7,5},{5,7},{10,8},{8,10},{11,... | collective-permute-start | bytes 4040 | tf_op jit(solution)/shard_map/ppermute | solution.py:24
  104.8 5.6 %collective-permute-start.19 = (f32[3,2,1,514]{3,2,1,0:T(1,128)S(1)}, f32[3,2,1,514]{3,2,1,0:T(1,128)S(1)}, u32[]{:S(2)}, u32[]{:S(2)}) collective-permute-start(f32[3,2,1,514]{3,2,1,0:T(1,128)S(1)} %get-tuple-element.25), channel_id=1, source_target_pairs={{4,0},{8,4},{12,8},{5,1},{9,5},{13,9},{6,2},{10,6},{14,10},{7,3},{... | collective-permute-start | bytes 37016 | tf_op jit(solution)/shard_map/ppermute | solution.py:24
  111.6 5.5 %collective-permute-start.20 = (f32[3,2,56,1]{3,2,1,0:T(8,128)S(1)}, f32[3,2,56,1]{3,2,1,0:T(8,128)S(1)}, u32[]{:S(2)}, u32[]{:S(2)}) collective-permute-start(f32[3,2,56,1]{3,2,1,0:T(8,128)S(1)} %get-tuple-element.32), channel_id=1, source_target_pairs={{0,2},{2,0},{1,3},{3,1},{4,6},{6,4},{5,7},{7,5},{8,10},{10,8},{9,1... | collective-permute-start | bytes 4040 | tf_op jit(solution)/shard_map/ppermute | solution.py:22
  112.3 6.6 %collective-permute-start.21 = (f32[3,2,56,1]{3,2,1,0:T(8,128)S(1)}, f32[3,2,56,1]{3,2,1,0:T(8,128)S(1)}, u32[]{:S(2)}, u32[]{:S(2)}) collective-permute-start(f32[3,2,56,1]{3,2,1,0:T(8,128)S(1)} %get-tuple-element.33), channel_id=1, source_target_pairs={{2,0},{0,2},{3,1},{1,3},{6,4},{4,6},{7,5},{5,7},{10,8},{8,10},{11,... | collective-permute-start | bytes 4040 | tf_op jit(solution)/shard_map/ppermute | solution.py:24
  121.6 5.6 %collective-permute-start.23 = (f32[3,2,1,514]{3,2,1,0:T(1,128)S(1)}, f32[3,2,1,514]{3,2,1,0:T(1,128)S(1)}, u32[]{:S(2)}, u32[]{:S(2)}) collective-permute-start(f32[3,2,1,514]{3,2,1,0:T(1,128)S(1)} %get-tuple-element.23), channel_id=1, source_target_pairs={{4,0},{8,4},{12,8},{5,1},{9,5},{13,9},{6,2},{10,6},{14,10},{7,3},{... | collective-permute-start | bytes 37016 | tf_op jit(solution)/shard_map/ppermute | solution.py:24
  133.4 4.4 %collective-permute-start.26 = (f32[1,2,1,514]{3,2,1,0:T(1,128)S(1)}, f32[1,2,1,514]{3,2,1,0:T(1,128)S(1)}, u32[]{:S(2)}, u32[]{:S(2)}) collective-permute-start(f32[1,2,1,514]{3,2,1,0:T(1,128)S(1)} %get-tuple-element.38), channel_id=1, source_target_pairs={{0,4},{4,8},{8,12},{1,5},{5,9},{9,13},{2,6},{6,10},{10,14},{3,7},{... | collective-permute-start | bytes 12344 | tf_op jit(solution)/shard_map/ppermute | solution.py:22
  136.3 5.5 %collective-permute-start.27 = (f32[1,2,1,514]{3,2,1,0:T(1,128)S(1)}, f32[1,2,1,514]{3,2,1,0:T(1,128)S(1)}, u32[]{:S(2)}, u32[]{:S(2)}) collective-permute-start(f32[1,2,1,514]{3,2,1,0:T(1,128)S(1)} %get-tuple-element.39), channel_id=1, source_target_pairs={{4,0},{8,4},{12,8},{5,1},{9,5},{13,9},{6,2},{10,6},{14,10},{7,3},{... | collective-permute-start | bytes 12344 | tf_op jit(solution)/shard_map/ppermute | solution.py:24
  150.0 5.5 %collective-permute-start.31 = (f32[1,2,1,514]{3,2,1,0:T(1,128)S(1)}, f32[1,2,1,514]{3,2,1,0:T(1,128)S(1)}, u32[]{:S(2)}, u32[]{:S(2)}) collective-permute-start(f32[1,2,1,514]{3,2,1,0:T(1,128)S(1)} %get-tuple-element.37), channel_id=1, source_target_pairs={{4,0},{8,4},{12,8},{5,1},{9,5},{13,9},{6,2},{10,6},{14,10},{7,3},{... | collective-permute-start | bytes 12344 | tf_op jit(solution)/shard_map/ppermute | solution.py:24
  (23 other events, 144.4 us)
where the time goes:
time: 194 us; the launch traced here: 193 us
  waiting for transfers between devices  68.9 us (36%)
  starting transfers between devices  58.6 us (30%)
  blocking collectives  43.9 us (23%)
  other arithmetic  7.55 us (4%)
  matrix products  6.55 us (3%)
  local copies, waits for them, and re-layouts  5 us (3%)
  between operations  2.55 us (1%)
    ppermute x16, waiting for transfers between devices, padded_2(): lax.ppermute(head, axis, [((i + 1) % count, i) for i in range(ends)])  44 us
    ppermute x16, starting transfers between devices, padded_2(): lax.ppermute(tail, axis, [(i, (i + 1) % count) for i in range(ends)])  33.9 us
    psum x1, blocking collectives, local(): sum_squares = lax.psum(jnp.sum(gradient * gradient), ('lat', 'lon', 'lev'))  30.2 us
    ppermute x16, waiting for transfers between devices, padded_2(): lax.ppermute(tail, axis, [(i, (i + 1) % count) for i in range(ends)])  18.5 us
    ppermute x16, starting transfers between devices, padded_2(): lax.ppermute(head, axis, [((i + 1) % count, i) for i in range(ends)])  18 us
    all_to_all x1, blocking collectives, local(): lax.all_to_all(result, ('lat', 'lon'), split_axis=0, concat_axis=0, tiled...  8.88 us
    all_to_all x1, waiting for transfers between devices, local(): lax.all_to_all(departure, ('lat', 'lon'), split_axis=0, concat_axis=0, ti...  6.44 us
    all_gather x2, blocking collectives, all_layers(): return lax.all_gather(field_now, 'lev', axis=0, tiled=True)  4.82 us
  transfers between devices with their start and end apart: 34, of which 25 were waited for; matrix products, arithmetic and copies ran while one was open for 1% of the time, Pallas kernels for 0%

commit v1 on v0

v1 whole, which is shorter than its diff:
```python
import functools
import jax
import jax.numpy as jnp
from jax import lax
from jax.experimental import pallas as pl
from jax.experimental.pallas import tpu as pltpu
from jax.sharding import PartitionSpec as P

FILTER = 2
STEPS = 2
HALO = 4
WIDTHS = (4, 4, 4, 4, 2)
LANES = 128
smoothing = 0.1
diffusion = 0.15
f32 = jnp.float32
bf16 = jnp.bfloat16
VMEM = pl.BlockSpec(memory_space=pltpu.VMEM)
SMEM = pl.BlockSpec(memory_space=pltpu.SMEM)
NT = (((1,), (1,)), ((), ()))
NN = (((1,), (0,)), ((), ()))


def call(kernel, out_shape, in_specs, scratch=(), limit=16 << 20, flops=1 << 20):
    many = isinstance(out_shape, (list, tuple))
    return pl.pallas_call(
        kernel,
        out_shape=out_shape,
        in_specs=in_specs,
        out_specs=[VMEM] * len(out_shape) if many else VMEM,
        scratch_shapes=list(scratch),
        compiler_params=pltpu.CompilerParams(vmem_limit_bytes=limit),
        cost_estimate=pl.CostEstimate(flops=flops, bytes_accessed=1 << 20, transcendentals=0),
    )


def shape(*dims):
    return jax.ShapeDtypeStruct(dims, f32)


def split(value):
    high = value.astype(bf16)
    return high, (value - high.astype(f32)).astype(bf16)


def dot(left, right, dims):
    lh, ll = split(left)
    rh, rl = split(right)
    part = lambda a, b: lax.dot_general(a, b, dims, preferred_element_type=f32)
    return part(lh, rh) + (part(ll, rh) + part(lh, rl))


def for_each(count, body, start):
    if count <= 32:
        for i in range(count):
            start = body(i, start)
        return start
    return lax.fori_loop(0, count, body, start)


def north(x):
    return pltpu.roll(x, x.shape[0] - 1, 0)


def south(x):
    return pltpu.roll(x, 1, 0)


def east(x):
    return pltpu.roll(x, x.shape[1] - 1, 1)


def west(x):
    return pltpu.roll(x, 1, 1)


def smooth(s, spread):
    for repeat in range(FILTER):
        q = spread * s
        s = s + smoothing * spread * (north(q) + south(q) + east(q) + west(q) - 4.0 * q)
    return s


def edge_block(rows):
    lane = lax.broadcasted_iota(jnp.int32, (rows.shape[0], LANES), 1)
    return jnp.where(lane < LANES // 2, rows[:, :LANES], rows[:, rows.shape[1] - LANES :])


def blend(flags, vertical, control, others, layer, transposed):
    layers = control.shape[0]
    levs = 1 + len(others)
    total = None
    for shift, source in enumerate([control] + list(others)):
        lev = lax.rem(flags[3] + levs - shift, levs)
        for m in range(layers):
            a, b = flags[3] * layers + layer, lev * layers + m
            weight = vertical[b, a] if transposed else vertical[a, b]
            term = weight * source[m]
            total = term if total is None else total + term
    return total


def pack_kernel(n_other, *refs):
    flags, vertical, control = refs[:3]
    others = refs[3 : 3 + n_other]
    spread, scale, wind_e, wind_n, blocks = refs[3 + n_other : 8 + n_other]
    blended, lon_out, lat_1, lat_2, diag_1, diag_2, first, last = refs[8 + n_other :]
    layers, rows, cols = control.shape
    for l in range(layers):
        blended[l] = blend(flags, vertical, control, others, l, False)
    fields = (blended, spread, wind_e, wind_n, scale)
    lane = lax.broadcasted_iota(jnp.int32, (rows, LANES), 1)
    packed = jnp.zeros((rows, LANES), f32)
    item = 0
    for field in fields:
        for l in range(layers):
            tile = jnp.where(lane < LANES // 2, field[l, :, :LANES], field[l, :, cols - LANES :])
            if item:
                tile = pltpu.roll(tile, 8 * item, 1)
            packed = jnp.where((lane + HALO - 8 * item) % LANES < 8, tile, packed)
            item += 1
    lon_out[:rows, :] = packed
    lon_out[rows:, :] = jnp.zeros((lon_out.shape[0] - rows, LANES), f32)
    lon_out[rows : rows + blocks.shape[0], :] = blocks[...]
    for out, low in ((first, True), (last, False)):
        at = 0
        for field, width in zip(fields, WIDTHS):
            for l in range(layers):
                begin = 0 if low else rows - width
                out[at : at + width, :] = field[l, begin : begin + width, :]
                at += width
        out[at:, :] = jnp.zeros((out.shape[0] - at, cols), f32)
        out[at : at + blocks.shape[0], :LANES] = blocks[...]
        out[at : at + blocks.shape[0], cols - LANES :] = blocks[...]
    a, b = first[...], last[...]
    even = jnp.full(a.shape, flags[0], jnp.int32) == 0
    one = jnp.where(even, b, a)
    two = jnp.where(even, a, b)
    lat_1[...] = one
    lat_2[...] = two
    diag_1[...] = edge_block(one)
    diag_2[...] = edge_block(two)


def unpack(flags, own, lon_in, lat_1, lat_2, diag_1, diag_2, ext):
    layers, rows, cols = own[0].shape
    lane = lax.broadcasted_iota(jnp.int32, (rows, LANES), 1)
    keep = (lane < HALO) | (lane >= LANES - HALO)
    packed = lon_in[:rows, :]
    item = 0
    for field, out in zip(own, ext):
        for l in range(layers):
            out[l, :rows, :cols] = field[l]
            tile = pltpu.roll(packed, LANES - 8 * item, 1) if item else packed
            out[l, :rows, cols:] = jnp.where(keep, tile, 0.0)
            item += 1
    count = sum(WIDTHS) * layers
    for one, two, begin in ((lat_1, lat_2, 0), (diag_1, diag_2, cols)):
        width = one.shape[1]
        a, b = one[:count, :], two[:count, :]
        even = jnp.full(a.shape, flags[0], jnp.int32) == 0
        top = jnp.full(a.shape, flags[2], jnp.int32) == 0
        bottom = jnp.full(a.shape, flags[1], jnp.int32) == 0
        if begin:
            lane_d = lax.broadcasted_iota(jnp.int32, a.shape, 1)
            inside = (lane_d < HALO) | (lane_d >= LANES - HALO)
            top = top & inside
            bottom = bottom & inside
        from_north = jnp.where(top, jnp.where(even, a, b), 0.0)
        from_south = jnp.where(bottom, jnp.where(even, b, a), 0.0)
        at = 0
        for out, l, w in [(e, l, w) for e, w in zip(ext, WIDTHS) for l in range(layers)]:
            if w < HALO:
                out[l, rows : rows + 8, begin : begin + width] = jnp.zeros((8, width), f32)
            out[l, rows : rows + w, begin : begin + width] = from_north[at : at + w, :]
            out[l, rows + 8 - w : rows + 8, begin : begin + width] = from_south[at : at + w, :]
            at += w


def inside_mask(flags, ext_shape):
    row = lax.broadcasted_iota(jnp.int32, ext_shape, 0)
    rows = ext_shape[0] - 8
    north_cut = jnp.where(flags[2] != 0, rows, rows + 8)
    south_cut = jnp.where(flags[1] != 0, rows + 4, rows + 8)
    cut = ((row >= north_cut) & (row < rows + 4)) | (row >= south_cut)
    return jnp.where(cut, 0.0, 1.0).astype(f32)


def forward_kernel(*refs):
    flags, at = refs[:2]
    own = refs[2:7]
    lon_in, lat_1, lat_2, diag_1, diag_2, interp, innovation, live, platform = refs[7:16]
    sent, spread, scale, wind_e, wind_n, mixed, field = refs[16:]
    ext = (mixed, spread, wind_e, wind_n, scale)
    unpack(flags, own, lon_in, lat_1, lat_2, diag_1, diag_2, ext)
    layers, ext_rows, ext_cols = mixed.shape
    mask = inside_mask(flags, (ext_rows, ext_cols))
    for l in range(layers):
        x = scale[l] * smooth(mixed[l], spread[l])
        u, v = 0.5 * wind_e[l], 0.5 * wind_n[l]
        for step in range(STEPS):
            if step:
                x = x * mask
            x = (
                (1.0 - 4.0 * diffusion) * x
                + (diffusion - u) * east(x)
                + (diffusion + u) * west(x)
                + (diffusion - v) * north(x)
                + (diffusion + v) * south(x)
            )
        per = ext_cols // LANES - 1
        for c in range(per):
            begin = (l * per + c) * ext_rows
            field[begin : begin + ext_rows, :] = x[:, c * LANES : (c + 1) * LANES]
    count, width = innovation.shape
    row = lax.broadcasted_iota(jnp.int32, (count, width), 0)

    def body(b, total):
        cells = field[pl.ds(at[b], 1), :]
        left = jnp.where(row == b, jnp.broadcast_to(cells, (count, width)), 0.0)
        return total + dot(left, interp[b], NT)

    evolved = for_each(count, body, jnp.zeros((count, width), f32))
    departure = jnp.where(live[...] > 0.5, evolved - innovation[...], 0.0)
    owners, height = sent.shape[:2]
    slots = count // owners
    half = height // 2
    sent[...] = platform[...]
    for o in range(owners):
        sent[o, :slots, :] = departure[o * slots : (o + 1) * slots, :]


def weigh_kernel(arrived, matrices, out):
    tiles, height, width = arrived.shape
    rows = arrived[...].reshape(tiles * height, width)
    platform = pltpu.roll(rows, rows.shape[0] - height // 2, 0)
    total = jnp.zeros(rows.shape, f32)
    for p in range(matrices.shape[0]):
        left = jnp.where(platform == float(p), rows, 0.0)
        total = total + dot(left, matrices[p], NT)
    out[...] = total.reshape(tiles, height, width)


def transpose_kernel(slots, returned, interp, out):
    count, width = out.shape
    row = lax.broadcasted_iota(jnp.int32, (count, width), 0)

    def body(b, total):
        weighted = returned[b // slots, pl.ds(b % slots, 1), :]
        left = jnp.where(row == b, jnp.broadcast_to(weighted, (count, width)), 0.0)
        return total + dot(left, interp[b], NN)

    out[...] = for_each(count, body, jnp.zeros((count, width), f32))


def adjoint_kernel(n_source, *refs):
    flags, target, lane_mask = refs[:3]
    sources = refs[3 : 3 + n_source]
    spread, scale, wind_e, wind_n = refs[3 + n_source : 7 + n_source]
    filtered, = refs[7 + n_source :]
    layers, ext_rows, ext_cols = spread.shape
    rows, cols = filtered.shape[1:]
    values = jnp.concatenate([s[...] for s in sources], axis=0) * lane_mask[...]
    high, low = split(values)
    places = layers * ext_rows * (ext_cols // LANES)
    place = lax.broadcasted_iota(jnp.int32, (places, values.shape[0]), 0)
    chosen = jnp.where(place == target[...], 1.0, 0.0).astype(bf16)
    forcing = lax.dot_general(chosen, high, NN, preferred_element_type=f32)
    forcing = forcing + lax.dot_general(chosen, low, NN, preferred_element_type=f32)
    mask = inside_mask(flags, (ext_rows, ext_cols))
    per = ext_cols // LANES
    for l in range(layers):
        y = jnp.concatenate(
            [forcing[(l * per + c) * ext_rows : (l * per + c + 1) * ext_rows, :] for c in range(per)], axis=1
        )
        u, v = 0.5 * wind_e[l], 0.5 * wind_n[l]
        for step in range(STEPS):
            if step:
                y = y * mask
            y = (
                (1.0 - 4.0 * diffusion) * y
                + east((diffusion + u) * y)
                + west((diffusion - u) * y)
                + north((diffusion + v) * y)
                + south((diffusion - v) * y)
            )
        s = smooth(scale[l] * y, spread[l])
        filtered[l] = s[:rows, :cols]


def gradient_kernel(n_other, *refs):
    flags, vertical, control, filtered = refs[:4]
    others = refs[4 : 4 + n_other]
    gradient, partial = refs[4 + n_other :]
    layers, rows, cols = control.shape
    total = jnp.zeros((8, LANES), f32)
    for m in range(layers):
        g = control[m] + blend(flags, vertical, filtered, others, m, True)
        gradient[m] = g
        square = g * g
        for r in range(0, rows, 8):
            for c in range(0, cols, LANES):
                total = total + square[r : r + 8, c : c + LANES]
    total = jnp.sum(total, axis=0, keepdims=True)
    partial[...] = jnp.broadcast_to(total[None], partial.shape)


def direction_kernel(cell_count, gradient, sums, previous, previous_square, direction):
    square = jnp.sum(sums[...]) / cell_count
    factor = square / previous_square[0]
    direction[...] = factor * previous[...] - gradient[...]


def local(
    control,
    vertical,
    spread,
    error_scale,
    wind_lon,
    wind_lat,
    obs_block,
    obs_platform,
    obs_count,
    interp,
    innovation,
    error_inverse,
    previous_direction,
    previous_square,
):
    n_lat, n_lon, n_lev = (lax.axis_size(a) for a in ("lat", "lon", "lev"))
    lat, lev = lax.axis_index("lat"), lax.axis_index("lev")
    layers, rows, cols = control.shape
    ext_rows, ext_cols = rows + 8, cols + LANES
    owners = obs_count.shape[-1]
    slots = obs_block.shape[-1]
    width = interp.shape[-1]
    count = owners * slots
    blocks = obs_block.reshape(count)
    weights = interp.reshape(count, width, width)
    flags = jnp.stack([lat % 2, lat == 0, lat == n_lat - 1, lev]).astype(jnp.int32)
    limit = (16 << 20) + 3 * weights.size * 4

    def from_levs(field):
        return [
            lax.ppermute(field, "lev", [(i, (i + k) % n_lev) for i in range(n_lev)]) for k in range(1, n_lev)
        ]

    def partner(a, phase):
        step = 1 if (a % 2 == 0) == (phase == 1) else -1
        return (a + step) % n_lat

    def exchange(field, phase, lon_step):
        pairs = []
        for a in range(n_lat):
            for b in range(n_lon):
                to = partner(a, phase) if phase else a
                pairs.append((a * n_lon + b, to * n_lon + (b + lon_step) % n_lon))
        return lax.ppermute(field, ("lat", "lon"), pairs)

    lon_steps = (1,) if n_lon == 2 else (1, -1)

    def from_sides(field, phase, first_lanes):
        if n_lon == 2:
            return exchange(field, phase, 1)
        return jnp.where(first_lanes, exchange(field, phase, -1), exchange(field, phase, 1))

    block_rows = -(-count // LANES)
    lat_fields = sum(WIDTHS) * layers
    lat_rows = -(-(lat_fields + block_rows) // 8) * 8
    lon_rows = rows + -(-block_rows // 8) * 8
    block_tile = jnp.zeros((block_rows * LANES,), f32).at[:count].set(blocks.astype(f32))
    block_tile = block_tile.reshape(block_rows, LANES)

    others = from_levs(control)
    blended, lon_out, lat_1, lat_2, diag_1, diag_2 = call(
        functools.partial(pack_kernel, len(others)),
        [
            shape(layers, rows, cols),
            shape(lon_rows, LANES),
            shape(lat_rows, cols),
            shape(lat_rows, cols),
            shape(lat_rows, LANES),
            shape(lat_rows, LANES),
        ],
        [SMEM, SMEM] + [VMEM] * (6 + len(others)),
        [pltpu.VMEM((lat_rows, cols), f32)] * 2,
    )(flags, vertical, control, *others, spread, error_scale, wind_lon, wind_lat, block_tile)

    lane = jnp.arange(LANES, dtype=jnp.int32)
    lat_in = {phase: exchange(phase_out, phase, 0) for phase, phase_out in ((1, lat_1), (2, lat_2))}
    lon_raw = {step: exchange(lon_out, 0, -step) for step in lon_steps}
    diag_raw = {
        (phase, step): exchange(phase_out, phase, -step)
        for phase, phase_out in ((1, diag_1), (2, diag_2))
        for step in lon_steps
    }
    if n_lon == 2:
        lon_in = lon_raw[1]
        diag_in = {phase: diag_raw[phase, 1] for phase in (1, 2)}
    else:
        lon_in = jnp.where(lane % 8 < HALO, lon_raw[1], lon_raw[-1])
        diag_in = {
            phase: jnp.where(lane < LANES // 2, diag_raw[phase, 1], diag_raw[phase, -1]) for phase in (1, 2)
        }

    per = cols // LANES
    at = (blocks // (rows * per) * per + blocks % per) * ext_rows + (blocks // per) % rows
    live = jnp.arange(slots, dtype=jnp.int32)[None, :] < obs_count.reshape(owners)[:, None]
    live = jnp.broadcast_to(live.reshape(count, 1), (count, width)).astype(f32)
    half = -(-slots // 4) * 4
    platform = jnp.zeros((owners, 2 * half, width), f32)
    platform = platform.at[:, half : half + slots, :].set(
        jnp.broadcast_to(obs_platform.reshape(owners, slots, 1).astype(f32), (owners, slots, width))
    )
    ext = shape(layers, ext_rows, ext_cols)
    sent, ext_spread, ext_scale, ext_e, ext_n = call(
        forward_kernel,
        [shape(owners, 2 * half, width), ext, ext, ext, ext],
        [SMEM] * 2 + [VMEM] * 14,
        [pltpu.VMEM((layers, ext_rows, ext_cols), f32), pltpu.VMEM((layers * ext_rows * per, LANES), f32)],
        limit,
    )(
        flags, at, blended, spread, wind_lon, wind_lat, error_scale,
        lon_in, lat_in[1], lat_in[2], diag_in[1], diag_in[2],
        weights, innovation.reshape(count, width), live, platform,
    )

    arrived = lax.all_to_all(sent, ("lat", "lon"), split_axis=0, concat_axis=0, tiled=True)
    matrices = error_inverse.reshape(error_inverse.shape[-3:])
    result = call(weigh_kernel, shape(owners, 2 * half, width), [VMEM] * 2)(arrived, matrices)
    returned = lax.all_to_all(result, ("lat", "lon"), split_axis=0, concat_axis=0, tiled=True)
    adjoint_obs = call(
        functools.partial(transpose_kernel, slots), shape(count, width), [VMEM] * 2, (), limit
    )(returned, weights)

    odd = lat % 2
    wide = lane[None, :] < LANES // 2
    sources, targets, masks = [], [], []

    def numbers(tile, begin):
        return tile[begin : begin + block_rows, :LANES].reshape(-1)[:count].astype(jnp.int32)

    def add_source(values, block, is_north, is_south, lon_step):
        block_layer, row, block_col = block // (rows * per), (block // per) % rows, block % per
        place_row = jnp.where(is_north, rows + row, jnp.where(is_south, row + 8, row))
        valid = jnp.where(is_north, row < HALO, jnp.where(is_south, row >= rows - HALO, True))
        valid = valid & ~(is_north & (lat == n_lat - 1)) & ~(is_south & (lat == 0))
        keep = jnp.ones((count, LANES), f32)
        if lon_step:
            at_first, at_last = block_col == 0, block_col == per - 1
            if n_lon > 2:
                at_first, at_last = at_first & (lon_step == 1), at_last & (lon_step == -1)
            valid = valid & (at_first | at_last)
            keep = jnp.where(at_first[:, None], wide, ~wide).astype(f32)
            block_col = jnp.full_like(block_col, per)
        place = (block_layer * (per + 1) + block_col) * ext_rows + place_row
        sources.append(values)
        targets.append(jnp.where(valid, place, -1))
        masks.append(keep)

    no = jnp.zeros((), bool)
    add_source(adjoint_obs, blocks, no, no, 0)
    for step in lon_steps:
        add_source(exchange(adjoint_obs, 0, -step), numbers(lon_raw[step], rows), no, no, step)
    for phase in (1, 2):
        is_north = (odd == 0) == (phase == 1)
        add_source(exchange(adjoint_obs, phase, 0), numbers(lat_in[phase], lat_fields), is_north, ~is_north, 0)
        for step in lon_steps:
            add_source(
                exchange(adjoint_obs, phase, -step), numbers(diag_raw[phase, step], lat_fields), is_north, ~is_north, step
            )
    target = jnp.concatenate(targets)[None, :]
    lane_mask = jnp.concatenate(masks, axis=0)

    filtered = call(
        functools.partial(adjoint_kernel, len(sources)),
        shape(layers, rows, cols),
        [SMEM] + [VMEM] * (6 + len(sources)),
        (),
        limit,
    )(flags, target, lane_mask, *sources, ext_spread, ext_scale, ext_e, ext_n)

    others = from_levs(filtered)
    group = n_lat * n_lon * n_lev
    gradient, partial = call(
        functools.partial(gradient_kernel, len(others)),
        [shape(layers, rows, cols), shape(group, 1, LANES)],
        [SMEM] * 2 + [VMEM] * (2 + len(others)),
    )(flags, vertical, control, filtered, *others)
    sums = lax.all_to_all(partial, ("lat", "lon", "lev"), split_axis=0, concat_axis=0, tiled=True)
    direction = call(
        functools.partial(direction_kernel, float(control.size * group)),
        shape(layers, rows, cols),
        [VMEM] * 3 + [SMEM],
    )(gradient, sums, previous_direction, previous_square)
    return (gradient, direction)


def solution(mesh):
    field = P("lev", ("member", "lat"), "lon")
    shared = P("lev", "lat", "lon")
    placed = (
        field,
        P(),
        shared,
        shared,
        field,
        field,
        P("lev", "lat", "lon", None, None),
        P("lev", "lat", "lon", None, None),
        P("lev", "lat", "lon", None),
        P("lev", "lat", "lon", None, None, None, None),
        P("lev", ("member", "lat"), "lon", None, None, None),
        P("lat", "lon", None, None, None),
        field,
        P("member"),
    )
    return jax.shard_map(local, mesh=mesh, in_specs=placed, out_specs=(field, field), check_vma=False)
```

time: 194 us -> 84.7 us (0.44)
  blocking collectives: 43.9 us -> 0 us
  waiting for transfers between devices: 68.9 us -> 26.6 us
  starting transfers between devices: 58.6 us -> 29.3 us
  Pallas kernels: 0 us -> 9.05 us
  local copies, waits for them, and re-layouts: 5 us -> 13.1 us
  matrix products: 6.55 us -> 0 us
  other arithmetic: 7.55 us -> 4.43 us
    ppermute x32 -> x12, waiting for transfers between devices: 62.5 us -> 9.02 us  [the longest x10 7.55 us: exchange(): return lax.ppermute(field, ('lat', 'lon'), pairs)]
    ppermute x32 -> x12, starting transfers between devices: 51.9 us -> 17.2 us  [the longest x10 16.6 us: exchange(): return lax.ppermute(field, ('lat', 'lon'), pairs)]
    psum x1 -> x0, blocking collectives: 30.2 us -> none  [local(): sum_squares = lax.psum(jnp.sum(gradient * gradient), ('lat', 'lon', 'lev'))]
    all_to_all x2 -> x3, waiting for transfers between devices: 6.44 us -> 17.6 us  [the longest x1 6.59 us: local(): lax.all_to_all(result, ('lat', 'lon'), split_axis=0, concat_axis=0, tiled...]
    unnamed x29 -> x58, local copies, waits for them, and re-layouts: 2.88 us -> 12.5 us
    pallas_call x0 -> x7, Pallas kernels: none -> 9.05 us  [the longest x1 2.54 us: local(): call(forward_kernel, [shape(owners, 2 * half, width), ext, ext, ext, ext]...]
    all_to_all x1 -> x0, blocking collectives: 8.88 us -> none  [local(): lax.all_to_all(result, ('lat', 'lon'), split_axis=0, concat_axis=0, tiled...]
    dot_general x5 -> x0, matrix products: 6.55 us -> none  [the longest x1 2.22 us: local(): jnp.einsum('lm,lij->mij', own_columns, all_layers(filtered), precision=hi...]
  transfers between devices with their start and end apart: 34 -> 15, of which waited for: 25 -> 6; matrix products, arithmetic and copies ran while one was open for 1% -> 7% of each run, Pallas kernels for 0% -> 0%
where the time goes in v1:
time: 84.7 us; the launch traced here: 84 us
  starting transfers between devices  29.3 us (35%)
  waiting for transfers between devices  26.6 us (31%)
  local copies, waits for them, and re-layouts  13.1 us (15%)
  Pallas kernels  9.05 us (11%)
  other arithmetic  4.43 us (5%)
  between operations  1.49 us (2%)
    ppermute x10, starting transfers between devices, exchange(): return lax.ppermute(field, ('lat', 'lon'), pairs)  16.6 us
    unnamed x58, local copies, waits for them, and re-layouts  12.5 us
    ppermute x10, waiting for transfers between devices, exchange(): return lax.ppermute(field, ('lat', 'lon'), pairs)  7.55 us
    all_to_all x1, waiting for transfers between devices, local(): lax.all_to_all(result, ('lat', 'lon'), split_axis=0, concat_axis=0, tiled...  6.59 us
    all_to_all x1, waiting for transfers between devices, local(): lax.all_to_all(partial, ('lat', 'lon', 'lev'), split_axis=0, concat_axis=...  5.68 us
    all_to_all x1, starting transfers between devices, local(): lax.all_to_all(partial, ('lat', 'lon', 'lev'), split_axis=0, concat_axis=...  5.45 us
    all_to_all x1, waiting for transfers between devices, local(): lax.all_to_all(sent, ('lat', 'lon'), split_axis=0, concat_axis=0, tiled=T...  5.28 us
    all_to_all x1, starting transfers between devices, local(): lax.all_to_all(sent, ('lat', 'lon'), split_axis=0, concat_axis=0, tiled=T...  3.34 us
  transfers between devices with their start and end apart: 15, of which 6 were waited for; matrix products, arithmetic and copies ran while one was open for 7% of the time, Pallas kernels for 0%

profile of v1, /device:TPU:0, one launch (start us, length us, event | category | flops | bytes accessed | tf_op | source)
XLA Modules:
  0.0 84.0 jit_solution(17327390572069227776)
XLA Ops:
  4.4 0.9 %copy-done.1 = f32[2,56,512]{2,1,0:T(8,128)S(1)} copy-done((f32[2,56,512]{2,1,0:T(8,128)S(1)}, f32[2,56,512]{2,1,0:T(8,128)}, u32[]{:S(2)}) %copy-start.1) | copy-done | bytes 229400
  5.3 0.9 %copy-done.3 = f32[2,56,512]{2,1,0:T(8,128)S(1)} copy-done((f32[2,56,512]{2,1,0:T(8,128)S(1)}, f32[2,56,512]{2,1,0:T(8,128)}, u32[]{:S(2)}) %copy-start.3) | copy-done | bytes 229400
  7.2 0.9 %copy-done.7 = f32[2,56,512]{2,1,0:T(8,128)S(1)} copy-done((f32[2,56,512]{2,1,0:T(8,128)S(1)}, f32[2,56,512]{2,1,0:T(8,128)}, u32[]{:S(2)}) %copy-start.7) | copy-done | bytes 229400
  8.1 0.9 %copy-done.9 = f32[2,56,512]{2,1,0:T(8,128)S(1)} copy-done((f32[2,56,512]{2,1,0:T(8,128)S(1)}, f32[2,56,512]{2,1,0:T(8,128)}, u32[]{:S(2)}) %copy-start.9) | copy-done | bytes 229400
  11.2 3.6 %collective-permute-start.3 = (f32[40,128]{1,0:T(8,128)S(1)}, f32[40,128]{1,0:T(8,128)S(1)}, u32[]{:S(2)}, u32[]{:S(2)}) collective-permute-start(f32[40,128]{1,0:T(8,128)S(1)} %get-tuple-element.41), channel_id=1, source_target_pairs={{0,6},{2,4},{4,2},{6,0},{8,14},{10,12},{12,10},{14,8},{1,7},{3,5},... | collective-permute-start | bytes 61448 | tf_op jit(solution)/shard_map/ppermute | solution.py:358
  15.6 3.6 %collective-permute-start.4 = (f32[40,512]{1,0:T(8,128)S(1)}, f32[40,512]{1,0:T(8,128)S(1)}, u32[]{:S(2)}, u32[]{:S(2)}) collective-permute-start(f32[40,512]{1,0:T(8,128)S(1)} %get-tuple-element.42), channel_id=1, source_target_pairs={{0,12},{2,14},{4,8},{6,10},{8,4},{10,6},{12,0},{14,2},{1,13},{3,15... | collective-permute-start | bytes 245768 | tf_op jit(solution)/shard_map/ppermute | solution.py:358
  19.7 1.1 %collective-permute-start.5 = (f32[40,128]{1,0:T(8,128)S(1)}, f32[40,128]{1,0:T(8,128)S(1)}, u32[]{:S(2)}, u32[]{:S(2)}) collective-permute-start(f32[40,128]{1,0:T(8,128)S(1)} %get-tuple-element.43), channel_id=1, source_target_pairs={{0,14},{2,12},{4,10},{6,8},{8,6},{10,4},{12,2},{14,0},{1,15},{3,13... | collective-permute-start | bytes 61448 | tf_op jit(solution)/shard_map/ppermute | solution.py:358
  20.9 5.3 %collective-permute-done.5.refs_11_ = f32[40,128]{1,0:T(8,128)S(1)} collective-permute-done((f32[40,128]{1,0:T(8,128)S(1)}, f32[40,128]{1,0:T(8,128)S(1)}, u32[]{:S(2)}, u32[]{:S(2)}) %collective-permute-start.5) | collective-permute-done | bytes 20512 | tf_op jit(solution)/shard_map/ppermute | solution.py:358
  31.2 2.5 %shard_map.150 = (f32[8,8,128]{2,1,0:T(8,128)S(1)}, f32[2,64,640]{2,1,0:T(8,128)S(1)}, f32[2,64,640]{2,1,0:T(8,128)S(1)}, f32[2,64,640]{2,1,0:T(8,128)S(1)}, f32[2,64,640]{2,1,0:T(8,128)S(1)}) custom-call(s32[4]{0:T(128)S(1)} %pad_add_fusion.refs_0_, s32[16]{0:T(128)S(1)} %get-tuple-element.52.refs_1_, f32[2,56,512]{2,1,0:T(8,128)S(1)} %copy-done.13, ...), custom_call_target="tpu_custom_call" | custom-call | flops 1048576 | bytes 1048576 | tf_op jit(solution)/shard_map/pallas_call | solution.py:416
  34.4 3.3 %all-to-all-start = ((f32[8,8,128]{2,1,0:T(8,128)}), f32[8,8,128]{2,1,0:T(8,128)S(1)}, u32[]{:S(2)}, u32[]{:S(2)}) async-start(f32[8,8,128]{2,1,0:T(8,128)} %copy-done.19), calls=%async_computation | async-start | bytes 65536 | tf_op jit(solution)/shard_map/all_to_all | solution.py:428
  39.1 5.3 %all-to-all-done.arrived = f32[8,8,128]{2,1,0:T(8,128)S(1)} async-done(((f32[8,8,128]{2,1,0:T(8,128)}), f32[8,8,128]{2,1,0:T(8,128)S(1)}, u32[]{:S(2)}, u32[]{:S(2)}) %all-to-all-start) | async-done | bytes 32800 | tf_op jit(solution)/shard_map/all_to_all | solution.py:428
  44.4 1.2 %shard_map.151 = f32[8,8,128]{2,1,0:T(8,128)} custom-call(f32[8,8,128]{2,1,0:T(8,128)S(1)} %all-to-all-done.arrived, f32[8,128,128]{2,1,0:T(8,128)S(1)} %bitcast.52), custom_call_target="tpu_custom_call" | custom-call | flops 1048576 | bytes 1048576 | tf_op jit(solution)/shard_map/pallas_call | solution.py:430
  45.6 3.3 %all-to-all-start.1 = ((f32[8,8,128]{2,1,0:T(8,128)}), f32[8,8,128]{2,1,0:T(8,128)S(1)}, u32[]{:S(2)}, u32[]{:S(2)}) async-start(f32[8,8,128]{2,1,0:T(8,128)} %shard_map.151), calls=%async_computation.1 | async-start | bytes 65536 | tf_op jit(solution)/shard_map/all_to_all | solution.py:431
  49.0 6.6 %all-to-all-done.1.returned = f32[8,8,128]{2,1,0:T(8,128)S(1)} async-done(((f32[8,8,128]{2,1,0:T(8,128)}), f32[8,8,128]{2,1,0:T(8,128)S(1)}, u32[]{:S(2)}, u32[]{:S(2)}) %all-to-all-start.1) | async-done | bytes 32800 | tf_op jit(solution)/shard_map/all_to_all | solution.py:431
  56.8 1.4 %collective-permute-start.6 = (f32[16,128]{1,0:T(8,128)S(1)}, f32[16,128]{1,0:T(8,128)S(1)}, u32[]{:S(2)}, u32[]{:S(2)}) collective-permute-start(f32[16,128]{1,0:T(8,128)S(1)} %shard_map.152.refs_3_), channel_id=1, source_target_pairs={{0,2},{2,0},{4,6},{6,4},{8,10},{10,8},{12,14},{14,12},{1,3},{3,1},... | collective-permute-start | bytes 24584 | tf_op jit(solution)/shard_map/ppermute | solution.py:358
  58.7 1.6 %collective-permute-start.8 = (f32[16,128]{1,0:T(8,128)S(1)}, f32[16,128]{1,0:T(8,128)S(1)}, u32[]{:S(2)}, u32[]{:S(2)}) collective-permute-start(f32[16,128]{1,0:T(8,128)S(1)} %shard_map.152.refs_3_), channel_id=1, source_target_pairs={{0,6},{2,4},{4,2},{6,0},{8,14},{10,12},{12,10},{14,8},{1,7},{3,5},... | collective-permute-start | bytes 24584 | tf_op jit(solution)/shard_map/ppermute | solution.py:358
  60.3 3.1 %collective-permute-start.9 = (f32[16,128]{1,0:T(8,128)S(1)}, f32[16,128]{1,0:T(8,128)S(1)}, u32[]{:S(2)}, u32[]{:S(2)}) collective-permute-start(f32[16,128]{1,0:T(8,128)S(1)} %shard_map.152.refs_3_), channel_id=1, source_target_pairs={{0,12},{2,14},{4,8},{6,10},{8,4},{10,6},{12,0},{14,2},{1,13},{3,15... | collective-permute-start | bytes 24584 | tf_op jit(solution)/shard_map/ppermute | solution.py:358
  63.5 2.2 %collective-permute-done.9.refs_7_ = f32[16,128]{1,0:T(8,128)S(1)} collective-permute-done((f32[16,128]{1,0:T(8,128)S(1)}, f32[16,128]{1,0:T(8,128)S(1)}, u32[]{:S(2)}, u32[]{:S(2)}) %collective-permute-start.9) | collective-permute-done | bytes 8224 | tf_op jit(solution)/shard_map/ppermute | solution.py:358
  65.7 1.8 %shard_map.153.refs_3_ = f32[2,56,512]{2,1,0:T(8,128)S(1)} custom-call(s32[4]{0:T(128)S(1)} %pad_add_fusion.refs_0_, s32[1,96]{1,0:T(1,128)S(1)} %bitcast.54, f32[96,128]{1,0:T(8,128)S(1)} %copy-done.17, f32[16,128]{1,0:T(8,128)S(1)} %shard_map.152.refs_3_, f32[16,128]{1,0:T(8,128)S(1)} %collective-permute-done.6.refs_4_, ...), custom_call_target="tpu_custom_call" | custom-call | flops 1048576 | bytes 1048576 | tf_op jit(solution)/shard_map/pallas_call | solution.py:475
  67.6 1.5 %collective-permute-done.11.refs_4_ = f32[2,56,512]{2,1,0:T(8,128)S(1)} collective-permute-done((f32[2,56,512]{2,1,0:T(8,128)S(1)}, f32[2,56,512]{2,1,0:T(8,128)S(1)}, u32[]{:S(2)}, u32[]{:S(2)}) %collective-permute-start.11) | collective-permute-done | bytes 229408 | tf_op jit(solution)/shard_map/ppermute | solution.py:345
  69.1 1.4 %shard_map.154 = (f32[2,56,512]{2,1,0:T(8,128)}, f32[16,1,128]{2,1,0:T(1,128)}) custom-call(s32[4]{0:T(128)S(1)} %pad_add_fusion.refs_0_, f32[4,4]{1,0:T(4,128)S(1)} %copy-done.24, f32[2,56,512]{2,1,0:T(8,128)S(1)} %copy-done.10, f32[2,56,512]{2,1,0:T(8,128)S(1)} %shard_map.153.refs_3_, f32[2,56,512]{2,1,0:T(8,128)S(1)} %collective-permute-done.11.refs_4_), custom_call_target="tpu_custom_call" | custom-call | flops 1048576 | bytes 1048576 | tf_op jit(solution)/shard_map/pallas_call | solution.py:485
  70.4 5.5 %all-to-all-start.2 = ((f32[16,1,128]{2,1,0:T(1,128)}), f32[16,1,128]{2,1,0:T(1,128)S(1)}, u32[]{:S(2)}, u32[]{:S(2)}) async-start(f32[16,1,128]{2,1,0:T(1,128)} %get-tuple-element.51), calls=%async_computation.2 | async-start | bytes 16384 | tf_op jit(solution)/shard_map/all_to_all | solution.py:490
  76.5 5.7 %all-to-all-done.2.sums = f32[16,1,128]{2,1,0:T(1,128)S(1)} async-done(((f32[16,1,128]{2,1,0:T(1,128)}), f32[16,1,128]{2,1,0:T(1,128)S(1)}, u32[]{:S(2)}, u32[]{:S(2)}) %all-to-all-start.2) | async-done | bytes 8224 | tf_op jit(solution)/shard_map/all_to_all | solution.py:490
  82.2 0.9 %copy-done.15 = f32[2,56,512]{2,1,0:T(8,128)S(1)} copy-done((f32[2,56,512]{2,1,0:T(8,128)S(1)}, f32[2,56,512]{2,1,0:T(8,128)}, u32[]{:S(2)}) %copy-start.15) | copy-done | bytes 229400
  (99 shorter events, 17.9 us)
Async XLA Ops:
  0.6 27.7 %copy-start = (f32[1,1,1,8,2,128,128]{6,5,4,3,2,1,0:T(8,128)S(1)}, f32[1,1,1,8,2,128,128]{6,5,4,3,2,1,0:T(8,128)}, u32[]{:S(2)}) copy-start(f32[1,1,1,8,2,128,128]{6,5,4,3,2,1,0:T(8,128)} %param.27) | copy-start | bytes 3145732
  0.6 3.7 %collective-permute-start = (f32[2,56,512]{2,1,0:T(8,128)}, f32[2,56,512]{2,1,0:T(8,128)S(1)}, u32[]{:S(2)}, u32[]{:S(2)}) collective-permute-start(f32[2,56,512]{2,1,0:T(8,128)} %refs_2_.3), channel_id=1, source_target_pairs={{0,1},{1,0},{2,3},{3,2},{4,5},{5,4},{6,7},{7,6},{8,9},{9,8},{10,11... | collective-permute-start | bytes 688136 | tf_op jit(solution)/shard_map/ppermute | solution.py:345
  9.8 18.6 %copy-start.2 = (f32[2,56,512]{2,1,0:T(8,128)S(1)}, f32[2,56,512]{2,1,0:T(8,128)}, u32[]{:S(2)}) copy-start(f32[2,56,512]{2,1,0:T(8,128)} %refs_3_.1) | copy-start | bytes 688132
  9.8 18.6 %copy-start.4 = (f32[2,56,512]{2,1,0:T(8,128)S(1)}, f32[2,56,512]{2,1,0:T(8,128)}, u32[]{:S(2)}) copy-start(f32[2,56,512]{2,1,0:T(8,128)} %refs_6_.3) | copy-start | bytes 688132
  11.2 9.6 %collective-permute-start.3 = (f32[40,128]{1,0:T(8,128)S(1)}, f32[40,128]{1,0:T(8,128)S(1)}, u32[]{:S(2)}, u32[]{:S(2)}) collective-permute-start(f32[40,128]{1,0:T(8,128)S(1)} %get-tuple-element.41), channel_id=1, source_target_pairs={{0,6},{2,4},{4,2},{6,0},{8,14},{10,12},{12,10},{14,8},{1,7},{3,5},... | collective-permute-start | bytes 61448 | tf_op jit(solution)/shard_map/ppermute | solution.py:358
  15.1 13.2 %collective-permute-start.2 = (f32[40,512]{1,0:T(8,128)S(1)}, f32[40,512]{1,0:T(8,128)S(1)}, u32[]{:S(2)}, u32[]{:S(2)}) collective-permute-start(f32[40,512]{1,0:T(8,128)S(1)} %get-tuple-element.40), channel_id=1, source_target_pairs={{0,4},{2,6},{4,0},{6,2},{8,12},{10,14},{12,8},{14,10},{1,5},{3,7},... | collective-permute-start | bytes 245768 | tf_op jit(solution)/shard_map/ppermute | solution.py:358
  15.6 12.7 %collective-permute-start.4 = (f32[40,512]{1,0:T(8,128)S(1)}, f32[40,512]{1,0:T(8,128)S(1)}, u32[]{:S(2)}, u32[]{:S(2)}) collective-permute-start(f32[40,512]{1,0:T(8,128)S(1)} %get-tuple-element.42), channel_id=1, source_target_pairs={{0,12},{2,14},{4,8},{6,10},{8,4},{10,6},{12,0},{14,2},{1,13},{3,15... | collective-permute-start | bytes 245768 | tf_op jit(solution)/shard_map/ppermute | solution.py:358
  19.2 7.7 %collective-permute-start.1 = (f32[64,128]{1,0:T(8,128)S(1)}, f32[64,128]{1,0:T(8,128)S(1)}, u32[]{:S(2)}, u32[]{:S(2)}) collective-permute-start(f32[64,128]{1,0:T(8,128)S(1)} %get-tuple-element.39), channel_id=1, source_target_pairs={{0,2},{2,0},{4,6},{6,4},{8,10},{10,8},{12,14},{14,12},{1,3},{3,1},... | collective-permute-start | bytes 98312 | tf_op jit(solution)/shard_map/ppermute | solution.py:358
  19.7 6.5 %collective-permute-start.5 = (f32[40,128]{1,0:T(8,128)S(1)}, f32[40,128]{1,0:T(8,128)S(1)}, u32[]{:S(2)}, u32[]{:S(2)}) collective-permute-start(f32[40,128]{1,0:T(8,128)S(1)} %get-tuple-element.43), channel_id=1, source_target_pairs={{0,14},{2,12},{4,10},{6,8},{8,6},{10,4},{12,2},{14,0},{1,15},{3,13... | collective-permute-start | bytes 61448 | tf_op jit(solution)/shard_map/ppermute | solution.py:358
  20.9 6.7 %copy-start.20 = (f32[40,128]{1,0:T(8,128)}, f32[40,128]{1,0:T(8,128)S(1)}, u32[]{:S(2)}) copy-start(f32[40,128]{1,0:T(8,128)S(1)} %collective-permute-done.3.refs_10_) | copy-start | bytes 61444
  31.2 13.2 %copy-start.11 = (f32[1,1,8,128,128]{4,3,2,1,0:T(8,128)S(1)}, f32[1,1,8,128,128]{4,3,2,1,0:T(8,128)}, u32[]{:S(2)}) copy-start(f32[1,1,8,128,128]{4,3,2,1,0:T(8,128)} %param.29) | copy-start | bytes 1572868
  34.4 10.0 %all-to-all-start = ((f32[8,8,128]{2,1,0:T(8,128)}), f32[8,8,128]{2,1,0:T(8,128)S(1)}, u32[]{:S(2)}, u32[]{:S(2)}) async-start(f32[8,8,128]{2,1,0:T(8,128)} %copy-done.19), calls=%async_computation | async-start | bytes 65536 | tf_op jit(solution)/shard_map/all_to_all | solution.py:428
  45.6 10.0 %all-to-all-start.1 = ((f32[8,8,128]{2,1,0:T(8,128)}), f32[8,8,128]{2,1,0:T(8,128)S(1)}, u32[]{:S(2)}, u32[]{:S(2)}) async-start(f32[8,8,128]{2,1,0:T(8,128)} %shard_map.151), calls=%async_computation.1 | async-start | bytes 65536 | tf_op jit(solution)/shard_map/all_to_all | solution.py:431
  55.6 10.1 %copy-start.17 = (f32[96,128]{1,0:T(8,128)S(1)}, f32[96,128]{1,0:T(8,128)}, u32[]{:S(2)}) copy-start(f32[96,128]{1,0:T(8,128)} %copy-done.16) | copy-start | bytes 147460
  56.1 7.3 %copy-start.25 = (s32[16]{0:T(128)S(1)}, s32[16]{0:T(128)}, u32[]{:S(2)}) copy-start(s32[16]{0:T(128)} %and_select_fusion.11) | copy-start | bytes 196
  56.1 7.4 %collective-permute-start.10 = (f32[16,128]{1,0:T(8,128)S(1)}, f32[16,128]{1,0:T(8,128)S(1)}, u32[]{:S(2)}, u32[]{:S(2)}) collective-permute-start(f32[16,128]{1,0:T(8,128)S(1)} %shard_map.152.refs_3_), channel_id=1, source_target_pairs={{0,14},{2,12},{4,10},{6,8},{8,6},{10,4},{12,2},{14,0},{1,15},{3,13... | collective-permute-start | bytes 24584 | tf_op jit(solution)/shard_map/ppermute | solution.py:358
  56.8 6.7 %collective-permute-start.6 = (f32[16,128]{1,0:T(8,128)S(1)}, f32[16,128]{1,0:T(8,128)S(1)}, u32[]{:S(2)}, u32[]{:S(2)}) collective-permute-start(f32[16,128]{1,0:T(8,128)S(1)} %shard_map.152.refs_3_), channel_id=1, source_target_pairs={{0,2},{2,0},{4,6},{6,4},{8,10},{10,8},{12,14},{14,12},{1,3},{3,1},... | collective-permute-start | bytes 24584 | tf_op jit(solution)/shard_map/ppermute | solution.py:358
  58.1 5.3 %collective-permute-start.7 = (f32[16,128]{1,0:T(8,128)S(1)}, f32[16,128]{1,0:T(8,128)S(1)}, u32[]{:S(2)}, u32[]{:S(2)}) collective-permute-start(f32[16,128]{1,0:T(8,128)S(1)} %shard_map.152.refs_3_), channel_id=1, source_target_pairs={{0,4},{2,6},{4,0},{6,2},{8,12},{10,14},{12,8},{14,10},{1,5},{3,7},... | collective-permute-start | bytes 24584 | tf_op jit(solution)/shard_map/ppermute | solution.py:358
  58.7 4.8 %collective-permute-start.8 = (f32[16,128]{1,0:T(8,128)S(1)}, f32[16,128]{1,0:T(8,128)S(1)}, u32[]{:S(2)}, u32[]{:S(2)}) collective-permute-start(f32[16,128]{1,0:T(8,128)S(1)} %shard_map.152.refs_3_), channel_id=1, source_target_pairs={{0,6},{2,4},{4,2},{6,0},{8,14},{10,12},{12,10},{14,8},{1,7},{3,5},... | collective-permute-start | bytes 24584 | tf_op jit(solution)/shard_map/ppermute | solution.py:358
  60.3 5.4 %collective-permute-start.9 = (f32[16,128]{1,0:T(8,128)S(1)}, f32[16,128]{1,0:T(8,128)S(1)}, u32[]{:S(2)}, u32[]{:S(2)}) collective-permute-start(f32[16,128]{1,0:T(8,128)S(1)} %shard_map.152.refs_3_), channel_id=1, source_target_pairs={{0,12},{2,14},{4,8},{6,10},{8,4},{10,6},{12,0},{14,2},{1,13},{3,15... | collective-permute-start | bytes 24584 | tf_op jit(solution)/shard_map/ppermute | solution.py:358
  65.7 3.4 %copy-start.24 = (f32[4,4]{1,0:T(4,128)S(1)}, f32[4,4]{1,0:T(4,128)}, u32[]{:S(2)}) copy-start(f32[4,4]{1,0:T(4,128)} %refs_1_.3) | copy-start | bytes 196
  67.5 14.7 %copy-start.14 = (f32[2,56,512]{2,1,0:T(8,128)S(1)}, f32[2,56,512]{2,1,0:T(8,128)}, u32[]{:S(2)}) copy-start(f32[2,56,512]{2,1,0:T(8,128)} %previous.1) | copy-start | bytes 688132
  67.5 1.6 %collective-permute-start.11 = (f32[2,56,512]{2,1,0:T(8,128)S(1)}, f32[2,56,512]{2,1,0:T(8,128)S(1)}, u32[]{:S(2)}, u32[]{:S(2)}) collective-permute-start(f32[2,56,512]{2,1,0:T(8,128)S(1)} %shard_map.153.refs_3_), channel_id=1, source_target_pairs={{0,1},{1,0},{2,3},{3,2},{4,5},{5,4},{6,7},{7,6},{8,9},{9,8},{10,11... | collective-permute-start | bytes 688136 | tf_op jit(solution)/shard_map/ppermute | solution.py:345
  70.4 11.8 %all-to-all-start.2 = ((f32[16,1,128]{2,1,0:T(1,128)}), f32[16,1,128]{2,1,0:T(1,128)S(1)}, u32[]{:S(2)}, u32[]{:S(2)}) async-start(f32[16,1,128]{2,1,0:T(1,128)} %get-tuple-element.51), calls=%async_computation.2 | async-start | bytes 16384 | tf_op jit(solution)/shard_map/all_to_all | solution.py:490
  (18 other events, 18.2 us)

commit v2 on v1

v2 whole, which is shorter than its diff:
```python
import functools
import jax
import jax.numpy as jnp
from jax import lax
from jax.experimental import pallas as pl
from jax.experimental.pallas import tpu as pltpu
from jax.sharding import PartitionSpec as P

FILTER = 2
STEPS = 2
HALO = 4
WIDTHS = (4, 4, 4, 4, 2)
LANES = 128
smoothing = 0.1
diffusion = 0.15
f32 = jnp.float32
bf16 = jnp.bfloat16
VMEM = pl.BlockSpec(memory_space=pltpu.VMEM)
SMEM = pl.BlockSpec(memory_space=pltpu.SMEM)
HBM = pl.BlockSpec(memory_space=pltpu.HBM)
NN = (((1,), (0,)), ((), ()))


def call(kernel, out_shape, in_specs, scratch=(), limit=8 << 20, flops=1 << 20):
    many = isinstance(out_shape, (list, tuple))
    return pl.pallas_call(
        kernel,
        out_shape=out_shape,
        in_specs=in_specs,
        out_specs=[VMEM] * len(out_shape) if many else VMEM,
        scratch_shapes=list(scratch),
        compiler_params=pltpu.CompilerParams(vmem_limit_bytes=limit),
        cost_estimate=pl.CostEstimate(flops=flops, bytes_accessed=1 << 20, transcendentals=0),
    )


def held(*dims, dtype=f32):
    return pltpu.VMEM(dims, dtype)


def shape(*dims):
    return jax.ShapeDtypeStruct(dims, f32)


def split(value):
    high = value.astype(bf16)
    return high, (value - high.astype(f32)).astype(bf16)


def halves(value):
    high, low = split(value)
    return jnp.concatenate(
        [jnp.concatenate([high, high], axis=1), jnp.concatenate([low, jnp.zeros_like(low)], axis=1)], axis=0
    )


def dot(left, right, axis):
    pair = jnp.concatenate(split(right), axis=axis)
    result = lax.dot_general(halves(left), pair, (((1,), (axis,)), ((), ())), preferred_element_type=f32)
    return result[: left.shape[0]] + result[left.shape[0] :]


def for_each(count, body, start):
    if count <= 32:
        for i in range(count):
            start = body(i, start)
        return start
    return lax.fori_loop(0, count, body, start)


def north(x):
    return pltpu.roll(x, x.shape[0] - 1, 0)


def south(x):
    return pltpu.roll(x, 1, 0)


def east(x):
    return pltpu.roll(x, x.shape[1] - 1, 1)


def west(x):
    return pltpu.roll(x, 1, 1)


def smooth(s, spread):
    for repeat in range(FILTER):
        q = spread * s
        s = s + smoothing * spread * (north(q) + south(q) + east(q) + west(q) - 4.0 * q)
    return s


def edge_block(rows):
    lane = lax.broadcasted_iota(jnp.int32, (rows.shape[0], LANES), 1)
    return jnp.where(lane < LANES // 2, rows[:, :LANES], rows[:, rows.shape[1] - LANES :])


def blend(weights, own, others, layer):
    layers = own.shape[0]
    total = None
    for i, source in enumerate([own] + list(others)):
        for m in range(layers):
            at = layer * layers * (1 + len(others)) + i * layers + m
            term = weights[at : at + 1, 0:1] * source[m]
            total = term if total is None else total + term
    return total


def load_kernel(
    vertical, blocks, previous_square, control, spread, wind_e, wind_n, scale, previous, innovation,
    forth, back, square_v, control_v, spread_v, wind_e_v, wind_n_v, scale_v, previous_v, innovation_v,
    lon_out, first, last, vertical_s, blocks_s, square_s, sems,
):
    pairs = (
        (spread, spread_v), (wind_e, wind_e_v), (wind_n, wind_n_v), (scale, scale_v), (blocks, blocks_s),
        (vertical, vertical_s), (previous_square, square_s), (control, control_v),
        (innovation, innovation_v), (previous, previous_v),
    )
    copies = [pltpu.make_async_copy(a, b, sems.at[i]) for i, (a, b) in enumerate(pairs)]
    for copy in copies:
        copy.start()
    layers, rows, cols = control.shape
    slots, owners = blocks.shape
    for copy in copies[:5]:
        copy.wait()
    line = lax.broadcasted_iota(jnp.int32, (1, LANES), 1)
    numbers = jnp.full((1, LANES), -1.0, f32)
    for s in range(slots):
        for o in range(owners):
            numbers = jnp.where(line == s * owners + o, blocks_s[s, o].astype(f32), numbers)
    lane = lax.broadcasted_iota(jnp.int32, (rows, LANES), 1)
    packed = jnp.zeros((rows, LANES), f32)
    fields = (spread_v, wind_e_v, wind_n_v, scale_v)
    for i, field in enumerate(fields):
        for l in range(layers):
            packed = lon_item(packed, field[l], (1 + i) * layers + l, lane)
    lon_out[:rows, :] = packed
    lon_out[rows:, :] = jnp.broadcast_to(numbers, (8, LANES))
    for out, low in ((first, True), (last, False)):
        at = WIDTHS[0] * layers
        for field, width in zip(fields, WIDTHS[1:]):
            for l in range(layers):
                begin = 0 if low else rows - width
                out[at : at + width, :] = field[l, begin : begin + width, :]
                at += width
        for c in range(0, cols, LANES):
            out[at:, c : c + LANES] = jnp.broadcast_to(numbers, (out.shape[0] - at, LANES))
    for copy in copies[5:]:
        copy.wait()
    lev, levs = lax.axis_index("lev"), lax.axis_size("lev")
    for l in range(layers):
        for shift in range(levs):
            other = lax.rem(lev + levs - shift, levs)
            for m in range(layers):
                at = (l * levs + shift) * layers + m
                a, b = lev * layers + l, other * layers + m
                forth[at : at + 1, :] = jnp.full((1, LANES), vertical_s[a, b], f32)
                back[at : at + 1, :] = jnp.full((1, LANES), vertical_s[b, a], f32)
    square_v[...] = jnp.full((1, LANES), square_s[0], f32)


def lon_item(packed, field, item, lane):
    cols = field.shape[1]
    tile = jnp.where(lane < LANES // 2, field[:, :LANES], field[:, cols - LANES :])
    if item:
        tile = pltpu.roll(tile, 8 * item, 1)
    return jnp.where((lane + HALO - 8 * item) % LANES < 8, tile, packed)


def pack_kernel(n_other, *refs):
    forth, control, lon_part, first, last = refs[:5]
    others = refs[5 : 5 + n_other]
    blended, lon_out, lat_1, lat_2, diag_1, diag_2 = refs[5 + n_other :]
    layers, rows, cols = control.shape
    packed = lon_part[:rows, :]
    lane = lax.broadcasted_iota(jnp.int32, (rows, LANES), 1)
    firsts, lasts = [], []
    for l in range(layers):
        value = blend(forth, control, others, l)
        blended[l] = value
        packed = lon_item(packed, value, l, lane)
        firsts.append(value[:HALO, :])
        lasts.append(value[rows - HALO :, :])
    lon_out[:rows, :] = packed
    lon_out[rows:, :] = lon_part[rows:, :]
    even = lax.axis_index("lat") % 2 == 0
    for out, diag, use_last in ((lat_1, diag_1, even), (lat_2, diag_2, jnp.logical_not(even))):
        begin = HALO * layers
        flag = jnp.where(use_last, 1, 0)
        for l in range(layers):
            chosen = jnp.full((HALO, cols), flag, jnp.int32) == 1
            out[HALO * l : HALO * (l + 1), :] = jnp.where(chosen, lasts[l], firsts[l])
        chosen = jnp.full((first.shape[0] - begin, cols), flag, jnp.int32) == 1
        out[begin:, :] = jnp.where(chosen, last[begin:, :], first[begin:, :])
        diag[...] = edge_block(out[...])


def at_ends():
    lat = lax.axis_index("lat")
    return lat == 0, lat == lax.axis_size("lat") - 1


def unpack(own, lon_in, lat_1, lat_2, diag_1, diag_2, ext):
    layers, rows, cols = own[0].shape
    lane = lax.broadcasted_iota(jnp.int32, (rows, LANES), 1)
    keep = (lane < HALO) | (lane >= LANES - HALO)
    packed = lon_in[:rows, :]
    item = 0
    for field, out in zip(own, ext):
        for l in range(layers):
            out[l, :rows, :cols] = field[l]
            tile = pltpu.roll(packed, LANES - 8 * item, 1) if item else packed
            out[l, :rows, cols:] = jnp.where(keep, tile, 0.0)
            item += 1
    count = sum(WIDTHS) * layers
    for one, two, begin in ((lat_1, lat_2, 0), (diag_1, diag_2, cols)):
        width = one.shape[1]
        a, b = one[:count, :], two[:count, :]
        even = jnp.full(a.shape, lax.axis_index("lat") % 2, jnp.int32) == 0
        south_end, north_end = at_ends()
        top = jnp.full(a.shape, jnp.where(north_end, 1, 0), jnp.int32) == 0
        bottom = jnp.full(a.shape, jnp.where(south_end, 1, 0), jnp.int32) == 0
        if begin:
            lane_d = lax.broadcasted_iota(jnp.int32, a.shape, 1)
            inside = (lane_d < HALO) | (lane_d >= LANES - HALO)
            top = top & inside
            bottom = bottom & inside
        from_north = jnp.where(top, jnp.where(even, a, b), 0.0)
        from_south = jnp.where(bottom, jnp.where(even, b, a), 0.0)
        at = 0
        for out, l, w in [(e, l, w) for e, w in zip(ext, WIDTHS) for l in range(layers)]:
            if w < HALO:
                out[l, rows : rows + 8, begin : begin + width] = jnp.zeros((8, width), f32)
            out[l, rows : rows + w, begin : begin + width] = from_north[at : at + w, :]
            out[l, rows + 8 - w : rows + 8, begin : begin + width] = from_south[at : at + w, :]
            at += w


def inside_mask(ext_shape):
    south_end, north_end = at_ends()
    row = lax.broadcasted_iota(jnp.int32, ext_shape, 0)
    rows = ext_shape[0] - 8
    north_cut = jnp.where(north_end, rows, rows + 8)
    south_cut = jnp.where(south_end, rows + 4, rows + 8)
    cut = ((row >= north_cut) & (row < rows + 4)) | (row >= south_cut)
    return jnp.where(cut, 0.0, 1.0).astype(f32)


def forward_kernel(
    blocks, platforms, counts, mixed_in, spread_in, wind_e_in, wind_n_in, scale_in,
    lon_in, lat_1, lat_2, diag_1, diag_2, interp, innovation,
    sent, spread, scale, wind_e, wind_n,
    mixed, field, blocks_s, platforms_s, counts_s, sems,
):
    pairs = ((blocks, blocks_s), (platforms, platforms_s), (counts, counts_s))
    copies = [pltpu.make_async_copy(a, b, sems.at[i]) for i, (a, b) in enumerate(pairs)]
    for copy in copies:
        copy.start()
    own = (mixed_in, spread_in, wind_e_in, wind_n_in, scale_in)
    unpack(own, lon_in, lat_1, lat_2, diag_1, diag_2, (mixed, spread, wind_e, wind_n, scale))
    layers, ext_rows, ext_cols = mixed.shape
    rows, per = ext_rows - 8, ext_cols // LANES - 1
    mask = inside_mask((ext_rows, ext_cols))
    for l in range(layers):
        x = scale[l] * smooth(mixed[l], spread[l])
        u, v = 0.5 * wind_e[l], 0.5 * wind_n[l]
        for step in range(STEPS):
            if step:
                x = x * mask
            x = (
                (1.0 - 4.0 * diffusion) * x
                + (diffusion - u) * east(x)
                + (diffusion + u) * west(x)
                + (diffusion - v) * north(x)
                + (diffusion + v) * south(x)
            )
        for c in range(per):
            begin = (l * per + c) * ext_rows
            field[begin : begin + ext_rows, :] = x[:, c * LANES : (c + 1) * LANES]
    for copy in copies:
        copy.wait()
    count, width = innovation.shape
    slots, owners = blocks.shape
    row = lax.broadcasted_iota(jnp.int32, (count, width), 0)

    def body(b, total):
        block = blocks_s[b % slots, b // slots]
        at = (block // (rows * per) * per + block % per) * ext_rows + (block // per) % rows
        left = jnp.where(row == b, jnp.broadcast_to(field[pl.ds(at, 1), :], (count, width)), 0.0)
        return total + dot(left, interp[b], 1)

    departure = for_each(count, body, jnp.zeros((count, width), f32)) - innovation[...]
    half = sent.shape[1] // 2
    sent[...] = jnp.zeros(sent.shape, f32)
    for o in range(owners):
        for s in range(slots):
            live = jnp.full((1, width), counts_s[0, o], jnp.int32) > s
            b = o * slots + s
            sent[o, s : s + 1, :] = jnp.where(live, departure[b : b + 1, :], 0.0)
            sent[o, half + s : half + s + 1, :] = jnp.full((1, width), platforms_s[s, o].astype(f32), f32)


def weigh_kernel(slots, arrived, matrices, out, values, platform):
    tiles, height, width = arrived.shape
    for t in range(tiles):
        for s in range(slots):
            at = s * tiles + t
            values[at : at + 1, :] = arrived[t, s : s + 1, :]
            platform[at : at + 1, :] = arrived[t, height // 2 + s : height // 2 + s + 1, :]
    x, where = values[...], platform[...]
    total = jnp.zeros(x.shape, f32)
    for p in range(matrices.shape[0]):
        total = total + dot(jnp.where(where == float(p), x, 0.0), matrices[p], 1)
    out[...] = jnp.zeros(out.shape, f32)
    for t in range(tiles):
        for s in range(slots):
            at = s * tiles + t
            out[t, s : s + 1, :] = total[at : at + 1, :]


def transpose_kernel(slots, returned, interp, out):
    count, width = out.shape
    row = lax.broadcasted_iota(jnp.int32, (count, width), 0)

    def body(b, total):
        owner, slot = b // slots, b % slots
        weighted = returned[owner, pl.ds(slot, 1), :]
        left = jnp.where(
            row == slot * (count // slots) + owner, jnp.broadcast_to(weighted, (count, width)), 0.0
        )
        return total + dot(left, interp[b], 0)

    out[...] = for_each(count, body, jnp.zeros((count, width), f32))


def place_kernel(count, kinds, rows, layers, per, *refs):
    tiles, out = refs[:-1], refs[-1]
    line = lax.broadcasted_iota(jnp.int32, (1, LANES), 1)
    south_end, north_end = at_ends()
    odd = lax.axis_index("lat") % 2
    packs = -(-len(kinds) * count // LANES)
    targets = [jnp.full((1, LANES), -1.0, f32) for _ in range(packs)]
    for i, (tile, (phase, lon_step, begin)) in enumerate(zip(tiles, kinds)):
        block = tile[begin : begin + 1, :LANES]
        block_row = jnp.floor((block + 0.5) / per)
        col = block - block_row * per
        layer = jnp.floor((block_row + 0.5) / rows)
        row = block_row - layer * rows
        valid = block >= 0.0
        if phase:
            is_north = jnp.where(odd == phase - 1, 1, 0)
            usable = jnp.where(is_north == 1, jnp.where(north_end, 0, 1), jnp.where(south_end, 0, 1))
            is_north = jnp.full((1, LANES), is_north, jnp.int32) == 1
            usable = jnp.full((1, LANES), usable, jnp.int32) == 1
            valid = valid & usable
            valid = valid & ((is_north & (row < HALO)) | (jnp.logical_not(is_north) & (row >= rows - HALO)))
            row = jnp.where(is_north, row + rows, row + 8)
        if lon_step:
            at_first, at_last = col == 0.0, col == per - 1.0
            both = at_first | at_last
            if lon_step == 1:
                both = at_first
            if lon_step == -1:
                both = at_last
            valid = valid & both
            col = jnp.where(at_first, float(per), float(per + 1))
        place = jnp.where(valid, (layer * (per + 2) + col) * (rows + 8) + row, -1.0)
        pack, shift = divmod(i * count, LANES)
        if shift:
            place = pltpu.roll(place, shift, 1)
        mine = (line >= shift) & (line < shift + count)
        targets[pack] = jnp.where(mine, place, targets[pack])
    places = out.shape[0]
    index = lax.broadcasted_iota(jnp.int32, (places, LANES), 0)
    for pack, target in enumerate(targets):
        chosen = jnp.where(index == target.astype(jnp.int32), 1.0, 0.0).astype(bf16)
        out[:, pack * LANES : (pack + 1) * LANES] = chosen
        out[:, (packs + pack) * LANES : (packs + pack + 1) * LANES] = chosen


def adjoint_kernel(n_source, *refs):
    chosen = refs[0]
    sources = refs[1 : 1 + n_source]
    spread, scale, wind_e, wind_n = refs[1 + n_source : 5 + n_source]
    filtered, = refs[5 + n_source :]
    layers, ext_rows, ext_cols = spread.shape
    rows, cols = filtered.shape[1:]
    values = [s[...] for s in sources]
    spare = chosen.shape[1] // 2 - sum(v.shape[0] for v in values)
    if spare:
        values.append(jnp.zeros((spare, LANES), f32))
    parts = jnp.concatenate(split(jnp.concatenate(values, axis=0)), axis=0)
    forcing = lax.dot_general(chosen[...], parts, NN, preferred_element_type=f32)
    mask = inside_mask((ext_rows, ext_cols))
    lane = lax.broadcasted_iota(jnp.int32, (ext_rows, LANES), 1)
    per = cols // LANES
    for l in range(layers):
        begin = l * (per + 2) * ext_rows
        tiles = [forcing[begin + c * ext_rows : begin + (c + 1) * ext_rows, :] for c in range(per + 2)]
        y = jnp.concatenate(tiles[:per] + [jnp.where(lane < LANES // 2, tiles[per], tiles[per + 1])], axis=1)
        u, v = 0.5 * wind_e[l], 0.5 * wind_n[l]
        for step in range(STEPS):
            if step:
                y = y * mask
            y = (
                (1.0 - 4.0 * diffusion) * y
                + east((diffusion + u) * y)
                + west((diffusion - u) * y)
                + north((diffusion + v) * y)
                + south((diffusion - v) * y)
            )
        s = smooth(scale[l] * y, spread[l])
        filtered[l] = s[:rows, :cols]


def gradient_kernel(n_other, *refs):
    back, control, filtered = refs[:3]
    others = refs[3 : 3 + n_other]
    gradient, partial = refs[3 + n_other :]
    layers, rows, cols = control.shape
    total = jnp.zeros((8, LANES), f32)
    for m in range(layers):
        g = control[m] + blend(back, filtered, others, m)
        gradient[m] = g
        square = g * g
        for r in range(0, rows, 8):
            for c in range(0, cols, LANES):
                total = total + square[r : r + 8, c : c + LANES]
    total = jnp.sum(total, axis=0, keepdims=True)
    partial[...] = jnp.broadcast_to(total[None], partial.shape)


def direction_kernel(cell_count, gradient, sums, previous, previous_square, direction):
    total = jnp.sum(jnp.sum(sums[...], axis=0), axis=1, keepdims=True)
    factor = total / cell_count / previous_square[:, 0:1]
    for l in range(gradient.shape[0]):
        direction[l] = factor * previous[l] - gradient[l]


def local(
    control,
    vertical,
    spread,
    error_scale,
    wind_lon,
    wind_lat,
    obs_block,
    obs_platform,
    obs_count,
    interp,
    innovation,
    error_inverse,
    previous_direction,
    previous_square,
):
    n_lat, n_lon, n_lev = (lax.axis_size(a) for a in ("lat", "lon", "lev"))
    layers, rows, cols = control.shape
    ext_rows, ext_cols = rows + 8, cols + LANES
    owners = obs_count.shape[-1]
    slots = obs_block.shape[-1]
    width = interp.shape[-1]
    count = owners * slots
    blocks = obs_block.reshape(owners, slots).T
    platforms = obs_platform.reshape(owners, slots).T
    counts = obs_count.reshape(1, owners)
    weights = interp.reshape(count, width, width)
    limit = (8 << 20) + 3 * weights.size * 4
    per = cols // LANES
    lat_fields = sum(WIDTHS) * layers
    lat_rows = lat_fields // 8 * 8 + 8

    def from_levs(field):
        return [
            lax.ppermute(field, "lev", [(i, (i + k) % n_lev) for i in range(n_lev)]) for k in range(1, n_lev)
        ]

    def partner(a, phase):
        step = 1 if (a % 2 == 0) == (phase == 1) else -1
        return (a + step) % n_lat

    def exchange(field, phase, lon_step):
        pairs = []
        for a in range(n_lat):
            for b in range(n_lon):
                to = partner(a, phase) if phase else a
                pairs.append((a * n_lon + b, to * n_lon + (b + lon_step) % n_lon))
        return lax.ppermute(field, ("lat", "lon"), pairs)

    lon_steps = (2,) if n_lon == 2 else (1, -1)

    def from_lon(field, phase, step):
        return exchange(field, phase, 1 if step == 2 else -step)

    others = from_levs(control)
    field = held(layers, rows, cols)
    mix = held(layers * layers * n_lev, LANES)
    innovations = innovation.reshape(count, width)
    (
        forth, back, square_v, control_v, spread_v, wind_e_v, wind_n_v, scale_v, previous_v, innovation_v,
        lon_part, first, last,
    ) = call(
        load_kernel,
        [mix, mix, held(1, LANES)] + [field] * 6 + [held(count, width)]
        + [held(rows + 8, LANES), held(lat_rows, cols), held(lat_rows, cols)],
        [HBM] * 10,
        [
            pltpu.SMEM(vertical.shape, f32),
            pltpu.SMEM(blocks.shape, jnp.int32),
            pltpu.SMEM((1,), f32),
            pltpu.SemaphoreType.DMA((10,)),
        ],
    )(
        vertical, blocks, previous_square, control, spread, wind_lon, wind_lat, error_scale, previous_direction,
        innovations,
    )
    blended, lon_out, lat_1, lat_2, diag_1, diag_2 = call(
        functools.partial(pack_kernel, len(others)),
        [field, held(rows + 8, LANES)] + [held(lat_rows, cols)] * 2 + [held(lat_rows, LANES)] * 2,
        [VMEM] * (5 + len(others)),
    )(forth, control_v, lon_part, first, last, *others)

    lane = jnp.arange(LANES, dtype=jnp.int32)
    lat_in = {phase: exchange(out, phase, 0) for phase, out in ((1, lat_1), (2, lat_2))}
    lon_raw = {step: from_lon(lon_out, 0, step) for step in lon_steps}
    diag_raw = {
        (phase, step): from_lon(out, phase, step)
        for phase, out in ((1, diag_1), (2, diag_2))
        for step in lon_steps
    }
    if n_lon == 2:
        lon_in = lon_raw[2]
        diag_in = {phase: diag_raw[phase, 2] for phase in (1, 2)}
    else:
        lon_in = jnp.where(lane % 8 < HALO, lon_raw[1], lon_raw[-1])
        diag_in = {
            phase: jnp.where(lane < LANES // 2, diag_raw[phase, 1], diag_raw[phase, -1]) for phase in (1, 2)
        }

    half = -(-slots // 4) * 4
    ext = held(layers, ext_rows, ext_cols)
    sent, ext_spread, ext_scale, ext_e, ext_n = call(
        forward_kernel,
        [shape(owners, 2 * half, width), ext, ext, ext, ext],
        [HBM] * 3 + [VMEM] * 12,
        [
            pltpu.VMEM((layers, ext_rows, ext_cols), f32),
            pltpu.VMEM((layers * ext_rows * per, LANES), f32),
            pltpu.SMEM(blocks.shape, jnp.int32),
            pltpu.SMEM(blocks.shape, jnp.int32),
            pltpu.SMEM(counts.shape, jnp.int32),
            pltpu.SemaphoreType.DMA((3,)),
        ],
        limit,
    )(
        blocks, platforms, counts, blended, spread_v, wind_e_v, wind_n_v, scale_v,
        lon_in, lat_in[1], lat_in[2], diag_in[1], diag_in[2], weights, innovation_v,
    )

    arrived = lax.all_to_all(sent, ("lat", "lon"), split_axis=0, concat_axis=0, tiled=True)
    matrices = error_inverse.reshape(error_inverse.shape[-3:])
    result = call(
        functools.partial(weigh_kernel, slots),
        shape(owners, 2 * half, width),
        [VMEM] * 2,
        [pltpu.VMEM((count, width), f32)] * 2,
    )(arrived, matrices)
    returned = lax.all_to_all(result, ("lat", "lon"), split_axis=0, concat_axis=0, tiled=True)
    adjoint_obs = call(
        functools.partial(transpose_kernel, slots), shape(count, width), [VMEM] * 2, (), limit
    )(returned, weights)

    sources, tiles, kinds = [adjoint_obs], [lon_out], [(0, 0, rows)]
    for step in lon_steps:
        sources.append(from_lon(adjoint_obs, 0, step))
        tiles.append(lon_raw[step])
        kinds.append((0, step, rows))
    for phase in (1, 2):
        sources.append(exchange(adjoint_obs, phase, 0))
        tiles.append(lat_in[phase])
        kinds.append((phase, 0, lat_fields))
        for step in lon_steps:
            sources.append(from_lon(adjoint_obs, phase, step))
            tiles.append(diag_raw[phase, step])
            kinds.append((phase, step, lat_fields))
    depth = -(-len(kinds) * count // LANES) * LANES
    chosen = call(
        functools.partial(place_kernel, count, kinds, rows, layers, per),
        held(layers * (per + 2) * ext_rows, 2 * depth, dtype=bf16),
        [VMEM] * len(tiles),
        (),
        limit,
    )(*tiles)
    filtered = call(
        functools.partial(adjoint_kernel, len(sources)),
        shape(layers, rows, cols),
        [VMEM] * (5 + len(sources)),
        (),
        limit,
    )(chosen, *sources, ext_spread, ext_scale, ext_e, ext_n)

    others = from_levs(filtered)
    group = n_lat * n_lon * n_lev
    gradient, partial = call(
        functools.partial(gradient_kernel, len(others)),
        [field, shape(group, 1, LANES)],
        [VMEM] * (3 + len(others)),
    )(back, control_v, filtered, *others)
    sums = lax.all_to_all(partial, ("lat", "lon", "lev"), split_axis=0, concat_axis=0, tiled=True)
    direction = call(
        functools.partial(direction_kernel, float(control.size * group)),
        shape(layers, rows, cols),
        [VMEM] * 4,
    )(gradient, sums, previous_v, square_v)
    return (gradient, direction)


def solution(mesh):
    field = P("lev", ("member", "lat"), "lon")
    shared = P("lev", "lat", "lon")
    placed = (
        field,
        P(),
        shared,
        shared,
        field,
        field,
        P("lev", "lat", "lon", None, None),
        P("lev", "lat", "lon", None, None),
        P("lev", "lat", "lon", None),
        P("lev", "lat", "lon", None, None, None, None),
        P("lev", ("member", "lat"), "lon", None, None, None),
        P("lat", "lon", None, None, None),
        field,
        P("member"),
    )
    return jax.shard_map(local, mesh=mesh, in_specs=placed, out_specs=(field, field), check_vma=False)
```

time: 84.7 us -> 73.3 us (0.87)
  blocking collectives: 0 us -> 18.7 us
  waiting for transfers between devices: 26.6 us -> 14.8 us
  starting transfers between devices: 29.3 us -> 20.4 us
  other arithmetic: 4.43 us -> 0 us
  local copies, waits for them, and re-layouts: 13.1 us -> 9.03 us
    all_to_all x0 -> x2, blocking collectives: none -> 18.7 us  [the longest x1 9.59 us: local(): lax.all_to_all(sent, ('lat', 'lon'), split_axis=0, concat_axis=0, tiled=T...]
    all_to_all x2 -> x0, waiting for transfers between devices: 11.9 us -> none  [the longest x1 6.59 us: local(): lax.all_to_all(result, ('lat', 'lon'), split_axis=0, concat_axis=0, tiled...]
    all_to_all x2 -> x0, starting transfers between devices: 6.68 us -> none  [the longest x1 3.34 us: local(): lax.all_to_all(sent, ('lat', 'lon'), split_axis=0, concat_axis=0, tiled=T...]
    unnamed x58 -> x29, local copies, waits for them, and re-layouts: 12.5 us -> 9.03 us
    convert_element_type x3 -> x0, other arithmetic: 2.09 us -> none  [the longest x1 0.73 us: local(): live = jnp.broadcast_to(live.reshape(count, 1), (count, width)).astype(f32)]
    all_to_all x1, starting transfers between devices: 5.45 us -> 3.47 us  [local(): lax.all_to_all(partial, ('lat', 'lon', 'lev'), split_axis=0, concat_axis=...]
    select_n x5 -> x0, other arithmetic: 1.41 us -> none  [add_source(): targets.append(jnp.where(valid, place, -1))]
    pallas_call x3 -> x5, Pallas kernels: 3.37 us -> 3.66 us  [the longest x1 2.27 us: local(): call(load_kernel, [mix, mix, held(1, LANES)] + [field] * 6 + [held(count,...]
  transfers between devices with their start and end apart: 15 -> 13, of which waited for: 6 -> 7; matrix products, arithmetic and copies ran while one was open for 7% -> 1% of each run, Pallas kernels for 0% -> 3%
where the time goes in v2:
time: 73.3 us; the launch traced here: 72.7 us
  starting transfers between devices  20.4 us (28%)
  blocking collectives  18.7 us (26%)
  waiting for transfers between devices  14.8 us (20%)
  local copies, waits for them, and re-layouts  9.03 us (12%)
  Pallas kernels  8.35 us (11%)
  between operations  1.43 us (2%)
    ppermute x10, starting transfers between devices, exchange(): return lax.ppermute(field, ('lat', 'lon'), pairs)  16.4 us
    all_to_all x1, blocking collectives, local(): lax.all_to_all(sent, ('lat', 'lon'), split_axis=0, concat_axis=0, tiled=T...  9.59 us
    all_to_all x1, blocking collectives, local(): lax.all_to_all(result, ('lat', 'lon'), split_axis=0, concat_axis=0, tiled...  9.15 us
    unnamed x29, local copies, waits for them, and re-layouts  9.03 us
    ppermute x10, waiting for transfers between devices, exchange(): return lax.ppermute(field, ('lat', 'lon'), pairs)  7.69 us
    all_to_all x1, waiting for transfers between devices, local(): lax.all_to_all(partial, ('lat', 'lon', 'lev'), split_axis=0, concat_axis=...  5.6 us
    all_to_all x1, starting transfers between devices, local(): lax.all_to_all(partial, ('lat', 'lon', 'lev'), split_axis=0, concat_axis=...  3.47 us
    pallas_call x1, Pallas kernels, local(): call(forward_kernel, [shape(owners, 2 * half, width), ext, ext, ext, ext]...  2.41 us
  transfers between devices with their start and end apart: 13, of which 7 were waited for; matrix products, arithmetic and copies ran while one was open for 1% of the time, Pallas kernels for 3%

profile of v2, /device:TPU:0, one launch (start us, length us, event | category | flops | bytes accessed | tf_op | source)
XLA Modules:
  0.0 72.7 jit_solution(1050760967818408521)
XLA Ops:
  1.8 0.9 %copy-done.2 = f32[2,56,512]{2,1,0:T(8,128)S(1)} copy-done((f32[2,56,512]{2,1,0:T(8,128)S(1)}, f32[2,56,512]{2,1,0:T(8,128)}, u32[]{:S(2)}) %copy-start.2) | copy-done | bytes 229400
  2.8 0.9 %copy-done.3 = f32[2,56,512]{2,1,0:T(8,128)S(1)} copy-done((f32[2,56,512]{2,1,0:T(8,128)S(1)}, f32[2,56,512]{2,1,0:T(8,128)}, u32[]{:S(2)}) %copy-start.3) | copy-done | bytes 229400
  3.7 0.9 %copy-done.4 = f32[2,56,512]{2,1,0:T(8,128)S(1)} copy-done((f32[2,56,512]{2,1,0:T(8,128)S(1)}, f32[2,56,512]{2,1,0:T(8,128)}, u32[]{:S(2)}) %copy-start.4) | copy-done | bytes 229400
  4.6 0.9 %copy-done.5 = f32[2,56,512]{2,1,0:T(8,128)S(1)} copy-done((f32[2,56,512]{2,1,0:T(8,128)S(1)}, f32[2,56,512]{2,1,0:T(8,128)}, u32[]{:S(2)}) %copy-start.5) | copy-done | bytes 229400
  5.6 0.9 %copy-done.6 = f32[2,56,512]{2,1,0:T(8,128)S(1)} copy-done((f32[2,56,512]{2,1,0:T(8,128)S(1)}, f32[2,56,512]{2,1,0:T(8,128)}, u32[]{:S(2)}) %copy-start.6) | copy-done | bytes 229400
  6.5 0.9 %copy-done.7 = f32[2,56,512]{2,1,0:T(8,128)S(1)} copy-done((f32[2,56,512]{2,1,0:T(8,128)S(1)}, f32[2,56,512]{2,1,0:T(8,128)}, u32[]{:S(2)}) %copy-start.7) | copy-done | bytes 229400
  9.5 2.3 %shard_map.149 = (f32[8,128]{1,0:T(8,128)S(1)}, f32[8,128]{1,0:T(8,128)S(1)}, f32[1,128]{1,0:T(1,128)S(1)}, f32[2,56,512]{2,1,0:T(8,128)S(1)}, f32[2,56,512]{2,1...) custom-call(f32[4,4]{1,0:T(4,128)S(1)} %copy-done.11, ...), custom_call_target="tpu_custom_call" | custom-call | flops 1048576 | bytes 1048576 | tf_op jit(solution)/shard_map/pallas_call | solution.py:502
  12.0 2.7 %collective-permute-start.2 = (f32[40,512]{1,0:T(8,128)S(1)}, f32[40,512]{1,0:T(8,128)S(1)}, u32[]{:S(2)}, u32[]{:S(2)}) collective-permute-start(f32[40,512]{1,0:T(8,128)S(1)} %get-tuple-element.35), channel_id=1, source_target_pairs={{0,4},{2,6},{4,0},{6,2},{8,12},{10,14},{12,8},{14,10},{1,5},{3,7},... | collective-permute-start | bytes 245768 | tf_op jit(solution)/shard_map/ppermute | solution.py:488
  14.7 2.5 %collective-permute-start.4 = (f32[40,512]{1,0:T(8,128)S(1)}, f32[40,512]{1,0:T(8,128)S(1)}, u32[]{:S(2)}, u32[]{:S(2)}) collective-permute-start(f32[40,512]{1,0:T(8,128)S(1)} %get-tuple-element.37), channel_id=1, source_target_pairs={{0,12},{2,14},{4,8},{6,10},{8,4},{10,6},{12,0},{14,2},{1,13},{3,15... | collective-permute-start | bytes 245768 | tf_op jit(solution)/shard_map/ppermute | solution.py:488
  17.1 1.5 %collective-permute-start.1 = (f32[64,128]{1,0:T(8,128)S(1)}, f32[64,128]{1,0:T(8,128)S(1)}, u32[]{:S(2)}, u32[]{:S(2)}) collective-permute-start(f32[64,128]{1,0:T(8,128)S(1)} %get-tuple-element.34.refs_0_), channel_id=1, source_target_pairs={{0,2},{2,0},{4,6},{6,4},{8,10},{10,8},{12,14},{14,12},{1,3},{3,1},... | collective-permute-start | bytes 98312 | tf_op jit(solution)/shard_map/ppermute | solution.py:488
  19.3 1.8 %collective-permute-start.5 = (f32[40,128]{1,0:T(8,128)S(1)}, f32[40,128]{1,0:T(8,128)S(1)}, u32[]{:S(2)}, u32[]{:S(2)}) collective-permute-start(f32[40,128]{1,0:T(8,128)S(1)} %get-tuple-element.38), channel_id=1, source_target_pairs={{0,14},{2,12},{4,10},{6,8},{8,6},{10,4},{12,2},{14,0},{1,15},{3,13... | collective-permute-start | bytes 61448 | tf_op jit(solution)/shard_map/ppermute | solution.py:488
  21.1 2.2 %collective-permute-done.3.refs_3_.diag_1 = f32[40,128]{1,0:T(8,128)S(1)} collective-permute-done((f32[40,128]{1,0:T(8,128)S(1)}, f32[40,128]{1,0:T(8,128)S(1)}, u32[]{:S(2)}, u32[]{:S(2)}) %collective-permute-start.3) | collective-permute-done | bytes 20512 | tf_op jit(solution)/shard_map/ppermute | solution.py:488
  23.3 2.4 %collective-permute-done.5.refs_5_.diag_2 = f32[40,128]{1,0:T(8,128)S(1)} collective-permute-done((f32[40,128]{1,0:T(8,128)S(1)}, f32[40,128]{1,0:T(8,128)S(1)}, u32[]{:S(2)}, u32[]{:S(2)}) %collective-permute-start.5) | collective-permute-done | bytes 20512 | tf_op jit(solution)/shard_map/ppermute | solution.py:488
  26.5 2.4 %shard_map.152 = (f32[8,8,128]{2,1,0:T(8,128)S(1)}, f32[2,64,640]{2,1,0:T(8,128)S(1)}, f32[2,64,640]{2,1,0:T(8,128)S(1)}, f32[2,64,640]{2,1,0:T(8,128)S(1)}, f32[2,64,640]{2,1,0:T(8,128)S(1)}) custom-call(s32[2,8]{1,0:T(2,128)S(1)} %bitcast.15, s32[2,8]{1,0:T(2,128)S(1)} %bitcast.16, s32[1,8]{1,0:T(1,128)S(1)} %bitcast.17, ...), custom_call_target="tpu_custom_call" | custom-call | flops 1048576 | bytes 1048576 | tf_op jit(solution)/shard_map/pallas_call | solution.py:542
  28.9 9.6 %all_to_all.15.arrived = f32[8,8,128]{2,1,0:T(8,128)S(1)} all-to-all(f32[8,8,128]{2,1,0:T(8,128)S(1)} %get-tuple-element.45), channel_id=1, replica_groups=mesh['member'=2,'lat'=4,'lon'=2,'lev'=2] {'lat','lon'}, dimensions={0} | all-to-all | bytes 65536 | tf_op jit(solution)/shard_map/all_to_all | solution.py:560
  38.7 9.2 %all_to_all.16.returned = f32[8,8,128]{2,1,0:T(8,128)S(1)} all-to-all(f32[8,8,128]{2,1,0:T(8,128)S(1)} %shard_map.153), channel_id=1, replica_groups=mesh['member'=2,'lat'=4,'lon'=2,'lev'=2] {'lat','lon'}, dimensions={0} | all-to-all | bytes 65536 | tf_op jit(solution)/shard_map/all_to_all | solution.py:568
  48.8 3.1 %collective-permute-start.9 = (f32[16,128]{1,0:T(8,128)S(1)}, f32[16,128]{1,0:T(8,128)S(1)}, u32[]{:S(2)}, u32[]{:S(2)}) collective-permute-start(f32[16,128]{1,0:T(8,128)S(1)} %shard_map.154.refs_1_), channel_id=1, source_target_pairs={{0,12},{2,14},{4,8},{6,10},{8,4},{10,6},{12,0},{14,2},{1,13},{3,15... | collective-permute-start | bytes 24584 | tf_op jit(solution)/shard_map/ppermute | solution.py:488
  51.9 3.1 %collective-permute-start.7 = (f32[16,128]{1,0:T(8,128)S(1)}, f32[16,128]{1,0:T(8,128)S(1)}, u32[]{:S(2)}, u32[]{:S(2)}) collective-permute-start(f32[16,128]{1,0:T(8,128)S(1)} %shard_map.154.refs_1_), channel_id=1, source_target_pairs={{0,4},{2,6},{4,0},{6,2},{8,12},{10,14},{12,8},{14,10},{1,5},{3,7},... | collective-permute-start | bytes 24584 | tf_op jit(solution)/shard_map/ppermute | solution.py:488
  56.7 1.9 %collective-permute-done.6.refs_2_ = f32[16,128]{1,0:T(8,128)S(1)} collective-permute-done((f32[16,128]{1,0:T(8,128)S(1)}, f32[16,128]{1,0:T(8,128)S(1)}, u32[]{:S(2)}, u32[]{:S(2)}) %collective-permute-start.6) | collective-permute-done | bytes 8224 | tf_op jit(solution)/shard_map/ppermute | solution.py:488
  58.6 1.2 %shard_map.155.refs_2_ = f32[2,56,512]{2,1,0:T(8,128)S(1)} custom-call(bf16[768,256]{1,0:T(8,128)(2,1)S(1)} %shard_map.151.refs_0_, f32[16,128]{1,0:T(8,128)S(1)} %shard_map.154.refs_1_, f32[16,128]{1,0:T(8,128)S(1)} %collective-permute-done.6.refs_2_, f32[16,128]{1,0:T(8,128)S(1)} %collective-permute-done.7.refs_3_, ...), custom_call_target="tpu_custom_call" | custom-call | flops 1048576 | bytes 1048576 | tf_op jit(solution)/shard_map/pallas_call | solution.py:594
  59.9 1.5 %collective-permute-done.11.refs_3_ = f32[2,56,512]{2,1,0:T(8,128)S(1)} collective-permute-done((f32[2,56,512]{2,1,0:T(8,128)S(1)}, f32[2,56,512]{2,1,0:T(8,128)S(1)}, u32[]{:S(2)}, u32[]{:S(2)}) %collective-permute-start.11) | collective-permute-done | bytes 229408 | tf_op jit(solution)/shard_map/ppermute | solution.py:475
  62.1 3.5 %all-to-all-start.2 = ((f32[16,1,128]{2,1,0:T(1,128)}), f32[16,1,128]{2,1,0:T(1,128)S(1)}, u32[]{:S(2)}, u32[]{:S(2)}) async-start(f32[16,1,128]{2,1,0:T(1,128)} %get-tuple-element.51), calls=%async_computation.2 | async-start | bytes 16384 | tf_op jit(solution)/shard_map/all_to_all | solution.py:609
  66.3 5.6 %all-to-all-done.2.sums = f32[16,1,128]{2,1,0:T(1,128)S(1)} async-done(((f32[16,1,128]{2,1,0:T(1,128)}), f32[16,1,128]{2,1,0:T(1,128)S(1)}, u32[]{:S(2)}, u32[]{:S(2)}) %all-to-all-start.2) | async-done | bytes 8224 | tf_op jit(solution)/shard_map/all_to_all | solution.py:609
  71.9 0.8 %shard_map.157 = f32[2,56,512]{2,1,0:T(8,128)} custom-call(f32[2,56,512]{2,1,0:T(8,128)S(1)} %get-tuple-element.54.gradient, f32[16,1,128]{2,1,0:T(1,128)S(1)} %all-to-all-done.2.sums, f32[2,56,512]{2,1,0:T(8,128)S(1)} %get-tuple-element.52.previous, f32[1,128]{1,0:T(1,128)S(1)} %get-tuple-element.53.previous_square), custom_call_target="tpu_custom_call" | custom-call | flops 1048576 | bytes 1048576 | tf_op jit(solution)/shard_map/pallas_call | solution.py:610
  (42 shorter events, 8.5 us)
Async XLA Ops:
  0.6 25.2 %copy-start = (f32[1,1,1,8,2,128,128]{6,5,4,3,2,1,0:T(8,128)S(1)}, f32[1,1,1,8,2,128,128]{6,5,4,3,2,1,0:T(8,128)}, u32[]{:S(2)}) copy-start(f32[1,1,1,8,2,128,128]{6,5,4,3,2,1,0:T(8,128)} %param.23) | copy-start | bytes 3145732
  0.6 11.1 %collective-permute-start = (f32[2,56,512]{2,1,0:T(8,128)}, f32[2,56,512]{2,1,0:T(8,128)S(1)}, u32[]{:S(2)}, u32[]{:S(2)}) collective-permute-start(f32[2,56,512]{2,1,0:T(8,128)} %control.1), channel_id=1, source_target_pairs={{0,1},{1,0},{2,3},{3,2},{4,5},{5,4},{6,7},{7,6},{8,9},{9,8},{10,11... | collective-permute-start | bytes 688136 | tf_op jit(solution)/shard_map/ppermute | solution.py:475
  1.8 0.9 %copy-start.2 = (f32[2,56,512]{2,1,0:T(8,128)S(1)}, f32[2,56,512]{2,1,0:T(8,128)}, u32[]{:S(2)}) copy-start(f32[2,56,512]{2,1,0:T(8,128)} %spread.1) | copy-start | bytes 688132
  2.8 0.9 %copy-start.3 = (f32[2,56,512]{2,1,0:T(8,128)S(1)}, f32[2,56,512]{2,1,0:T(8,128)}, u32[]{:S(2)}) copy-start(f32[2,56,512]{2,1,0:T(8,128)} %wind_e.1) | copy-start | bytes 688132
  3.7 0.9 %copy-start.4 = (f32[2,56,512]{2,1,0:T(8,128)S(1)}, f32[2,56,512]{2,1,0:T(8,128)}, u32[]{:S(2)}) copy-start(f32[2,56,512]{2,1,0:T(8,128)} %wind_n.1) | copy-start | bytes 688132
  4.6 0.9 %copy-start.5 = (f32[2,56,512]{2,1,0:T(8,128)S(1)}, f32[2,56,512]{2,1,0:T(8,128)}, u32[]{:S(2)}) copy-start(f32[2,56,512]{2,1,0:T(8,128)} %scale.1) | copy-start | bytes 688132
  5.6 0.9 %copy-start.6 = (f32[2,56,512]{2,1,0:T(8,128)S(1)}, f32[2,56,512]{2,1,0:T(8,128)}, u32[]{:S(2)}) copy-start(f32[2,56,512]{2,1,0:T(8,128)} %previous.1) | copy-start | bytes 688132
  6.5 0.9 %copy-start.7 = (f32[2,56,512]{2,1,0:T(8,128)S(1)}, f32[2,56,512]{2,1,0:T(8,128)}, u32[]{:S(2)}) copy-start(f32[2,56,512]{2,1,0:T(8,128)} %control.1) | copy-start | bytes 688132
  7.4 0.7 copy-start.8
  12.0 13.8 %collective-permute-start.2 = (f32[40,512]{1,0:T(8,128)S(1)}, f32[40,512]{1,0:T(8,128)S(1)}, u32[]{:S(2)}, u32[]{:S(2)}) collective-permute-start(f32[40,512]{1,0:T(8,128)S(1)} %get-tuple-element.35), channel_id=1, source_target_pairs={{0,4},{2,6},{4,0},{6,2},{8,12},{10,14},{12,8},{14,10},{1,5},{3,7},... | collective-permute-start | bytes 245768 | tf_op jit(solution)/shard_map/ppermute | solution.py:488
  14.7 11.1 %collective-permute-start.4 = (f32[40,512]{1,0:T(8,128)S(1)}, f32[40,512]{1,0:T(8,128)S(1)}, u32[]{:S(2)}, u32[]{:S(2)}) collective-permute-start(f32[40,512]{1,0:T(8,128)S(1)} %get-tuple-element.37), channel_id=1, source_target_pairs={{0,12},{2,14},{4,8},{6,10},{8,4},{10,6},{12,0},{14,2},{1,13},{3,15... | collective-permute-start | bytes 245768 | tf_op jit(solution)/shard_map/ppermute | solution.py:488
  17.1 8.7 %copy-start.12 = (s32[1,1,1,8,2]{3,4,2,1,0:T(2,128)S(1)}, s32[1,1,1,8,2]{3,4,2,1,0:T(2,128)}, u32[]{:S(2)}) copy-start(s32[1,1,1,8,2]{3,4,2,1,0:T(2,128)} %param.21) | copy-start | bytes 196
  17.1 8.6 %collective-permute-start.1 = (f32[64,128]{1,0:T(8,128)S(1)}, f32[64,128]{1,0:T(8,128)S(1)}, u32[]{:S(2)}, u32[]{:S(2)}) collective-permute-start(f32[64,128]{1,0:T(8,128)S(1)} %get-tuple-element.34.refs_0_), channel_id=1, source_target_pairs={{0,2},{2,0},{4,6},{6,4},{8,10},{10,8},{12,14},{14,12},{1,3},{3,1},... | collective-permute-start | bytes 98312 | tf_op jit(solution)/shard_map/ppermute | solution.py:488
  18.6 4.7 %collective-permute-start.3 = (f32[40,128]{1,0:T(8,128)S(1)}, f32[40,128]{1,0:T(8,128)S(1)}, u32[]{:S(2)}, u32[]{:S(2)}) collective-permute-start(f32[40,128]{1,0:T(8,128)S(1)} %get-tuple-element.36), channel_id=1, source_target_pairs={{0,6},{2,4},{4,2},{6,0},{8,14},{10,12},{12,10},{14,8},{1,7},{3,5},... | collective-permute-start | bytes 61448 | tf_op jit(solution)/shard_map/ppermute | solution.py:488
  19.3 6.5 %collective-permute-start.5 = (f32[40,128]{1,0:T(8,128)S(1)}, f32[40,128]{1,0:T(8,128)S(1)}, u32[]{:S(2)}, u32[]{:S(2)}) collective-permute-start(f32[40,128]{1,0:T(8,128)S(1)} %get-tuple-element.38), channel_id=1, source_target_pairs={{0,14},{2,12},{4,10},{6,8},{8,6},{10,4},{12,2},{14,0},{1,15},{3,13... | collective-permute-start | bytes 61448 | tf_op jit(solution)/shard_map/ppermute | solution.py:488
  25.8 0.7 copy-start.10
  26.5 12.0 %copy-start.1 = (f32[1,1,8,128,128]{4,3,2,1,0:T(8,128)S(1)}, f32[1,1,8,128,128]{4,3,2,1,0:T(8,128)}, u32[]{:S(2)}) copy-start(f32[1,1,8,128,128]{4,3,2,1,0:T(8,128)} %param.25) | copy-start | bytes 1572868
  48.2 7.4 %collective-permute-start.10 = (f32[16,128]{1,0:T(8,128)S(1)}, f32[16,128]{1,0:T(8,128)S(1)}, u32[]{:S(2)}, u32[]{:S(2)}) collective-permute-start(f32[16,128]{1,0:T(8,128)S(1)} %shard_map.154.refs_1_), channel_id=1, source_target_pairs={{0,14},{2,12},{4,10},{6,8},{8,6},{10,4},{12,2},{14,0},{1,15},{3,13... | collective-permute-start | bytes 24584 | tf_op jit(solution)/shard_map/ppermute | solution.py:488
  48.8 6.8 %collective-permute-start.9 = (f32[16,128]{1,0:T(8,128)S(1)}, f32[16,128]{1,0:T(8,128)S(1)}, u32[]{:S(2)}, u32[]{:S(2)}) collective-permute-start(f32[16,128]{1,0:T(8,128)S(1)} %shard_map.154.refs_1_), channel_id=1, source_target_pairs={{0,12},{2,14},{4,8},{6,10},{8,4},{10,6},{12,0},{14,2},{1,13},{3,15... | collective-permute-start | bytes 24584 | tf_op jit(solution)/shard_map/ppermute | solution.py:488
  51.9 4.5 %collective-permute-start.8 = (f32[16,128]{1,0:T(8,128)S(1)}, f32[16,128]{1,0:T(8,128)S(1)}, u32[]{:S(2)}, u32[]{:S(2)}) collective-permute-start(f32[16,128]{1,0:T(8,128)S(1)} %shard_map.154.refs_1_), channel_id=1, source_target_pairs={{0,6},{2,4},{4,2},{6,0},{8,14},{10,12},{12,10},{14,8},{1,7},{3,5},... | collective-permute-start | bytes 24584 | tf_op jit(solution)/shard_map/ppermute | solution.py:488
  51.9 4.8 %collective-permute-start.7 = (f32[16,128]{1,0:T(8,128)S(1)}, f32[16,128]{1,0:T(8,128)S(1)}, u32[]{:S(2)}, u32[]{:S(2)}) collective-permute-start(f32[16,128]{1,0:T(8,128)S(1)} %shard_map.154.refs_1_), channel_id=1, source_target_pairs={{0,4},{2,6},{4,0},{6,2},{8,12},{10,14},{12,8},{14,10},{1,5},{3,7},... | collective-permute-start | bytes 24584 | tf_op jit(solution)/shard_map/ppermute | solution.py:488
  55.0 3.7 %collective-permute-start.6 = (f32[16,128]{1,0:T(8,128)S(1)}, f32[16,128]{1,0:T(8,128)S(1)}, u32[]{:S(2)}, u32[]{:S(2)}) collective-permute-start(f32[16,128]{1,0:T(8,128)S(1)} %shard_map.154.refs_1_), channel_id=1, source_target_pairs={{0,2},{2,0},{4,6},{6,4},{8,10},{10,8},{12,14},{14,12},{1,3},{3,1},... | collective-permute-start | bytes 24584 | tf_op jit(solution)/shard_map/ppermute | solution.py:488
  59.8 1.6 %collective-permute-start.11 = (f32[2,56,512]{2,1,0:T(8,128)S(1)}, f32[2,56,512]{2,1,0:T(8,128)S(1)}, u32[]{:S(2)}, u32[]{:S(2)}) collective-permute-start(f32[2,56,512]{2,1,0:T(8,128)S(1)} %shard_map.155.refs_2_), channel_id=1, source_target_pairs={{0,1},{1,0},{2,3},{3,2},{4,5},{5,4},{6,7},{7,6},{8,9},{9,8},{10,11... | collective-permute-start | bytes 688136 | tf_op jit(solution)/shard_map/ppermute | solution.py:475
  62.1 9.8 %all-to-all-start.2 = ((f32[16,1,128]{2,1,0:T(1,128)}), f32[16,1,128]{2,1,0:T(1,128)S(1)}, u32[]{:S(2)}, u32[]{:S(2)}) async-start(f32[16,1,128]{2,1,0:T(1,128)} %get-tuple-element.51), calls=%async_computation.2 | async-start | bytes 16384 | tf_op jit(solution)/shard_map/all_to_all | solution.py:609
  (3 other events, 2.0 us)

commit v3 on v2

--- a/solution.py
+++ b/solution.py
@@ -109,13 +109,15 @@
 
 def load_kernel(
     vertical, blocks, previous_square, control, spread, wind_e, wind_n, scale, previous, innovation,
+    platforms, counts,
     forth, back, square_v, control_v, spread_v, wind_e_v, wind_n_v, scale_v, previous_v, innovation_v,
-    lon_out, first, last, vertical_s, blocks_s, square_s, sems,
+    blocks_v, platforms_v, counts_v, lon_out, first, last, vertical_s, blocks_s, square_s, sems,
 ):
     pairs = (
         (spread, spread_v), (wind_e, wind_e_v), (wind_n, wind_n_v), (scale, scale_v), (blocks, blocks_s),
         (vertical, vertical_s), (previous_square, square_s), (control, control_v),
-        (innovation, innovation_v), (previous, previous_v),
+        (innovation, innovation_v), (previous, previous_v), (blocks, blocks_v), (platforms, platforms_v),
+        (counts, counts_v),
     )
     copies = [pltpu.make_async_copy(a, b, sems.at[i]) for i, (a, b) in enumerate(pairs)]
     for copy in copies:
@@ -498,21 +500,23 @@
     innovations = innovation.reshape(count, width)
     (
         forth, back, square_v, control_v, spread_v, wind_e_v, wind_n_v, scale_v, previous_v, innovation_v,
-        lon_part, first, last,
+        blocks_v, platforms_v, counts_v, lon_part, first, last,
     ) = call(
         load_kernel,
         [mix, mix, held(1, LANES)] + [field] * 6 + [held(count, width)]
+        + [held(*x.shape, dtype=jnp.int32) for x in (blocks, platforms, counts)]
         + [held(rows + 8, LANES), held(lat_rows, cols), held(lat_rows, cols)],
-        [HBM] * 10,
+        [HBM] * 12,
         [
             pltpu.SMEM(vertical.shape, f32),
             pltpu.SMEM(blocks.shape, jnp.int32),
             pltpu.SMEM((1,), f32),
-            pltpu.SemaphoreType.DMA((10,)),
+            pltpu.SemaphoreType.DMA((13,)),
         ],
+        58 << 20,
     )(
         vertical, blocks, previous_square, control, spread, wind_lon, wind_lat, error_scale, previous_direction,
-        innovations,
+        innovations, platforms, counts,
     )
     blended, lon_out, lat_1, lat_2, diag_1, diag_2 = call(
         functools.partial(pack_kernel, len(others)),
@@ -542,7 +546,7 @@
     sent, ext_spread, ext_scale, ext_e, ext_n = call(
         forward_kernel,
         [shape(owners, 2 * half, width), ext, ext, ext, ext],
-        [HBM] * 3 + [VMEM] * 12,
+        [VMEM] * 15,
         [
             pltpu.VMEM((layers, ext_rows, ext_cols), f32),
             pltpu.VMEM((layers * ext_rows * per, LANES), f32),
@@ -553,7 +557,7 @@
         ],
         limit,
     )(
-        blocks, platforms, counts, blended, spread_v, wind_e_v, wind_n_v, scale_v,
+        blocks_v, platforms_v, counts_v, blended, spread_v, wind_e_v, wind_n_v, scale_v,
         lon_in, lat_in[1], lat_in[2], diag_in[1], diag_in[2], weights, innovation_v,
     )
 

time: 73.3 us -> 64 us (0.87)
  local copies, waits for them, and re-layouts: 9.03 us -> 0.7 us
    unnamed x29 -> x5, local copies, waits for them, and re-layouts: 9.03 us -> 0.7 us
where the time goes in v3:
time: 64 us; the launch traced here: 63.7 us
  starting transfers between devices  20.4 us (32%)
  blocking collectives  18.7 us (29%)
  waiting for transfers between devices  14.8 us (23%)
  Pallas kernels  7.68 us (12%)
  between operations  1.4 us (2%)
  local copies, waits for them, and re-layouts  0.7 us (1%)
    ppermute x10, starting transfers between devices, exchange(): return lax.ppermute(field, ('lat', 'lon'), pairs)  16.4 us
    all_to_all x1, blocking collectives, local(): lax.all_to_all(sent, ('lat', 'lon'), split_axis=0, concat_axis=0, tiled=T...  9.59 us
    all_to_all x1, blocking collectives, local(): lax.all_to_all(result, ('lat', 'lon'), split_axis=0, concat_axis=0, tiled...  9.15 us
    ppermute x10, waiting for transfers between devices, exchange(): return lax.ppermute(field, ('lat', 'lon'), pairs)  7.69 us
    all_to_all x1, waiting for transfers between devices, local(): lax.all_to_all(partial, ('lat', 'lon', 'lev'), split_axis=0, concat_axis=...  5.6 us
    all_to_all x1, starting transfers between devices, local(): lax.all_to_all(partial, ('lat', 'lon', 'lev'), split_axis=0, concat_axis=...  3.47 us
    pallas_call x1, Pallas kernels, local(): call(forward_kernel, [shape(owners, 2 * half, width), ext, ext, ext, ext]...  2.4 us
    pallas_call x1, Pallas kernels, local(): call(load_kernel, [mix, mix, held(1, LANES)] + [field] * 6 + [held(count,...  1.61 us
  transfers between devices with their start and end apart: 13, of which 7 were waited for; matrix products, arithmetic and copies ran while one was open for 1% of the time, Pallas kernels for 3%

profile of v3, /device:TPU:0, one launch (start us, length us, event | category | flops | bytes accessed | tf_op | source)
XLA Modules:
  0.0 63.7 jit_solution(13278950732701557678)
XLA Ops:
  0.6 0.5 collective-permute-start
  1.8 1.6 %shard_map.149 = (f32[8,128]{1,0:T(8,128)S(1)}, f32[8,128]{1,0:T(8,128)S(1)}, f32[1,128]{1,0:T(1,128)S(1)}, f32[2,56,512]{2,1,0:T(8,128)S(1)}, f32[2,56,512]{2,1...) custom-call(f32[4,4]{1,0:T(4,128)} %vertical.1, ...), custom_call_target="tpu_custom_call" | custom-call | flops 1048576 | bytes 1048576 | tf_op jit(solution)/shard_map/pallas_call | solution.py:504
  3.6 2.7 %collective-permute-start.2 = (f32[40,512]{1,0:T(8,128)S(1)}, f32[40,512]{1,0:T(8,128)S(1)}, u32[]{:S(2)}, u32[]{:S(2)}) collective-permute-start(f32[40,512]{1,0:T(8,128)S(1)} %get-tuple-element.38), channel_id=1, source_target_pairs={{0,4},{2,6},{4,0},{6,2},{8,12},{10,14},{12,8},{14,10},{1,5},{3,7},... | collective-permute-start | bytes 245768 | tf_op jit(solution)/shard_map/ppermute | solution.py:490
  6.3 2.5 %collective-permute-start.4 = (f32[40,512]{1,0:T(8,128)S(1)}, f32[40,512]{1,0:T(8,128)S(1)}, u32[]{:S(2)}, u32[]{:S(2)}) collective-permute-start(f32[40,512]{1,0:T(8,128)S(1)} %get-tuple-element.40), channel_id=1, source_target_pairs={{0,12},{2,14},{4,8},{6,10},{8,4},{10,6},{12,0},{14,2},{1,13},{3,15... | collective-permute-start | bytes 245768 | tf_op jit(solution)/shard_map/ppermute | solution.py:490
  8.8 1.5 %collective-permute-start.1 = (f32[64,128]{1,0:T(8,128)S(1)}, f32[64,128]{1,0:T(8,128)S(1)}, u32[]{:S(2)}, u32[]{:S(2)}) collective-permute-start(f32[64,128]{1,0:T(8,128)S(1)} %get-tuple-element.37.refs_0_), channel_id=1, source_target_pairs={{0,2},{2,0},{4,6},{6,4},{8,10},{10,8},{12,14},{14,12},{1,3},{3,1},... | collective-permute-start | bytes 98312 | tf_op jit(solution)/shard_map/ppermute | solution.py:490
  10.3 0.6 %collective-permute-start.3 = (f32[40,128]{1,0:T(8,128)S(1)}, f32[40,128]{1,0:T(8,128)S(1)}, u32[]{:S(2)}, u32[]{:S(2)}) collective-permute-start(f32[40,128]{1,0:T(8,128)S(1)} %get-tuple-element.39), channel_id=1, source_target_pairs={{0,6},{2,4},{4,2},{6,0},{8,14},{10,12},{12,10},{14,8},{1,7},{3,5},... | collective-permute-start | bytes 61448 | tf_op jit(solution)/shard_map/ppermute | solution.py:490
  10.9 1.8 %collective-permute-start.5 = (f32[40,128]{1,0:T(8,128)S(1)}, f32[40,128]{1,0:T(8,128)S(1)}, u32[]{:S(2)}, u32[]{:S(2)}) collective-permute-start(f32[40,128]{1,0:T(8,128)S(1)} %get-tuple-element.41), channel_id=1, source_target_pairs={{0,14},{2,12},{4,10},{6,8},{8,6},{10,4},{12,2},{14,0},{1,15},{3,13... | collective-permute-start | bytes 61448 | tf_op jit(solution)/shard_map/ppermute | solution.py:490
  12.8 2.2 %collective-permute-done.3.refs_3_.diag_1 = f32[40,128]{1,0:T(8,128)S(1)} collective-permute-done((f32[40,128]{1,0:T(8,128)S(1)}, f32[40,128]{1,0:T(8,128)S(1)}, u32[]{:S(2)}, u32[]{:S(2)}) %collective-permute-start.3) | collective-permute-done | bytes 20512 | tf_op jit(solution)/shard_map/ppermute | solution.py:490
  15.0 2.4 %collective-permute-done.5.refs_5_.diag_2 = f32[40,128]{1,0:T(8,128)S(1)} collective-permute-done((f32[40,128]{1,0:T(8,128)S(1)}, f32[40,128]{1,0:T(8,128)S(1)}, u32[]{:S(2)}, u32[]{:S(2)}) %collective-permute-start.5) | collective-permute-done | bytes 20512 | tf_op jit(solution)/shard_map/ppermute | solution.py:490
  17.4 2.4 %shard_map.152 = (f32[8,8,128]{2,1,0:T(8,128)S(1)}, f32[2,64,640]{2,1,0:T(8,128)S(1)}, f32[2,64,640]{2,1,0:T(8,128)S(1)}, f32[2,64,640]{2,1,0:T(8,128)S(1)}, f32[2,64,640]{2,1,0:T(8,128)S(1)}) custom-call(s32[2,8]{1,0:T(2,128)S(1)} %get-tuple-element.42.blocks, s32[2,8]{1,0:T(2,128)S(1)} %get-tuple-element.43.platforms, ...), custom_call_target="tpu_custom_call" | custom-call | flops 1048576 | bytes 1048576 | tf_op jit(solution)/shard_map/pallas_call | solution.py:546
  19.8 9.6 %all_to_all.15.arrived = f32[8,8,128]{2,1,0:T(8,128)S(1)} all-to-all(f32[8,8,128]{2,1,0:T(8,128)S(1)} %get-tuple-element.51), channel_id=1, replica_groups=mesh['member'=2,'lat'=4,'lon'=2,'lev'=2] {'lat','lon'}, dimensions={0} | all-to-all | bytes 65536 | tf_op jit(solution)/shard_map/all_to_all | solution.py:564
  29.7 9.2 %all_to_all.16.returned = f32[8,8,128]{2,1,0:T(8,128)S(1)} all-to-all(f32[8,8,128]{2,1,0:T(8,128)S(1)} %shard_map.153), channel_id=1, replica_groups=mesh['member'=2,'lat'=4,'lon'=2,'lev'=2] {'lat','lon'}, dimensions={0} | all-to-all | bytes 65536 | tf_op jit(solution)/shard_map/all_to_all | solution.py:572
  39.1 0.7 %collective-permute-start.10 = (f32[16,128]{1,0:T(8,128)S(1)}, f32[16,128]{1,0:T(8,128)S(1)}, u32[]{:S(2)}, u32[]{:S(2)}) collective-permute-start(f32[16,128]{1,0:T(8,128)S(1)} %shard_map.154.refs_1_), channel_id=1, source_target_pairs={{0,14},{2,12},{4,10},{6,8},{8,6},{10,4},{12,2},{14,0},{1,15},{3,13... | collective-permute-start | bytes 24584 | tf_op jit(solution)/shard_map/ppermute | solution.py:490
  39.8 3.1 %collective-permute-start.9 = (f32[16,128]{1,0:T(8,128)S(1)}, f32[16,128]{1,0:T(8,128)S(1)}, u32[]{:S(2)}, u32[]{:S(2)}) collective-permute-start(f32[16,128]{1,0:T(8,128)S(1)} %shard_map.154.refs_1_), channel_id=1, source_target_pairs={{0,12},{2,14},{4,8},{6,10},{8,4},{10,6},{12,0},{14,2},{1,13},{3,15... | collective-permute-start | bytes 24584 | tf_op jit(solution)/shard_map/ppermute | solution.py:490
  42.9 3.1 %collective-permute-start.7 = (f32[16,128]{1,0:T(8,128)S(1)}, f32[16,128]{1,0:T(8,128)S(1)}, u32[]{:S(2)}, u32[]{:S(2)}) collective-permute-start(f32[16,128]{1,0:T(8,128)S(1)} %shard_map.154.refs_1_), channel_id=1, source_target_pairs={{0,4},{2,6},{4,0},{6,2},{8,12},{10,14},{12,8},{14,10},{1,5},{3,7},... | collective-permute-start | bytes 24584 | tf_op jit(solution)/shard_map/ppermute | solution.py:490
  46.6 0.8 %collective-permute-done.8.refs_4_ = f32[16,128]{1,0:T(8,128)S(1)} collective-permute-done((f32[16,128]{1,0:T(8,128)S(1)}, f32[16,128]{1,0:T(8,128)S(1)}, u32[]{:S(2)}, u32[]{:S(2)}) %collective-permute-start.8) | collective-permute-done | bytes 8224 | tf_op jit(solution)/shard_map/ppermute | solution.py:490
  47.7 1.9 %collective-permute-done.6.refs_2_ = f32[16,128]{1,0:T(8,128)S(1)} collective-permute-done((f32[16,128]{1,0:T(8,128)S(1)}, f32[16,128]{1,0:T(8,128)S(1)}, u32[]{:S(2)}, u32[]{:S(2)}) %collective-permute-start.6) | collective-permute-done | bytes 8224 | tf_op jit(solution)/shard_map/ppermute | solution.py:490
  49.6 1.2 %shard_map.155.refs_2_ = f32[2,56,512]{2,1,0:T(8,128)S(1)} custom-call(bf16[768,256]{1,0:T(8,128)(2,1)S(1)} %shard_map.151.refs_0_, f32[16,128]{1,0:T(8,128)S(1)} %shard_map.154.refs_1_, f32[16,128]{1,0:T(8,128)S(1)} %collective-permute-done.6.refs_2_, f32[16,128]{1,0:T(8,128)S(1)} %collective-permute-done.7.refs_3_, ...), custom_call_target="tpu_custom_call" | custom-call | flops 1048576 | bytes 1048576 | tf_op jit(solution)/shard_map/pallas_call | solution.py:598
  50.9 1.5 %collective-permute-done.11.refs_3_ = f32[2,56,512]{2,1,0:T(8,128)S(1)} collective-permute-done((f32[2,56,512]{2,1,0:T(8,128)S(1)}, f32[2,56,512]{2,1,0:T(8,128)S(1)}, u32[]{:S(2)}, u32[]{:S(2)}) %collective-permute-start.11) | collective-permute-done | bytes 229408 | tf_op jit(solution)/shard_map/ppermute | solution.py:477
  52.4 0.8 %shard_map.156 = (f32[2,56,512]{2,1,0:T(8,128)S(1)}, f32[16,1,128]{2,1,0:T(1,128)}) custom-call(f32[8,128]{1,0:T(8,128)S(1)} %get-tuple-element.31.refs_0_, f32[2,56,512]{2,1,0:T(8,128)S(1)} %get-tuple-element.32.refs_1_, f32[2,56,512]{2,1,0:T(8,128)S(1)} %shard_map.155.refs_2_, f32[2,56,512]{2,1,0:T(8,128)S(1)} %collective-permute-done.11.refs_3_), custom_call_target="tpu_custom_call" | custom-call | flops 1048576 | bytes 1048576 | tf_op jit(solution)/shard_map/pallas_call | solution.py:608
  53.1 3.5 %all-to-all-start.2 = ((f32[16,1,128]{2,1,0:T(1,128)}), f32[16,1,128]{2,1,0:T(1,128)S(1)}, u32[]{:S(2)}, u32[]{:S(2)}) async-start(f32[16,1,128]{2,1,0:T(1,128)} %get-tuple-element.57), calls=%async_computation.2 | async-start | bytes 16384 | tf_op jit(solution)/shard_map/all_to_all | solution.py:613
  56.6 0.7 %copy.16 = f32[2,56,512]{2,1,0:T(8,128)} copy(f32[2,56,512]{2,1,0:T(8,128)S(1)} %get-tuple-element.60.gradient) | data formatting | bytes 458752
  57.3 5.6 %all-to-all-done.2.sums = f32[16,1,128]{2,1,0:T(1,128)S(1)} async-done(((f32[16,1,128]{2,1,0:T(1,128)}), f32[16,1,128]{2,1,0:T(1,128)S(1)}, u32[]{:S(2)}, u32[]{:S(2)}) %all-to-all-start.2) | async-done | bytes 8224 | tf_op jit(solution)/shard_map/all_to_all | solution.py:613
  62.9 0.8 %shard_map.157 = f32[2,56,512]{2,1,0:T(8,128)} custom-call(f32[2,56,512]{2,1,0:T(8,128)S(1)} %get-tuple-element.60.gradient, f32[16,1,128]{2,1,0:T(1,128)S(1)} %all-to-all-done.2.sums, f32[2,56,512]{2,1,0:T(8,128)S(1)} %get-tuple-element.58.previous, f32[1,128]{1,0:T(1,128)S(1)} %get-tuple-element.59.previous_square), custom_call_target="tpu_custom_call" | custom-call | flops 1048576 | bytes 1048576 | tf_op jit(solution)/shard_map/pallas_call | solution.py:614
  (18 shorter events, 1.7 us)
Async XLA Ops:
  0.6 16.8 %copy-start = (f32[1,1,1,8,2,128,128]{6,5,4,3,2,1,0:T(8,128)S(1)}, f32[1,1,1,8,2,128,128]{6,5,4,3,2,1,0:T(8,128)}, u32[]{:S(2)}) copy-start(f32[1,1,1,8,2,128,128]{6,5,4,3,2,1,0:T(8,128)} %param.23) | copy-start | bytes 3145732
  0.6 2.8 %collective-permute-start = (f32[2,56,512]{2,1,0:T(8,128)}, f32[2,56,512]{2,1,0:T(8,128)S(1)}, u32[]{:S(2)}, u32[]{:S(2)}) collective-permute-start(f32[2,56,512]{2,1,0:T(8,128)} %control.1), channel_id=1, source_target_pairs={{0,1},{1,0},{2,3},{3,2},{4,5},{5,4},{6,7},{7,6},{8,9},{9,8},{10,11... | collective-permute-start | bytes 688136 | tf_op jit(solution)/shard_map/ppermute | solution.py:477
  3.6 13.8 %collective-permute-start.2 = (f32[40,512]{1,0:T(8,128)S(1)}, f32[40,512]{1,0:T(8,128)S(1)}, u32[]{:S(2)}, u32[]{:S(2)}) collective-permute-start(f32[40,512]{1,0:T(8,128)S(1)} %get-tuple-element.38), channel_id=1, source_target_pairs={{0,4},{2,6},{4,0},{6,2},{8,12},{10,14},{12,8},{14,10},{1,5},{3,7},... | collective-permute-start | bytes 245768 | tf_op jit(solution)/shard_map/ppermute | solution.py:490
  6.3 11.1 %collective-permute-start.4 = (f32[40,512]{1,0:T(8,128)S(1)}, f32[40,512]{1,0:T(8,128)S(1)}, u32[]{:S(2)}, u32[]{:S(2)}) collective-permute-start(f32[40,512]{1,0:T(8,128)S(1)} %get-tuple-element.40), channel_id=1, source_target_pairs={{0,12},{2,14},{4,8},{6,10},{8,4},{10,6},{12,0},{14,2},{1,13},{3,15... | collective-permute-start | bytes 245768 | tf_op jit(solution)/shard_map/ppermute | solution.py:490
  8.8 8.6 %collective-permute-start.1 = (f32[64,128]{1,0:T(8,128)S(1)}, f32[64,128]{1,0:T(8,128)S(1)}, u32[]{:S(2)}, u32[]{:S(2)}) collective-permute-start(f32[64,128]{1,0:T(8,128)S(1)} %get-tuple-element.37.refs_0_), channel_id=1, source_target_pairs={{0,2},{2,0},{4,6},{6,4},{8,10},{10,8},{12,14},{14,12},{1,3},{3,1},... | collective-permute-start | bytes 98312 | tf_op jit(solution)/shard_map/ppermute | solution.py:490
  10.3 4.7 %collective-permute-start.3 = (f32[40,128]{1,0:T(8,128)S(1)}, f32[40,128]{1,0:T(8,128)S(1)}, u32[]{:S(2)}, u32[]{:S(2)}) collective-permute-start(f32[40,128]{1,0:T(8,128)S(1)} %get-tuple-element.39), channel_id=1, source_target_pairs={{0,6},{2,4},{4,2},{6,0},{8,14},{10,12},{12,10},{14,8},{1,7},{3,5},... | collective-permute-start | bytes 61448 | tf_op jit(solution)/shard_map/ppermute | solution.py:490
  10.9 6.5 %collective-permute-start.5 = (f32[40,128]{1,0:T(8,128)S(1)}, f32[40,128]{1,0:T(8,128)S(1)}, u32[]{:S(2)}, u32[]{:S(2)}) collective-permute-start(f32[40,128]{1,0:T(8,128)S(1)} %get-tuple-element.41), channel_id=1, source_target_pairs={{0,14},{2,12},{4,10},{6,8},{8,6},{10,4},{12,2},{14,0},{1,15},{3,13... | collective-permute-start | bytes 61448 | tf_op jit(solution)/shard_map/ppermute | solution.py:490
  17.4 12.0 %copy-start.1 = (f32[1,1,8,128,128]{4,3,2,1,0:T(8,128)S(1)}, f32[1,1,8,128,128]{4,3,2,1,0:T(8,128)}, u32[]{:S(2)}) copy-start(f32[1,1,8,128,128]{4,3,2,1,0:T(8,128)} %param.25) | copy-start | bytes 1572868
  39.1 7.4 %collective-permute-start.10 = (f32[16,128]{1,0:T(8,128)S(1)}, f32[16,128]{1,0:T(8,128)S(1)}, u32[]{:S(2)}, u32[]{:S(2)}) collective-permute-start(f32[16,128]{1,0:T(8,128)S(1)} %shard_map.154.refs_1_), channel_id=1, source_target_pairs={{0,14},{2,12},{4,10},{6,8},{8,6},{10,4},{12,2},{14,0},{1,15},{3,13... | collective-permute-start | bytes 24584 | tf_op jit(solution)/shard_map/ppermute | solution.py:490
  39.8 6.8 %collective-permute-start.9 = (f32[16,128]{1,0:T(8,128)S(1)}, f32[16,128]{1,0:T(8,128)S(1)}, u32[]{:S(2)}, u32[]{:S(2)}) collective-permute-start(f32[16,128]{1,0:T(8,128)S(1)} %shard_map.154.refs_1_), channel_id=1, source_target_pairs={{0,12},{2,14},{4,8},{6,10},{8,4},{10,6},{12,0},{14,2},{1,13},{3,15... | collective-permute-start | bytes 24584 | tf_op jit(solution)/shard_map/ppermute | solution.py:490
  42.9 4.5 %collective-permute-start.8 = (f32[16,128]{1,0:T(8,128)S(1)}, f32[16,128]{1,0:T(8,128)S(1)}, u32[]{:S(2)}, u32[]{:S(2)}) collective-permute-start(f32[16,128]{1,0:T(8,128)S(1)} %shard_map.154.refs_1_), channel_id=1, source_target_pairs={{0,6},{2,4},{4,2},{6,0},{8,14},{10,12},{12,10},{14,8},{1,7},{3,5},... | collective-permute-start | bytes 24584 | tf_op jit(solution)/shard_map/ppermute | solution.py:490
  42.9 4.8 %collective-permute-start.7 = (f32[16,128]{1,0:T(8,128)S(1)}, f32[16,128]{1,0:T(8,128)S(1)}, u32[]{:S(2)}, u32[]{:S(2)}) collective-permute-start(f32[16,128]{1,0:T(8,128)S(1)} %shard_map.154.refs_1_), channel_id=1, source_target_pairs={{0,4},{2,6},{4,0},{6,2},{8,12},{10,14},{12,8},{14,10},{1,5},{3,7},... | collective-permute-start | bytes 24584 | tf_op jit(solution)/shard_map/ppermute | solution.py:490
  46.0 3.7 %collective-permute-start.6 = (f32[16,128]{1,0:T(8,128)S(1)}, f32[16,128]{1,0:T(8,128)S(1)}, u32[]{:S(2)}, u32[]{:S(2)}) collective-permute-start(f32[16,128]{1,0:T(8,128)S(1)} %shard_map.154.refs_1_), channel_id=1, source_target_pairs={{0,2},{2,0},{4,6},{6,4},{8,10},{10,8},{12,14},{14,12},{1,3},{3,1},... | collective-permute-start | bytes 24584 | tf_op jit(solution)/shard_map/ppermute | solution.py:490
  50.8 1.6 %collective-permute-start.11 = (f32[2,56,512]{2,1,0:T(8,128)S(1)}, f32[2,56,512]{2,1,0:T(8,128)S(1)}, u32[]{:S(2)}, u32[]{:S(2)}) collective-permute-start(f32[2,56,512]{2,1,0:T(8,128)S(1)} %shard_map.155.refs_2_), channel_id=1, source_target_pairs={{0,1},{1,0},{2,3},{3,2},{4,5},{5,4},{6,7},{7,6},{8,9},{9,8},{10,11... | collective-permute-start | bytes 688136 | tf_op jit(solution)/shard_map/ppermute | solution.py:477
  53.1 9.8 %all-to-all-start.2 = ((f32[16,1,128]{2,1,0:T(1,128)}), f32[16,1,128]{2,1,0:T(1,128)S(1)}, u32[]{:S(2)}, u32[]{:S(2)}) async-start(f32[16,1,128]{2,1,0:T(1,128)} %get-tuple-element.57), calls=%async_computation.2 | async-start | bytes 16384 | tf_op jit(solution)/shard_map/all_to_all | solution.py:613

commit v4 on v3

--- a/solution.py
+++ b/solution.py
@@ -21,7 +21,7 @@
 NN = (((1,), (0,)), ((), ()))
 
 
-def call(kernel, out_shape, in_specs, scratch=(), limit=8 << 20, flops=1 << 20):
+def call(kernel, out_shape, in_specs, scratch=(), limit=8 << 20, aliases=None):
     many = isinstance(out_shape, (list, tuple))
     return pl.pallas_call(
         kernel,
@@ -29,8 +29,9 @@
         in_specs=in_specs,
         out_specs=[VMEM] * len(out_shape) if many else VMEM,
         scratch_shapes=list(scratch),
+        input_output_aliases=aliases or {},
         compiler_params=pltpu.CompilerParams(vmem_limit_bytes=limit),
-        cost_estimate=pl.CostEstimate(flops=flops, bytes_accessed=1 << 20, transcendentals=0),
+        cost_estimate=pl.CostEstimate(flops=1 << 20, bytes_accessed=1 << 20, transcendentals=0),
     )
 
 
@@ -54,9 +55,11 @@
     )
 
 
-def dot(left, right, axis):
-    pair = jnp.concatenate(split(right), axis=axis)
-    result = lax.dot_general(halves(left), pair, (((1,), (axis,)), ((), ())), preferred_element_type=f32)
+def dot(left, parts, axis):
+    if axis:
+        height = parts.shape[0] // 2
+        parts = jnp.concatenate([parts[:height, :], parts[height:, :]], axis=1)
+    result = lax.dot_general(halves(left), parts, (((1,), (axis,)), ((), ())), preferred_element_type=f32)
     return result[: left.shape[0]] + result[left.shape[0] :]
 
 
@@ -107,16 +110,22 @@
     return total
 
 
+def parts_of(block, rows, per):
+    block_row = jnp.floor((block + 0.5) / per)
+    layer = jnp.floor((block_row + 0.5) / rows)
+    return layer, block_row - layer * rows, block - block_row * per
+
+
 def load_kernel(
-    vertical, blocks, previous_square, control, spread, wind_e, wind_n, scale, previous, innovation,
+    vertical, blocks, control, spread, wind_e, wind_n, scale, previous, innovation,
     platforms, counts,
-    forth, back, square_v, control_v, spread_v, wind_e_v, wind_n_v, scale_v, previous_v, innovation_v,
-    blocks_v, platforms_v, counts_v, lon_out, first, last, vertical_s, blocks_s, square_s, sems,
+    forth, back, control_v, spread_v, wind_e_v, wind_n_v, scale_v, previous_v, innovation_v,
+    places, platforms_v, counts_v, lon_out, first, last, vertical_s, blocks_s, sems,
 ):
     pairs = (
         (spread, spread_v), (wind_e, wind_e_v), (wind_n, wind_n_v), (scale, scale_v), (blocks, blocks_s),
-        (vertical, vertical_s), (previous_square, square_s), (control, control_v),
-        (innovation, innovation_v), (previous, previous_v), (blocks, blocks_v), (platforms, platforms_v),
+        (vertical, vertical_s), (control, control_v),
+        (innovation, innovation_v), (previous, previous_v), (platforms, platforms_v),
         (counts, counts_v),
     )
     copies = [pltpu.make_async_copy(a, b, sems.at[i]) for i, (a, b) in enumerate(pairs)]
@@ -131,6 +140,8 @@
     for s in range(slots):
         for o in range(owners):
             numbers = jnp.where(line == s * owners + o, blocks_s[s, o].astype(f32), numbers)
+    layer, row, col = parts_of(numbers, rows, cols // LANES)
+    places[...] = ((layer * (cols // LANES) + col) * (rows + 8) + row).astype(jnp.int32)
     lane = lax.broadcasted_iota(jnp.int32, (rows, LANES), 1)
     packed = jnp.zeros((rows, LANES), f32)
     fields = (spread_v, wind_e_v, wind_n_v, scale_v)
@@ -159,7 +170,6 @@
                 a, b = lev * layers + l, other * layers + m
                 forth[at : at + 1, :] = jnp.full((1, LANES), vertical_s[a, b], f32)
                 back[at : at + 1, :] = jnp.full((1, LANES), vertical_s[b, a], f32)
-    square_v[...] = jnp.full((1, LANES), square_s[0], f32)
 
 
 def lon_item(packed, field, item, lane):
@@ -198,20 +208,38 @@
         diag[...] = edge_block(out[...])
 
 
+def extend_kernel(*refs):
+    half = len(refs) // 2
+    for field, out in zip(refs[:half], refs[half:]):
+        layers, rows, cols = field.shape
+        for l in range(layers):
+            out[l, :rows, :cols] = field[l]
+            out[l, rows:, :] = jnp.zeros((8, cols + LANES), f32)
+
+
+def parts_kernel(matrices, out):
+    count, height = matrices.shape[:2]
+
+    def body(i, carry):
+        out[i, :height, :], out[i, height:, :] = split(matrices[i])
+        return carry
+
+    for_each(count, body, 0)
+
+
 def at_ends():
     lat = lax.axis_index("lat")
     return lat == 0, lat == lax.axis_size("lat") - 1
 
 
-def unpack(own, lon_in, lat_1, lat_2, diag_1, diag_2, ext):
-    layers, rows, cols = own[0].shape
+def unpack(lon_in, lat_1, lat_2, diag_1, diag_2, ext):
+    layers, rows, cols = ext[0].shape[0], ext[0].shape[1] - 8, ext[0].shape[2] - LANES
     lane = lax.broadcasted_iota(jnp.int32, (rows, LANES), 1)
     keep = (lane < HALO) | (lane >= LANES - HALO)
     packed = lon_in[:rows, :]
     item = 0
-    for field, out in zip(own, ext):
+    for out in ext:
         for l in range(layers):
-            out[l, :rows, :cols] = field[l]
             tile = pltpu.roll(packed, LANES - 8 * item, 1) if item else packed
             out[l, :rows, cols:] = jnp.where(keep, tile, 0.0)
             item += 1
@@ -232,8 +260,6 @@
         from_south = jnp.where(bottom, jnp.where(even, b, a), 0.0)
         at = 0
         for out, l, w in [(e, l, w) for e, w in zip(ext, WIDTHS) for l in range(layers)]:
-            if w < HALO:
-                out[l, rows : rows + 8, begin : begin + width] = jnp.zeros((8, width), f32)
             out[l, rows : rows + w, begin : begin + width] = from_north[at : at + w, :]
             out[l, rows + 8 - w : rows + 8, begin : begin + width] = from_south[at : at + w, :]
             at += w
@@ -250,19 +276,18 @@
 
 
 def forward_kernel(
-    blocks, platforms, counts, mixed_in, spread_in, wind_e_in, wind_n_in, scale_in,
+    places, platforms, counts, mixed_in, spread_in, wind_e_in, wind_n_in, scale_in,
     lon_in, lat_1, lat_2, diag_1, diag_2, interp, innovation,
-    sent, spread, scale, wind_e, wind_n,
-    mixed, field, blocks_s, platforms_s, counts_s, sems,
+    sent, mixed, spread, wind_e, wind_n, scale,
+    field, places_s, platforms_s, counts_s, sems,
 ):
-    pairs = ((blocks, blocks_s), (platforms, platforms_s), (counts, counts_s))
+    pairs = ((places, places_s), (platforms, platforms_s), (counts, counts_s))
     copies = [pltpu.make_async_copy(a, b, sems.at[i]) for i, (a, b) in enumerate(pairs)]
     for copy in copies:
         copy.start()
-    own = (mixed_in, spread_in, wind_e_in, wind_n_in, scale_in)
-    unpack(own, lon_in, lat_1, lat_2, diag_1, diag_2, (mixed, spread, wind_e, wind_n, scale))
+    unpack(lon_in, lat_1, lat_2, diag_1, diag_2, (mixed, spread, wind_e, wind_n, scale))
     layers, ext_rows, ext_cols = mixed.shape
-    rows, per = ext_rows - 8, ext_cols // LANES - 1
+    per = ext_cols // LANES - 1
     mask = inside_mask((ext_rows, ext_cols))
     for l in range(layers):
         x = scale[l] * smooth(mixed[l], spread[l])
@@ -283,12 +308,11 @@
     for copy in copies:
         copy.wait()
     count, width = innovation.shape
-    slots, owners = blocks.shape
+    slots, owners = platforms.shape
     row = lax.broadcasted_iota(jnp.int32, (count, width), 0)
 
     def body(b, total):
-        block = blocks_s[b % slots, b // slots]
-        at = (block // (rows * per) * per + block % per) * ext_rows + (block // per) % rows
+        at = places_s[0, (b % slots) * owners + b // slots]
         left = jnp.where(row == b, jnp.broadcast_to(field[pl.ds(at, 1), :], (count, width)), 0.0)
         return total + dot(left, interp[b], 1)
 
@@ -313,7 +337,7 @@
     x, where = values[...], platform[...]
     total = jnp.zeros(x.shape, f32)
     for p in range(matrices.shape[0]):
-        total = total + dot(jnp.where(where == float(p), x, 0.0), matrices[p], 1)
+        total = total + dot(jnp.where(where == float(p), x, 0.0), jnp.concatenate(split(matrices[p]), axis=0), 1)
     out[...] = jnp.zeros(out.shape, f32)
     for t in range(tiles):
         for s in range(slots):
@@ -337,7 +361,8 @@
 
 
 def place_kernel(count, kinds, rows, layers, per, *refs):
-    tiles, out = refs[:-1], refs[-1]
+    tiles, square, out, square_out = refs[:-3], refs[-3], refs[-2], refs[-1]
+    square_out[...] = jnp.full((1, LANES), square[0], f32)
     line = lax.broadcasted_iota(jnp.int32, (1, LANES), 1)
     south_end, north_end = at_ends()
     odd = lax.axis_index("lat") % 2
@@ -345,10 +370,7 @@
     targets = [jnp.full((1, LANES), -1.0, f32) for _ in range(packs)]
     for i, (tile, (phase, lon_step, begin)) in enumerate(zip(tiles, kinds)):
         block = tile[begin : begin + 1, :LANES]
-        block_row = jnp.floor((block + 0.5) / per)
-        col = block - block_row * per
-        layer = jnp.floor((block_row + 0.5) / rows)
-        row = block_row - layer * rows
+        layer, row, col = parts_of(block, rows, per)
         valid = block >= 0.0
         if phase:
             is_north = jnp.where(odd == phase - 1, 1, 0)
@@ -499,23 +521,23 @@
     mix = held(layers * layers * n_lev, LANES)
     innovations = innovation.reshape(count, width)
     (
-        forth, back, square_v, control_v, spread_v, wind_e_v, wind_n_v, scale_v, previous_v, innovation_v,
-        blocks_v, platforms_v, counts_v, lon_part, first, last,
+        forth, back, control_v, spread_v, wind_e_v, wind_n_v, scale_v, previous_v, innovation_v,
+        places, platforms_v, counts_v, lon_part, first, last,
     ) = call(
         load_kernel,
-        [mix, mix, held(1, LANES)] + [field] * 6 + [held(count, width)]
-        + [held(*x.shape, dtype=jnp.int32) for x in (blocks, platforms, counts)]
+        [mix, mix] + [field] * 6 + [held(count, width)]
+        + [held(1, LANES, dtype=jnp.int32)]
+        + [held(*x.shape, dtype=jnp.int32) for x in (platforms, counts)]
         + [held(rows + 8, LANES), held(lat_rows, cols), held(lat_rows, cols)],
-        [HBM] * 12,
+        [HBM] * 11,
         [
             pltpu.SMEM(vertical.shape, f32),
             pltpu.SMEM(blocks.shape, jnp.int32),
-            pltpu.SMEM((1,), f32),
-            pltpu.SemaphoreType.DMA((13,)),
+            pltpu.SemaphoreType.DMA((11,)),
         ],
         58 << 20,
     )(
-        vertical, blocks, previous_square, control, spread, wind_lon, wind_lat, error_scale, previous_direction,
+        vertical, blocks, control, spread, wind_lon, wind_lat, error_scale, previous_direction,
         innovations, platforms, counts,
     )
     blended, lon_out, lat_1, lat_2, diag_1, diag_2 = call(
@@ -543,29 +565,30 @@
 
     half = -(-slots // 4) * 4
     ext = held(layers, ext_rows, ext_cols)
-    sent, ext_spread, ext_scale, ext_e, ext_n = call(
+    exts = call(extend_kernel, [ext] * 5, [VMEM] * 5)(blended, spread_v, wind_e_v, wind_n_v, scale_v)
+    matrices = error_inverse.reshape(error_inverse.shape[-3:])
+    weights = call(parts_kernel, held(count, 2 * width, width, dtype=bf16), [VMEM], (), limit)(weights)
+    sent, _, ext_spread, ext_e, ext_n, ext_scale = call(
         forward_kernel,
-        [shape(owners, 2 * half, width), ext, ext, ext, ext],
+        [held(owners, 2 * half, width)] + [ext] * 5,
         [VMEM] * 15,
         [
-            pltpu.VMEM((layers, ext_rows, ext_cols), f32),
             pltpu.VMEM((layers * ext_rows * per, LANES), f32),
-            pltpu.SMEM(blocks.shape, jnp.int32),
+            pltpu.SMEM((1, LANES), jnp.int32),
             pltpu.SMEM(blocks.shape, jnp.int32),
             pltpu.SMEM(counts.shape, jnp.int32),
             pltpu.SemaphoreType.DMA((3,)),
         ],
         limit,
+        {3 + i: 1 + i for i in range(5)},
     )(
-        blocks_v, platforms_v, counts_v, blended, spread_v, wind_e_v, wind_n_v, scale_v,
-        lon_in, lat_in[1], lat_in[2], diag_in[1], diag_in[2], weights, innovation_v,
+        places, platforms_v, counts_v, *exts, lon_in, lat_in[1], lat_in[2], diag_in[1], diag_in[2], weights, innovation_v,
     )
 
     arrived = lax.all_to_all(sent, ("lat", "lon"), split_axis=0, concat_axis=0, tiled=True)
-    matrices = error_inverse.reshape(error_inverse.shape[-3:])
     result = call(
         functools.partial(weigh_kernel, slots),
-        shape(owners, 2 * half, width),
+        held(owners, 2 * half, width),
         [VMEM] * 2,
         [pltpu.VMEM((count, width), f32)] * 2,
     )(arrived, matrices)
@@ -588,13 +611,13 @@
             tiles.append(diag_raw[phase, step])
             kinds.append((phase, step, lat_fields))
     depth = -(-len(kinds) * count // LANES) * LANES
-    chosen = call(
+    chosen, square_v = call(
         functools.partial(place_kernel, count, kinds, rows, layers, per),
-        held(layers * (per + 2) * ext_rows, 2 * depth, dtype=bf16),
-        [VMEM] * len(tiles),
+        [held(layers * (per + 2) * ext_rows, 2 * depth, dtype=bf16), held(1, LANES)],
+        [VMEM] * len(tiles) + [SMEM],
         (),
         limit,
-    )(*tiles)
+    )(*tiles, previous_square)
     filtered = call(
         functools.partial(adjoint_kernel, len(sources)),
         shape(layers, rows, cols),

time: 64 us -> 64.4 us (level)
  starting transfers between devices: 20.4 us -> 22.5 us
  waiting for transfers between devices: 14.8 us -> 13.1 us
    all_to_all x1, starting transfers between devices: 3.47 us -> 5.42 us  [local(): lax.all_to_all(partial, ('lat', 'lon', 'lev'), split_axis=0, concat_axis=...]
    ppermute x10, waiting for transfers between devices: 7.69 us -> 5.94 us  [exchange(): return lax.ppermute(field, ('lat', 'lon'), pairs)]
    pallas_call x4 -> x6, Pallas kernels: 4.48 us -> 4.56 us  [the longest x1 2.32 us: local(): call(forward_kernel, [held(owners, 2 * half, width)] + [ext] * 5, [VMEM]...]
  transfers between devices with their start and end apart: 13 -> 13, of which waited for: 7 -> 5; matrix products, arithmetic and copies ran while one was open for 1% -> 1% of each run, Pallas kernels for 3% -> 3%
where the time goes in v4:
time: 64.4 us; the launch traced here: 64.1 us
  starting transfers between devices  22.5 us (35%)
  blocking collectives  18.7 us (29%)
  waiting for transfers between devices  13.1 us (20%)
  Pallas kernels  7.76 us (12%)
  between operations  1.42 us (2%)
  local copies, waits for them, and re-layouts  0.7 us (1%)
    ppermute x10, starting transfers between devices, exchange(): return lax.ppermute(field, ('lat', 'lon'), pairs)  16.5 us
    all_to_all x1, blocking collectives, local(): lax.all_to_all(sent, ('lat', 'lon'), split_axis=0, concat_axis=0, tiled=T...  9.59 us
    all_to_all x1, blocking collectives, local(): lax.all_to_all(result, ('lat', 'lon'), split_axis=0, concat_axis=0, tiled...  9.07 us
    ppermute x10, waiting for transfers between devices, exchange(): return lax.ppermute(field, ('lat', 'lon'), pairs)  5.94 us
    all_to_all x1, waiting for transfers between devices, local(): lax.all_to_all(partial, ('lat', 'lon', 'lev'), split_axis=0, concat_axis=...  5.64 us
    all_to_all x1, starting transfers between devices, local(): lax.all_to_all(partial, ('lat', 'lon', 'lev'), split_axis=0, concat_axis=...  5.42 us
    pallas_call x1, Pallas kernels, local(): call(forward_kernel, [held(owners, 2 * half, width)] + [ext] * 5, [VMEM]...  2.32 us
    pallas_call x1, Pallas kernels, local(): call(load_kernel, [mix, mix] + [field] * 6 + [held(count, width)] + [held...  1.57 us
  transfers between devices with their start and end apart: 13, of which 5 were waited for; matrix products, arithmetic and copies ran while one was open for 1% of the time, Pallas kernels for 3%

profile of v4, /device:TPU:0, one launch (start us, length us, event | category | flops | bytes accessed | tf_op | source)
XLA Modules:
  0.0 64.1 jit_solution(8606093231540947747)
XLA Ops:
  1.2 1.6 %shard_map.149 = (f32[8,128]{1,0:T(8,128)S(1)}, f32[8,128]{1,0:T(8,128)S(1)}, f32[2,56,512]{2,1,0:T(8,128)S(1)}, f32[2,56,512]{2,1,0:T(8,128)S(1)}, f32[2,56,512...) custom-call(f32[4,4]{1,0:T(4,128)} %vertical.1, ...), custom_call_target="tpu_custom_call" | custom-call | flops 1048576 | bytes 1048576 | tf_op jit(solution)/shard_map/pallas_call | solution.py:526
  2.9 2.7 %collective-permute-start.2 = (f32[40,512]{1,0:T(8,128)S(1)}, f32[40,512]{1,0:T(8,128)S(1)}, u32[]{:S(2)}, u32[]{:S(2)}) collective-permute-start(f32[40,512]{1,0:T(8,128)S(1)} %get-tuple-element.44), channel_id=1, source_target_pairs={{0,4},{2,6},{4,0},{6,2},{8,12},{10,14},{12,8},{14,10},{1,5},{3,7},... | collective-permute-start | bytes 245768 | tf_op jit(solution)/shard_map/ppermute | solution.py:512
  5.7 2.5 %collective-permute-start.4 = (f32[40,512]{1,0:T(8,128)S(1)}, f32[40,512]{1,0:T(8,128)S(1)}, u32[]{:S(2)}, u32[]{:S(2)}) collective-permute-start(f32[40,512]{1,0:T(8,128)S(1)} %get-tuple-element.46), channel_id=1, source_target_pairs={{0,12},{2,14},{4,8},{6,10},{8,4},{10,6},{12,0},{14,2},{1,13},{3,15... | collective-permute-start | bytes 245768 | tf_op jit(solution)/shard_map/ppermute | solution.py:512
  8.1 1.5 %collective-permute-start.1 = (f32[64,128]{1,0:T(8,128)S(1)}, f32[64,128]{1,0:T(8,128)S(1)}, u32[]{:S(2)}, u32[]{:S(2)}) collective-permute-start(f32[64,128]{1,0:T(8,128)S(1)} %get-tuple-element.43.refs_0_), channel_id=1, source_target_pairs={{0,2},{2,0},{4,6},{6,4},{8,10},{10,8},{12,14},{14,12},{1,3},{3,1},... | collective-permute-start | bytes 98312 | tf_op jit(solution)/shard_map/ppermute | solution.py:512
  9.6 0.6 %collective-permute-start.3 = (f32[40,128]{1,0:T(8,128)S(1)}, f32[40,128]{1,0:T(8,128)S(1)}, u32[]{:S(2)}, u32[]{:S(2)}) collective-permute-start(f32[40,128]{1,0:T(8,128)S(1)} %get-tuple-element.45), channel_id=1, source_target_pairs={{0,6},{2,4},{4,2},{6,0},{8,14},{10,12},{12,10},{14,8},{1,7},{3,5},... | collective-permute-start | bytes 61448 | tf_op jit(solution)/shard_map/ppermute | solution.py:512
  10.3 1.8 %collective-permute-start.5 = (f32[40,128]{1,0:T(8,128)S(1)}, f32[40,128]{1,0:T(8,128)S(1)}, u32[]{:S(2)}, u32[]{:S(2)}) collective-permute-start(f32[40,128]{1,0:T(8,128)S(1)} %get-tuple-element.47), channel_id=1, source_target_pairs={{0,14},{2,12},{4,10},{6,8},{8,6},{10,4},{12,2},{14,0},{1,15},{3,13... | collective-permute-start | bytes 61448 | tf_op jit(solution)/shard_map/ppermute | solution.py:512
  12.3 2.0 %collective-permute-done.3.refs_3_.diag_1 = f32[40,128]{1,0:T(8,128)S(1)} collective-permute-done((f32[40,128]{1,0:T(8,128)S(1)}, f32[40,128]{1,0:T(8,128)S(1)}, u32[]{:S(2)}, u32[]{:S(2)}) %collective-permute-start.3) | collective-permute-done | bytes 20512 | tf_op jit(solution)/shard_map/ppermute | solution.py:512
  14.3 2.4 %collective-permute-done.5.refs_5_.diag_2 = f32[40,128]{1,0:T(8,128)S(1)} collective-permute-done((f32[40,128]{1,0:T(8,128)S(1)}, f32[40,128]{1,0:T(8,128)S(1)}, u32[]{:S(2)}, u32[]{:S(2)}) %collective-permute-start.5) | collective-permute-done | bytes 20512 | tf_op jit(solution)/shard_map/ppermute | solution.py:512
  16.8 2.3 %shard_map.154 = (f32[8,8,128]{2,1,0:T(8,128)S(1)}, f32[2,64,640]{2,1,0:T(8,128)S(1)}, f32[2,64,640]{2,1,0:T(8,128)S(1)}, f32[2,64,640]{2,1,0:T(8,128)S(1)}, f32...) custom-call(s32[1,128]{1,0:T(1,128)S(1)} %get-tuple-element.49.place, ...), custom_call_target="tpu_custom_call", output_to_operand_aliasing={{1}: (3, {}), {2}: (4, {}), {3}: (5, {}), {4}: (6, {}), {5}... | custom-call | flops 1048576 | bytes 1048576 | tf_op jit(solution)/shard_map/pallas_call | solution.py:571
  19.1 9.6 %all_to_all.15.arrived = f32[8,8,128]{2,1,0:T(8,128)S(1)} all-to-all(f32[8,8,128]{2,1,0:T(8,128)S(1)} %get-tuple-element.63), channel_id=1, replica_groups=mesh['member'=2,'lat'=4,'lon'=2,'lev'=2] {'lat','lon'}, dimensions={0} | all-to-all | bytes 65536 | tf_op jit(solution)/shard_map/all_to_all | solution.py:588
  29.0 9.1 %all_to_all.16.returned = f32[8,8,128]{2,1,0:T(8,128)S(1)} all-to-all(f32[8,8,128]{2,1,0:T(8,128)S(1)} %shard_map.155), channel_id=1, replica_groups=mesh['member'=2,'lat'=4,'lon'=2,'lev'=2] {'lat','lon'}, dimensions={0} | all-to-all | bytes 65536 | tf_op jit(solution)/shard_map/all_to_all | solution.py:595
  38.3 0.7 %collective-permute-start.10 = (f32[16,128]{1,0:T(8,128)S(1)}, f32[16,128]{1,0:T(8,128)S(1)}, u32[]{:S(2)}, u32[]{:S(2)}) collective-permute-start(f32[16,128]{1,0:T(8,128)S(1)} %shard_map.156.refs_1_), channel_id=1, source_target_pairs={{0,14},{2,12},{4,10},{6,8},{8,6},{10,4},{12,2},{14,0},{1,15},{3,13... | collective-permute-start | bytes 24584 | tf_op jit(solution)/shard_map/ppermute | solution.py:512
  39.0 1.3 %collective-permute-start.6 = (f32[16,128]{1,0:T(8,128)S(1)}, f32[16,128]{1,0:T(8,128)S(1)}, u32[]{:S(2)}, u32[]{:S(2)}) collective-permute-start(f32[16,128]{1,0:T(8,128)S(1)} %shard_map.156.refs_1_), channel_id=1, source_target_pairs={{0,2},{2,0},{4,6},{6,4},{8,10},{10,8},{12,14},{14,12},{1,3},{3,1},... | collective-permute-start | bytes 24584 | tf_op jit(solution)/shard_map/ppermute | solution.py:512
  40.4 0.5 collective-permute-start.7
  40.9 1.6 %collective-permute-start.8 = (f32[16,128]{1,0:T(8,128)S(1)}, f32[16,128]{1,0:T(8,128)S(1)}, u32[]{:S(2)}, u32[]{:S(2)}) collective-permute-start(f32[16,128]{1,0:T(8,128)S(1)} %shard_map.156.refs_1_), channel_id=1, source_target_pairs={{0,6},{2,4},{4,2},{6,0},{8,14},{10,12},{12,10},{14,8},{1,7},{3,5},... | collective-permute-start | bytes 24584 | tf_op jit(solution)/shard_map/ppermute | solution.py:512
  42.5 3.1 %collective-permute-start.9 = (f32[16,128]{1,0:T(8,128)S(1)}, f32[16,128]{1,0:T(8,128)S(1)}, u32[]{:S(2)}, u32[]{:S(2)}) collective-permute-start(f32[16,128]{1,0:T(8,128)S(1)} %shard_map.156.refs_1_), channel_id=1, source_target_pairs={{0,12},{2,14},{4,8},{6,10},{8,4},{10,6},{12,0},{14,2},{1,13},{3,15... | collective-permute-start | bytes 24584 | tf_op jit(solution)/shard_map/ppermute | solution.py:512
  46.5 1.5 %collective-permute-done.9.refs_5_ = f32[16,128]{1,0:T(8,128)S(1)} collective-permute-done((f32[16,128]{1,0:T(8,128)S(1)}, f32[16,128]{1,0:T(8,128)S(1)}, u32[]{:S(2)}, u32[]{:S(2)}) %collective-permute-start.9) | collective-permute-done | bytes 8224 | tf_op jit(solution)/shard_map/ppermute | solution.py:512
  48.0 1.2 %shard_map.157.refs_2_ = f32[2,56,512]{2,1,0:T(8,128)S(1)} custom-call(bf16[768,256]{1,0:T(8,128)(2,1)S(1)} %get-tuple-element.48.refs_0_, f32[16,128]{1,0:T(8,128)S(1)} %shard_map.156.refs_1_, f32[16,128]{1,0:T(8,128)S(1)} %collective-permute-done.6.refs_2_, f32[16,128]{1,0:T(8,128)S(1)} %collective-permute-done.7.refs_3_, ...), custom_call_target="tpu_custom_call" | custom-call | flops 1048576 | bytes 1048576 | tf_op jit(solution)/shard_map/pallas_call | solution.py:621
  49.3 1.5 %collective-permute-done.11.refs_3_ = f32[2,56,512]{2,1,0:T(8,128)S(1)} collective-permute-done((f32[2,56,512]{2,1,0:T(8,128)S(1)}, f32[2,56,512]{2,1,0:T(8,128)S(1)}, u32[]{:S(2)}, u32[]{:S(2)}) %collective-permute-start.11) | collective-permute-done | bytes 229408 | tf_op jit(solution)/shard_map/ppermute | solution.py:499
  50.7 0.8 %shard_map.158 = (f32[2,56,512]{2,1,0:T(8,128)S(1)}, f32[16,1,128]{2,1,0:T(1,128)}) custom-call(f32[8,128]{1,0:T(8,128)S(1)} %get-tuple-element.37.refs_0_, f32[2,56,512]{2,1,0:T(8,128)S(1)} %get-tuple-element.38.refs_1_, f32[2,56,512]{2,1,0:T(8,128)S(1)} %shard_map.157.refs_2_, f32[2,56,512]{2,1,0:T(8,128)S(1)} %collective-permute-done.11.refs_3_), custom_call_target="tpu_custom_call" | custom-call | flops 1048576 | bytes 1048576 | tf_op jit(solution)/shard_map/pallas_call | solution.py:631
  51.5 5.4 %all-to-all-start.2 = ((f32[16,1,128]{2,1,0:T(1,128)}), f32[16,1,128]{2,1,0:T(1,128)S(1)}, u32[]{:S(2)}, u32[]{:S(2)}) async-start(f32[16,1,128]{2,1,0:T(1,128)} %get-tuple-element.69), calls=%async_computation.2 | async-start | bytes 16384 | tf_op jit(solution)/shard_map/all_to_all | solution.py:636
  56.9 0.7 %copy.26 = f32[2,56,512]{2,1,0:T(8,128)} copy(f32[2,56,512]{2,1,0:T(8,128)S(1)} %get-tuple-element.72.gradient) | data formatting | bytes 458752
  57.6 5.6 %all-to-all-done.2.sums = f32[16,1,128]{2,1,0:T(1,128)S(1)} async-done(((f32[16,1,128]{2,1,0:T(1,128)}), f32[16,1,128]{2,1,0:T(1,128)S(1)}, u32[]{:S(2)}, u32[]{:S(2)}) %all-to-all-start.2) | async-done | bytes 8224 | tf_op jit(solution)/shard_map/all_to_all | solution.py:636
  63.2 0.8 %shard_map.159 = f32[2,56,512]{2,1,0:T(8,128)} custom-call(f32[2,56,512]{2,1,0:T(8,128)S(1)} %get-tuple-element.72.gradient, f32[16,1,128]{2,1,0:T(1,128)S(1)} %all-to-all-done.2.sums, f32[2,56,512]{2,1,0:T(8,128)S(1)} %get-tuple-element.70.previous, f32[1,128]{1,0:T(1,128)S(1)} %get-tuple-element.71.previous_square), custom_call_target="tpu_custom_call" | custom-call | flops 1048576 | bytes 1048576 | tf_op jit(solution)/shard_map/pallas_call | solution.py:637
  (20 shorter events, 1.7 us)
Async XLA Ops:
  0.6 11.5 %copy-start = (f32[1,1,1,8,2,128,128]{6,5,4,3,2,1,0:T(8,128)S(1)}, f32[1,1,1,8,2,128,128]{6,5,4,3,2,1,0:T(8,128)}, u32[]{:S(2)}) copy-start(f32[1,1,1,8,2,128,128]{6,5,4,3,2,1,0:T(8,128)} %param.23) | copy-start | bytes 3145732
  0.6 2.1 %collective-permute-start = (f32[2,56,512]{2,1,0:T(8,128)}, f32[2,56,512]{2,1,0:T(8,128)S(1)}, u32[]{:S(2)}, u32[]{:S(2)}) collective-permute-start(f32[2,56,512]{2,1,0:T(8,128)} %control.1), channel_id=1, source_target_pairs={{0,1},{1,0},{2,3},{3,2},{4,5},{5,4},{6,7},{7,6},{8,9},{9,8},{10,11... | collective-permute-start | bytes 688136 | tf_op jit(solution)/shard_map/ppermute | solution.py:499
  2.9 13.8 %collective-permute-start.2 = (f32[40,512]{1,0:T(8,128)S(1)}, f32[40,512]{1,0:T(8,128)S(1)}, u32[]{:S(2)}, u32[]{:S(2)}) collective-permute-start(f32[40,512]{1,0:T(8,128)S(1)} %get-tuple-element.44), channel_id=1, source_target_pairs={{0,4},{2,6},{4,0},{6,2},{8,12},{10,14},{12,8},{14,10},{1,5},{3,7},... | collective-permute-start | bytes 245768 | tf_op jit(solution)/shard_map/ppermute | solution.py:512
  5.7 11.1 %collective-permute-start.4 = (f32[40,512]{1,0:T(8,128)S(1)}, f32[40,512]{1,0:T(8,128)S(1)}, u32[]{:S(2)}, u32[]{:S(2)}) collective-permute-start(f32[40,512]{1,0:T(8,128)S(1)} %get-tuple-element.46), channel_id=1, source_target_pairs={{0,12},{2,14},{4,8},{6,10},{8,4},{10,6},{12,0},{14,2},{1,13},{3,15... | collective-permute-start | bytes 245768 | tf_op jit(solution)/shard_map/ppermute | solution.py:512
  8.1 8.6 %collective-permute-start.1 = (f32[64,128]{1,0:T(8,128)S(1)}, f32[64,128]{1,0:T(8,128)S(1)}, u32[]{:S(2)}, u32[]{:S(2)}) collective-permute-start(f32[64,128]{1,0:T(8,128)S(1)} %get-tuple-element.43.refs_0_), channel_id=1, source_target_pairs={{0,2},{2,0},{4,6},{6,4},{8,10},{10,8},{12,14},{14,12},{1,3},{3,1},... | collective-permute-start | bytes 98312 | tf_op jit(solution)/shard_map/ppermute | solution.py:512
  9.6 4.7 %collective-permute-start.3 = (f32[40,128]{1,0:T(8,128)S(1)}, f32[40,128]{1,0:T(8,128)S(1)}, u32[]{:S(2)}, u32[]{:S(2)}) collective-permute-start(f32[40,128]{1,0:T(8,128)S(1)} %get-tuple-element.45), channel_id=1, source_target_pairs={{0,6},{2,4},{4,2},{6,0},{8,14},{10,12},{12,10},{14,8},{1,7},{3,5},... | collective-permute-start | bytes 61448 | tf_op jit(solution)/shard_map/ppermute | solution.py:512
  10.3 6.5 %collective-permute-start.5 = (f32[40,128]{1,0:T(8,128)S(1)}, f32[40,128]{1,0:T(8,128)S(1)}, u32[]{:S(2)}, u32[]{:S(2)}) collective-permute-start(f32[40,128]{1,0:T(8,128)S(1)} %get-tuple-element.47), channel_id=1, source_target_pairs={{0,14},{2,12},{4,10},{6,8},{8,6},{10,4},{12,2},{14,0},{1,15},{3,13... | collective-permute-start | bytes 61448 | tf_op jit(solution)/shard_map/ppermute | solution.py:512
  16.8 11.9 %copy-start.1 = (f32[1,1,8,128,128]{4,3,2,1,0:T(8,128)S(1)}, f32[1,1,8,128,128]{4,3,2,1,0:T(8,128)}, u32[]{:S(2)}) copy-start(f32[1,1,8,128,128]{4,3,2,1,0:T(8,128)} %param.25) | copy-start | bytes 1572868
  38.3 8.2 %collective-permute-start.10 = (f32[16,128]{1,0:T(8,128)S(1)}, f32[16,128]{1,0:T(8,128)S(1)}, u32[]{:S(2)}, u32[]{:S(2)}) collective-permute-start(f32[16,128]{1,0:T(8,128)S(1)} %shard_map.156.refs_1_), channel_id=1, source_target_pairs={{0,14},{2,12},{4,10},{6,8},{8,6},{10,4},{12,2},{14,0},{1,15},{3,13... | collective-permute-start | bytes 24584 | tf_op jit(solution)/shard_map/ppermute | solution.py:512
  39.0 7.4 %collective-permute-start.6 = (f32[16,128]{1,0:T(8,128)S(1)}, f32[16,128]{1,0:T(8,128)S(1)}, u32[]{:S(2)}, u32[]{:S(2)}) collective-permute-start(f32[16,128]{1,0:T(8,128)S(1)} %shard_map.156.refs_1_), channel_id=1, source_target_pairs={{0,2},{2,0},{4,6},{6,4},{8,10},{10,8},{12,14},{14,12},{1,3},{3,1},... | collective-permute-start | bytes 24584 | tf_op jit(solution)/shard_map/ppermute | solution.py:512
  40.4 6.1 %collective-permute-start.7 = (f32[16,128]{1,0:T(8,128)S(1)}, f32[16,128]{1,0:T(8,128)S(1)}, u32[]{:S(2)}, u32[]{:S(2)}) collective-permute-start(f32[16,128]{1,0:T(8,128)S(1)} %shard_map.156.refs_1_), channel_id=1, source_target_pairs={{0,4},{2,6},{4,0},{6,2},{8,12},{10,14},{12,8},{14,10},{1,5},{3,7},... | collective-permute-start | bytes 24584 | tf_op jit(solution)/shard_map/ppermute | solution.py:512
  40.9 5.6 %collective-permute-start.8 = (f32[16,128]{1,0:T(8,128)S(1)}, f32[16,128]{1,0:T(8,128)S(1)}, u32[]{:S(2)}, u32[]{:S(2)}) collective-permute-start(f32[16,128]{1,0:T(8,128)S(1)} %shard_map.156.refs_1_), channel_id=1, source_target_pairs={{0,6},{2,4},{4,2},{6,0},{8,14},{10,12},{12,10},{14,8},{1,7},{3,5},... | collective-permute-start | bytes 24584 | tf_op jit(solution)/shard_map/ppermute | solution.py:512
  42.5 5.4 %collective-permute-start.9 = (f32[16,128]{1,0:T(8,128)S(1)}, f32[16,128]{1,0:T(8,128)S(1)}, u32[]{:S(2)}, u32[]{:S(2)}) collective-permute-start(f32[16,128]{1,0:T(8,128)S(1)} %shard_map.156.refs_1_), channel_id=1, source_target_pairs={{0,12},{2,14},{4,8},{6,10},{8,4},{10,6},{12,0},{14,2},{1,13},{3,15... | collective-permute-start | bytes 24584 | tf_op jit(solution)/shard_map/ppermute | solution.py:512
  49.2 1.6 %collective-permute-start.11 = (f32[2,56,512]{2,1,0:T(8,128)S(1)}, f32[2,56,512]{2,1,0:T(8,128)S(1)}, u32[]{:S(2)}, u32[]{:S(2)}) collective-permute-start(f32[2,56,512]{2,1,0:T(8,128)S(1)} %shard_map.157.refs_2_), channel_id=1, source_target_pairs={{0,1},{1,0},{2,3},{3,2},{4,5},{5,4},{6,7},{7,6},{8,9},{9,8},{10,11... | collective-permute-start | bytes 688136 | tf_op jit(solution)/shard_map/ppermute | solution.py:499
  51.5 11.8 %all-to-all-start.2 = ((f32[16,1,128]{2,1,0:T(1,128)}), f32[16,1,128]{2,1,0:T(1,128)S(1)}, u32[]{:S(2)}, u32[]{:S(2)}) async-start(f32[16,1,128]{2,1,0:T(1,128)} %get-tuple-element.69), calls=%async_computation.2 | async-start | bytes 16384 | tf_op jit(solution)/shard_map/all_to_all | solution.py:636

commit v5 on v4

--- a/solution.py
+++ b/solution.py
@@ -209,8 +209,10 @@
 
 
 def extend_kernel(*refs):
+    square, refs = refs[0], refs[1:]
     half = len(refs) // 2
-    for field, out in zip(refs[:half], refs[half:]):
+    refs[-1][...] = jnp.full((1, LANES), square[0], f32)
+    for field, out in zip(refs[:half], refs[half:-1]):
         layers, rows, cols = field.shape
         for l in range(layers):
             out[l, :rows, :cols] = field[l]
@@ -361,8 +363,7 @@
 
 
 def place_kernel(count, kinds, rows, layers, per, *refs):
-    tiles, square, out, square_out = refs[:-3], refs[-3], refs[-2], refs[-1]
-    square_out[...] = jnp.full((1, LANES), square[0], f32)
+    tiles, out = refs[:-1], refs[-1]
     line = lax.broadcasted_iota(jnp.int32, (1, LANES), 1)
     south_end, north_end = at_ends()
     odd = lax.axis_index("lat") % 2
@@ -455,11 +456,12 @@
     partial[...] = jnp.broadcast_to(total[None], partial.shape)
 
 
-def direction_kernel(cell_count, gradient, sums, previous, previous_square, direction):
+def direction_kernel(cell_count, gradient_in, sums, previous, previous_square, gradient, direction):
     total = jnp.sum(jnp.sum(sums[...], axis=0), axis=1, keepdims=True)
     factor = total / cell_count / previous_square[:, 0:1]
     for l in range(gradient.shape[0]):
-        direction[l] = factor * previous[l] - gradient[l]
+        gradient[l] = gradient_in[l]
+        direction[l] = factor * previous[l] - gradient_in[l]
 
 
 def local(
@@ -500,8 +502,8 @@
         ]
 
     def partner(a, phase):
-        step = 1 if (a % 2 == 0) == (phase == 1) else -1
-        return (a + step) % n_lat
+        to = a + (1 if (a % 2 == 0) == (phase == 1) else -1)
+        return to if 0 <= to < n_lat else a
 
     def exchange(field, phase, lon_step):
         pairs = []
@@ -565,7 +567,9 @@
 
     half = -(-slots // 4) * 4
     ext = held(layers, ext_rows, ext_cols)
-    exts = call(extend_kernel, [ext] * 5, [VMEM] * 5)(blended, spread_v, wind_e_v, wind_n_v, scale_v)
+    *exts, square_v = call(extend_kernel, [ext] * 5 + [held(1, LANES)], [SMEM] + [VMEM] * 5)(
+        previous_square, blended, spread_v, wind_e_v, wind_n_v, scale_v
+    )
     matrices = error_inverse.reshape(error_inverse.shape[-3:])
     weights = call(parts_kernel, held(count, 2 * width, width, dtype=bf16), [VMEM], (), limit)(weights)
     sent, _, ext_spread, ext_e, ext_n, ext_scale = call(
@@ -594,7 +598,7 @@
     )(arrived, matrices)
     returned = lax.all_to_all(result, ("lat", "lon"), split_axis=0, concat_axis=0, tiled=True)
     adjoint_obs = call(
-        functools.partial(transpose_kernel, slots), shape(count, width), [VMEM] * 2, (), limit
+        functools.partial(transpose_kernel, slots), held(count, width), [VMEM] * 2, (), limit
     )(returned, weights)
 
     sources, tiles, kinds = [adjoint_obs], [lon_out], [(0, 0, rows)]
@@ -611,16 +615,16 @@
             tiles.append(diag_raw[phase, step])
             kinds.append((phase, step, lat_fields))
     depth = -(-len(kinds) * count // LANES) * LANES
-    chosen, square_v = call(
+    chosen = call(
         functools.partial(place_kernel, count, kinds, rows, layers, per),
-        [held(layers * (per + 2) * ext_rows, 2 * depth, dtype=bf16), held(1, LANES)],
-        [VMEM] * len(tiles) + [SMEM],
+        held(layers * (per + 2) * ext_rows, 2 * depth, dtype=bf16),
+        [VMEM] * len(tiles),
         (),
         limit,
-    )(*tiles, previous_square)
+    )(*tiles)
     filtered = call(
         functools.partial(adjoint_kernel, len(sources)),
-        shape(layers, rows, cols),
+        held(layers, rows, cols),
         [VMEM] * (5 + len(sources)),
         (),
         limit,
@@ -630,13 +634,13 @@
     group = n_lat * n_lon * n_lev
     gradient, partial = call(
         functools.partial(gradient_kernel, len(others)),
-        [field, shape(group, 1, LANES)],
+        [field, held(group, 1, LANES)],
         [VMEM] * (3 + len(others)),
     )(back, control_v, filtered, *others)
     sums = lax.all_to_all(partial, ("lat", "lon", "lev"), split_axis=0, concat_axis=0, tiled=True)
-    direction = call(
+    gradient, direction = call(
         functools.partial(direction_kernel, float(control.size * group)),
-        shape(layers, rows, cols),
+        [shape(layers, rows, cols)] * 2,
         [VMEM] * 4,
     )(gradient, sums, previous_v, square_v)
     return (gradient, direction)

time: 64.4 us -> 61 us (0.947)
  blocking collectives: 18.7 us -> 30.9 us
  waiting for transfers between devices: 13.1 us -> 5.14 us
  starting transfers between devices: 22.5 us -> 16.1 us
  local copies, waits for them, and re-layouts: 0.7 us -> 0.01 us
    all_to_all x0 -> x1, blocking collectives: none -> 12.3 us  [local(): lax.all_to_all(partial, ('lat', 'lon', 'lev'), split_axis=0, concat_axis=...]
    all_to_all x1 -> x0, waiting for transfers between devices: 5.64 us -> none  [local(): lax.all_to_all(partial, ('lat', 'lon', 'lev'), split_axis=0, concat_axis=...]
    all_to_all x1 -> x0, starting transfers between devices: 5.42 us -> none  [local(): lax.all_to_all(partial, ('lat', 'lon', 'lev'), split_axis=0, concat_axis=...]
    ppermute x10, waiting for transfers between devices: 5.94 us -> 3.66 us  [exchange(): return lax.ppermute(field, ('lat', 'lon'), pairs)]
    ppermute x10, starting transfers between devices: 16.5 us -> 15.5 us  [exchange(): return lax.ppermute(field, ('lat', 'lon'), pairs)]
    unnamed x5 -> x4, local copies, waits for them, and re-layouts: 0.7 us -> 0.01 us
  transfers between devices with their start and end apart: 13 -> 12, of which waited for: 5 -> 4; matrix products, arithmetic and copies ran while one was open for 1% -> 0% of each run, Pallas kernels for 3% -> 3%
where the time goes in v5:
time: 61 us; the launch traced here: 60.8 us
  blocking collectives  30.9 us (51%)
  starting transfers between devices  16.1 us (26%)
  Pallas kernels  7.17 us (12%)
  waiting for transfers between devices  5.14 us (8%)
  between operations  1.43 us (2%)
    ppermute x10, starting transfers between devices, exchange(): return lax.ppermute(field, ('lat', 'lon'), pairs)  15.5 us
    all_to_all x1, blocking collectives, local(): lax.all_to_all(partial, ('lat', 'lon', 'lev'), split_axis=0, concat_axis=...  12.3 us
    all_to_all x1, blocking collectives, local(): lax.all_to_all(sent, ('lat', 'lon'), split_axis=0, concat_axis=0, tiled=T...  9.6 us
    all_to_all x1, blocking collectives, local(): lax.all_to_all(result, ('lat', 'lon'), split_axis=0, concat_axis=0, tiled...  9.07 us
    ppermute x10, waiting for transfers between devices, exchange(): return lax.ppermute(field, ('lat', 'lon'), pairs)  3.66 us
    pallas_call x1, Pallas kernels, local(): call(forward_kernel, [held(owners, 2 * half, width)] + [ext] * 5, [VMEM]...  2.33 us
    pallas_call x1, Pallas kernels, local(): call(load_kernel, [mix, mix] + [field] * 6 + [held(count, width)] + [held...  1.57 us
    ppermute x2, waiting for transfers between devices, from_levs(): lax.ppermute(field, 'lev', [(i, (i + k) % n_lev) for i in range(n_lev)])  1.48 us
  transfers between devices with their start and end apart: 12, of which 4 were waited for; matrix products, arithmetic and copies ran while one was open for 0% of the time, Pallas kernels for 3%

profile of v5, /device:TPU:0, one launch (start us, length us, event | category | flops | bytes accessed | tf_op | source)
XLA Modules:
  0.0 60.8 jit_solution(3326962323006315356)
XLA Ops:
  0.6 0.5 collective-permute-start
  1.2 1.6 %shard_map.149 = (f32[8,128]{1,0:T(8,128)S(1)}, f32[8,128]{1,0:T(8,128)S(1)}, f32[2,56,512]{2,1,0:T(8,128)S(1)}, f32[2,56,512]{2,1,0:T(8,128)S(1)}, f32[2,56,512...) custom-call(f32[4,4]{1,0:T(4,128)} %vertical.1, ...), custom_call_target="tpu_custom_call" | custom-call | flops 1048576 | bytes 1048576 | tf_op jit(solution)/shard_map/pallas_call | solution.py:528
  2.9 2.7 %collective-permute-start.2 = (f32[40,512]{1,0:T(8,128)S(1)}, f32[40,512]{1,0:T(8,128)S(1)}, u32[]{:S(2)}, u32[]{:S(2)}) collective-permute-start(f32[40,512]{1,0:T(8,128)S(1)} %get-tuple-element.43), channel_id=1, source_target_pairs={{0,4},{2,6},{4,0},{6,2},{8,12},{10,14},{12,8},{14,10},{1,5},{3,7},... | collective-permute-start | bytes 245768 | tf_op jit(solution)/shard_map/ppermute | solution.py:514
  5.7 0.7 %collective-permute-start.4 = (f32[40,512]{1,0:T(8,128)S(1)}, f32[40,512]{1,0:T(8,128)S(1)}, u32[]{:S(2)}, u32[]{:S(2)}) collective-permute-start(f32[40,512]{1,0:T(8,128)S(1)} %get-tuple-element.45), channel_id=1, source_target_pairs={{0,0},{2,2},{4,8},{6,10},{8,4},{10,6},{12,12},{14,14},{1,1},{3,3},... | collective-permute-start | bytes 245768 | tf_op jit(solution)/shard_map/ppermute | solution.py:514
  6.3 1.6 %collective-permute-start.1 = (f32[64,128]{1,0:T(8,128)S(1)}, f32[64,128]{1,0:T(8,128)S(1)}, u32[]{:S(2)}, u32[]{:S(2)}) collective-permute-start(f32[64,128]{1,0:T(8,128)S(1)} %get-tuple-element.42.refs_0_), channel_id=1, source_target_pairs={{0,2},{2,0},{4,6},{6,4},{8,10},{10,8},{12,14},{14,12},{1,3},{3,1},... | collective-permute-start | bytes 98312 | tf_op jit(solution)/shard_map/ppermute | solution.py:514
  7.9 4.4 %collective-permute-start.3 = (f32[40,128]{1,0:T(8,128)S(1)}, f32[40,128]{1,0:T(8,128)S(1)}, u32[]{:S(2)}, u32[]{:S(2)}) collective-permute-start(f32[40,128]{1,0:T(8,128)S(1)} %get-tuple-element.44), channel_id=1, source_target_pairs={{0,6},{2,4},{4,2},{6,0},{8,14},{10,12},{12,10},{14,8},{1,7},{3,5},... | collective-permute-start | bytes 61448 | tf_op jit(solution)/shard_map/ppermute | solution.py:514
  12.2 1.5 %collective-permute-start.5 = (f32[40,128]{1,0:T(8,128)S(1)}, f32[40,128]{1,0:T(8,128)S(1)}, u32[]{:S(2)}, u32[]{:S(2)}) collective-permute-start(f32[40,128]{1,0:T(8,128)S(1)} %get-tuple-element.46), channel_id=1, source_target_pairs={{0,2},{2,0},{4,10},{6,8},{8,6},{10,4},{12,14},{14,12},{1,3},{3,1},... | collective-permute-start | bytes 61448 | tf_op jit(solution)/shard_map/ppermute | solution.py:514
  14.6 1.4 %collective-permute-done.5.refs_5_.diag_2 = f32[40,128]{1,0:T(8,128)S(1)} collective-permute-done((f32[40,128]{1,0:T(8,128)S(1)}, f32[40,128]{1,0:T(8,128)S(1)}, u32[]{:S(2)}, u32[]{:S(2)}) %collective-permute-start.5) | collective-permute-done | bytes 20512 | tf_op jit(solution)/shard_map/ppermute | solution.py:514
  16.0 2.3 %shard_map.154 = (f32[8,8,128]{2,1,0:T(8,128)S(1)}, f32[2,64,640]{2,1,0:T(8,128)S(1)}, f32[2,64,640]{2,1,0:T(8,128)S(1)}, f32[2,64,640]{2,1,0:T(8,128)S(1)}, f32...) custom-call(s32[1,128]{1,0:T(1,128)S(1)} %get-tuple-element.47.place, ...), custom_call_target="tpu_custom_call", output_to_operand_aliasing={{1}: (3, {}), {2}: (4, {}), {3}: (5, {}), {4}: (6, {}), {5}... | custom-call | flops 1048576 | bytes 1048576 | tf_op jit(solution)/shard_map/pallas_call | solution.py:575
  18.4 9.6 %all_to_all.15.arrived = f32[8,8,128]{2,1,0:T(8,128)S(1)} all-to-all(f32[8,8,128]{2,1,0:T(8,128)S(1)} %get-tuple-element.61), channel_id=1, replica_groups=mesh['member'=2,'lat'=4,'lon'=2,'lev'=2] {'lat','lon'}, dimensions={0} | all-to-all | bytes 65536 | tf_op jit(solution)/shard_map/all_to_all | solution.py:592
  28.0 0.3 shard_map.155
  28.2 9.1 %all_to_all.16.returned = f32[8,8,128]{2,1,0:T(8,128)S(1)} all-to-all(f32[8,8,128]{2,1,0:T(8,128)S(1)} %shard_map.155), channel_id=1, replica_groups=mesh['member'=2,'lat'=4,'lon'=2,'lev'=2] {'lat','lon'}, dimensions={0} | all-to-all | bytes 65536 | tf_op jit(solution)/shard_map/all_to_all | solution.py:599
  37.3 0.3 shard_map.156.refs_1_
  37.6 0.5 collective-permute-start.10
  38.1 1.5 %collective-permute-start.6 = (f32[16,128]{1,0:T(8,128)S(1)}, f32[16,128]{1,0:T(8,128)S(1)}, u32[]{:S(2)}, u32[]{:S(2)}) collective-permute-start(f32[16,128]{1,0:T(8,128)S(1)} %shard_map.156.refs_1_), channel_id=1, source_target_pairs={{0,2},{2,0},{4,6},{6,4},{8,10},{10,8},{12,14},{14,12},{1,3},{3,1},... | collective-permute-start | bytes 24584 | tf_op jit(solution)/shard_map/ppermute | solution.py:514
  39.7 0.5 collective-permute-start.7
  40.2 1.4 %collective-permute-start.8 = (f32[16,128]{1,0:T(8,128)S(1)}, f32[16,128]{1,0:T(8,128)S(1)}, u32[]{:S(2)}, u32[]{:S(2)}) collective-permute-start(f32[16,128]{1,0:T(8,128)S(1)} %shard_map.156.refs_1_), channel_id=1, source_target_pairs={{0,6},{2,4},{4,2},{6,0},{8,14},{10,12},{12,10},{14,8},{1,7},{3,5},... | collective-permute-start | bytes 24584 | tf_op jit(solution)/shard_map/ppermute | solution.py:514
  41.6 0.6 %collective-permute-start.9 = (f32[16,128]{1,0:T(8,128)S(1)}, f32[16,128]{1,0:T(8,128)S(1)}, u32[]{:S(2)}, u32[]{:S(2)}) collective-permute-start(f32[16,128]{1,0:T(8,128)S(1)} %shard_map.156.refs_1_), channel_id=1, source_target_pairs={{0,0},{2,2},{4,8},{6,10},{8,4},{10,6},{12,12},{14,14},{1,1},{3,3},... | collective-permute-start | bytes 24584 | tf_op jit(solution)/shard_map/ppermute | solution.py:514
  42.5 0.8 %collective-permute-done.7.refs_3_ = f32[16,128]{1,0:T(8,128)S(1)} collective-permute-done((f32[16,128]{1,0:T(8,128)S(1)}, f32[16,128]{1,0:T(8,128)S(1)}, u32[]{:S(2)}, u32[]{:S(2)}) %collective-permute-start.7) | collective-permute-done | bytes 8224 | tf_op jit(solution)/shard_map/ppermute | solution.py:514
  43.3 1.4 %collective-permute-done.8.refs_4_ = f32[16,128]{1,0:T(8,128)S(1)} collective-permute-done((f32[16,128]{1,0:T(8,128)S(1)}, f32[16,128]{1,0:T(8,128)S(1)}, u32[]{:S(2)}, u32[]{:S(2)}) %collective-permute-start.8) | collective-permute-done | bytes 8224 | tf_op jit(solution)/shard_map/ppermute | solution.py:514
  44.8 1.2 %shard_map.157.refs_2_ = f32[2,56,512]{2,1,0:T(8,128)S(1)} custom-call(bf16[768,256]{1,0:T(8,128)(2,1)S(1)} %shard_map.151.refs_0_, f32[16,128]{1,0:T(8,128)S(1)} %shard_map.156.refs_1_, f32[16,128]{1,0:T(8,128)S(1)} %collective-permute-done.6.refs_2_, f32[16,128]{1,0:T(8,128)S(1)} %collective-permute-done.7.refs_3_, ...), custom_call_target="tpu_custom_call" | custom-call | flops 1048576 | bytes 1048576 | tf_op jit(solution)/shard_map/pallas_call | solution.py:625
  46.0 1.5 %collective-permute-done.11.refs_3_ = f32[2,56,512]{2,1,0:T(8,128)S(1)} collective-permute-done((f32[2,56,512]{2,1,0:T(8,128)S(1)}, f32[2,56,512]{2,1,0:T(8,128)S(1)}, u32[]{:S(2)}, u32[]{:S(2)}) %collective-permute-start.11) | collective-permute-done | bytes 229408 | tf_op jit(solution)/shard_map/ppermute | solution.py:501
  47.7 12.3 %all_to_all.17.sums = f32[16,1,128]{2,1,0:T(1,128)S(1)} all-to-all(f32[16,1,128]{2,1,0:T(1,128)S(1)} %get-tuple-element.67), channel_id=1, replica_groups=mesh['member'=2,'lat'=4,'lon'=2,'lev'=2] {'lat','lon','lev'}, dimensions={0} | all-to-all | bytes 16384 | tf_op jit(solution)/shard_map/all_to_all | solution.py:640
  59.9 0.8 %shard_map.159 = (f32[2,56,512]{2,1,0:T(8,128)}, f32[2,56,512]{2,1,0:T(8,128)}) custom-call(f32[2,56,512]{2,1,0:T(8,128)S(1)} %get-tuple-element.66.gradient_in, f32[16,1,128]{2,1,0:T(1,128)S(1)} %all_to_all.17.sums, f32[2,56,512]{2,1,0:T(8,128)S(1)} %get-tuple-element.68.previous, f32[1,128]{1,0:T(1,128)S(1)} %get-tuple-element.69.previous_square), custom_call_target="tpu_custom_call" | custom-call | flops 1048576 | bytes 1048576 | tf_op jit(solution)/shard_map/pallas_call | solution.py:641
  (18 shorter events, 0.8 us)
Async XLA Ops:
  0.6 13.7 %copy-start = (f32[1,1,1,8,2,128,128]{6,5,4,3,2,1,0:T(8,128)S(1)}, f32[1,1,1,8,2,128,128]{6,5,4,3,2,1,0:T(8,128)}, u32[]{:S(2)}) copy-start(f32[1,1,1,8,2,128,128]{6,5,4,3,2,1,0:T(8,128)} %param.23) | copy-start | bytes 3145732
  0.6 2.1 %collective-permute-start = (f32[2,56,512]{2,1,0:T(8,128)}, f32[2,56,512]{2,1,0:T(8,128)S(1)}, u32[]{:S(2)}, u32[]{:S(2)}) collective-permute-start(f32[2,56,512]{2,1,0:T(8,128)} %control.1), channel_id=1, source_target_pairs={{0,1},{1,0},{2,3},{3,2},{4,5},{5,4},{6,7},{7,6},{8,9},{9,8},{10,11... | collective-permute-start | bytes 688136 | tf_op jit(solution)/shard_map/ppermute | solution.py:501
  2.9 13.1 %collective-permute-start.2 = (f32[40,512]{1,0:T(8,128)S(1)}, f32[40,512]{1,0:T(8,128)S(1)}, u32[]{:S(2)}, u32[]{:S(2)}) collective-permute-start(f32[40,512]{1,0:T(8,128)S(1)} %get-tuple-element.43), channel_id=1, source_target_pairs={{0,4},{2,6},{4,0},{6,2},{8,12},{10,14},{12,8},{14,10},{1,5},{3,7},... | collective-permute-start | bytes 245768 | tf_op jit(solution)/shard_map/ppermute | solution.py:514
  5.7 10.4 %collective-permute-start.4 = (f32[40,512]{1,0:T(8,128)S(1)}, f32[40,512]{1,0:T(8,128)S(1)}, u32[]{:S(2)}, u32[]{:S(2)}) collective-permute-start(f32[40,512]{1,0:T(8,128)S(1)} %get-tuple-element.45), channel_id=1, source_target_pairs={{0,0},{2,2},{4,8},{6,10},{8,4},{10,6},{12,12},{14,14},{1,1},{3,3},... | collective-permute-start | bytes 245768 | tf_op jit(solution)/shard_map/ppermute | solution.py:514
  6.3 9.7 %collective-permute-start.1 = (f32[64,128]{1,0:T(8,128)S(1)}, f32[64,128]{1,0:T(8,128)S(1)}, u32[]{:S(2)}, u32[]{:S(2)}) collective-permute-start(f32[64,128]{1,0:T(8,128)S(1)} %get-tuple-element.42.refs_0_), channel_id=1, source_target_pairs={{0,2},{2,0},{4,6},{6,4},{8,10},{10,8},{12,14},{14,12},{1,3},{3,1},... | collective-permute-start | bytes 98312 | tf_op jit(solution)/shard_map/ppermute | solution.py:514
  7.9 6.7 %collective-permute-start.3 = (f32[40,128]{1,0:T(8,128)S(1)}, f32[40,128]{1,0:T(8,128)S(1)}, u32[]{:S(2)}, u32[]{:S(2)}) collective-permute-start(f32[40,128]{1,0:T(8,128)S(1)} %get-tuple-element.44), channel_id=1, source_target_pairs={{0,6},{2,4},{4,2},{6,0},{8,14},{10,12},{12,10},{14,8},{1,7},{3,5},... | collective-permute-start | bytes 61448 | tf_op jit(solution)/shard_map/ppermute | solution.py:514
  12.2 3.8 %collective-permute-start.5 = (f32[40,128]{1,0:T(8,128)S(1)}, f32[40,128]{1,0:T(8,128)S(1)}, u32[]{:S(2)}, u32[]{:S(2)}) collective-permute-start(f32[40,128]{1,0:T(8,128)S(1)} %get-tuple-element.46), channel_id=1, source_target_pairs={{0,2},{2,0},{4,10},{6,8},{8,6},{10,4},{12,14},{14,12},{1,3},{3,1},... | collective-permute-start | bytes 61448 | tf_op jit(solution)/shard_map/ppermute | solution.py:514
  16.0 11.9 %copy-start.1 = (f32[1,1,8,128,128]{4,3,2,1,0:T(8,128)S(1)}, f32[1,1,8,128,128]{4,3,2,1,0:T(8,128)}, u32[]{:S(2)}) copy-start(f32[1,1,8,128,128]{4,3,2,1,0:T(8,128)} %param.25) | copy-start | bytes 1572868
  37.6 4.9 %collective-permute-start.10 = (f32[16,128]{1,0:T(8,128)S(1)}, f32[16,128]{1,0:T(8,128)S(1)}, u32[]{:S(2)}, u32[]{:S(2)}) collective-permute-start(f32[16,128]{1,0:T(8,128)S(1)} %shard_map.156.refs_1_), channel_id=1, source_target_pairs={{0,2},{2,0},{4,10},{6,8},{8,6},{10,4},{12,14},{14,12},{1,3},{3,1},... | collective-permute-start | bytes 24584 | tf_op jit(solution)/shard_map/ppermute | solution.py:514
  38.1 4.4 %collective-permute-start.6 = (f32[16,128]{1,0:T(8,128)S(1)}, f32[16,128]{1,0:T(8,128)S(1)}, u32[]{:S(2)}, u32[]{:S(2)}) collective-permute-start(f32[16,128]{1,0:T(8,128)S(1)} %shard_map.156.refs_1_), channel_id=1, source_target_pairs={{0,2},{2,0},{4,6},{6,4},{8,10},{10,8},{12,14},{14,12},{1,3},{3,1},... | collective-permute-start | bytes 24584 | tf_op jit(solution)/shard_map/ppermute | solution.py:514
  39.7 3.7 %collective-permute-start.7 = (f32[16,128]{1,0:T(8,128)S(1)}, f32[16,128]{1,0:T(8,128)S(1)}, u32[]{:S(2)}, u32[]{:S(2)}) collective-permute-start(f32[16,128]{1,0:T(8,128)S(1)} %shard_map.156.refs_1_), channel_id=1, source_target_pairs={{0,4},{2,6},{4,0},{6,2},{8,12},{10,14},{12,8},{14,10},{1,5},{3,7},... | collective-permute-start | bytes 24584 | tf_op jit(solution)/shard_map/ppermute | solution.py:514
  40.2 4.5 %collective-permute-start.8 = (f32[16,128]{1,0:T(8,128)S(1)}, f32[16,128]{1,0:T(8,128)S(1)}, u32[]{:S(2)}, u32[]{:S(2)}) collective-permute-start(f32[16,128]{1,0:T(8,128)S(1)} %shard_map.156.refs_1_), channel_id=1, source_target_pairs={{0,6},{2,4},{4,2},{6,0},{8,14},{10,12},{12,10},{14,8},{1,7},{3,5},... | collective-permute-start | bytes 24584 | tf_op jit(solution)/shard_map/ppermute | solution.py:514
  41.6 3.1 %collective-permute-start.9 = (f32[16,128]{1,0:T(8,128)S(1)}, f32[16,128]{1,0:T(8,128)S(1)}, u32[]{:S(2)}, u32[]{:S(2)}) collective-permute-start(f32[16,128]{1,0:T(8,128)S(1)} %shard_map.156.refs_1_), channel_id=1, source_target_pairs={{0,0},{2,2},{4,8},{6,10},{8,4},{10,6},{12,12},{14,14},{1,1},{3,3},... | collective-permute-start | bytes 24584 | tf_op jit(solution)/shard_map/ppermute | solution.py:514
  45.9 1.6 %collective-permute-start.11 = (f32[2,56,512]{2,1,0:T(8,128)S(1)}, f32[2,56,512]{2,1,0:T(8,128)S(1)}, u32[]{:S(2)}, u32[]{:S(2)}) collective-permute-start(f32[2,56,512]{2,1,0:T(8,128)S(1)} %shard_map.157.refs_2_), channel_id=1, source_target_pairs={{0,1},{1,0},{2,3},{3,2},{4,5},{5,4},{6,7},{7,6},{8,9},{9,8},{10,11... | collective-permute-start | bytes 688136 | tf_op jit(solution)/shard_map/ppermute | solution.py:501

commit v6 on v5

--- a/solution.py
+++ b/solution.py
@@ -606,12 +606,12 @@
         sources.append(from_lon(adjoint_obs, 0, step))
         tiles.append(lon_raw[step])
         kinds.append((0, step, rows))
+    row_of_tiles = jnp.concatenate(sources, axis=0)
     for phase in (1, 2):
-        sources.append(exchange(adjoint_obs, phase, 0))
+        sources.append(exchange(row_of_tiles, phase, 0))
         tiles.append(lat_in[phase])
         kinds.append((phase, 0, lat_fields))
         for step in lon_steps:
-            sources.append(from_lon(adjoint_obs, phase, step))
             tiles.append(diag_raw[phase, step])
             kinds.append((phase, step, lat_fields))
     depth = -(-len(kinds) * count // LANES) * LANES

time: 61 us -> 60.6 us (level)
  waiting for transfers between devices: 5.14 us -> 8.55 us
  starting transfers between devices: 16.1 us -> 13 us
  blocking collectives: 30.9 us -> 30.2 us
    ppermute x10 -> x8, waiting for transfers between devices: 3.66 us -> 7.07 us  [exchange(): return lax.ppermute(field, ('lat', 'lon'), pairs)]
    ppermute x10 -> x8, starting transfers between devices: 15.5 us -> 12.4 us  [exchange(): return lax.ppermute(field, ('lat', 'lon'), pairs)]
    all_to_all x1, blocking collectives: 12.3 us -> 11.5 us  [local(): lax.all_to_all(partial, ('lat', 'lon', 'lev'), split_axis=0, concat_axis=...]
  transfers between devices with their start and end apart: 12 -> 10, of which waited for: 4 -> 4; matrix products, arithmetic and copies ran while one was open for 0% -> 0% of each run, Pallas kernels for 3% -> 3%
where the time goes in v6:
time: 60.6 us; the launch traced here: 60.3 us
  blocking collectives  30.2 us (50%)
  starting transfers between devices  13 us (21%)
  waiting for transfers between devices  8.55 us (14%)
  Pallas kernels  7.17 us (12%)
  between operations  1.41 us (2%)
    ppermute x8, starting transfers between devices, exchange(): return lax.ppermute(field, ('lat', 'lon'), pairs)  12.4 us
    all_to_all x1, blocking collectives, local(): lax.all_to_all(partial, ('lat', 'lon', 'lev'), split_axis=0, concat_axis=...  11.5 us
    all_to_all x1, blocking collectives, local(): lax.all_to_all(sent, ('lat', 'lon'), split_axis=0, concat_axis=0, tiled=T...  9.6 us
    all_to_all x1, blocking collectives, local(): lax.all_to_all(result, ('lat', 'lon'), split_axis=0, concat_axis=0, tiled...  9.07 us
    ppermute x8, waiting for transfers between devices, exchange(): return lax.ppermute(field, ('lat', 'lon'), pairs)  7.07 us
    pallas_call x1, Pallas kernels, local(): call(forward_kernel, [held(owners, 2 * half, width)] + [ext] * 5, [VMEM]...  2.33 us
    pallas_call x1, Pallas kernels, local(): call(load_kernel, [mix, mix] + [field] * 6 + [held(count, width)] + [held...  1.57 us
    ppermute x2, waiting for transfers between devices, from_levs(): lax.ppermute(field, 'lev', [(i, (i + k) % n_lev) for i in range(n_lev)])  1.48 us
  transfers between devices with their start and end apart: 10, of which 4 were waited for; matrix products, arithmetic and copies ran while one was open for 0% of the time, Pallas kernels for 3%

profile of v6, /device:TPU:0, one launch (start us, length us, event | category | flops | bytes accessed | tf_op | source)
XLA Modules:
  0.0 60.3 jit_solution(1335833753866989508)
XLA Ops:
  0.6 0.5 collective-permute-start
  1.2 1.6 %shard_map.149 = (f32[8,128]{1,0:T(8,128)S(1)}, f32[8,128]{1,0:T(8,128)S(1)}, f32[2,56,512]{2,1,0:T(8,128)S(1)}, f32[2,56,512]{2,1,0:T(8,128)S(1)}, f32[2,56,512...) custom-call(f32[4,4]{1,0:T(4,128)} %vertical.1, ...), custom_call_target="tpu_custom_call" | custom-call | flops 1048576 | bytes 1048576 | tf_op jit(solution)/shard_map/pallas_call | solution.py:528
  2.9 2.7 %collective-permute-start.2 = (f32[40,512]{1,0:T(8,128)S(1)}, f32[40,512]{1,0:T(8,128)S(1)}, u32[]{:S(2)}, u32[]{:S(2)}) collective-permute-start(f32[40,512]{1,0:T(8,128)S(1)} %get-tuple-element.43), channel_id=1, source_target_pairs={{0,4},{2,6},{4,0},{6,2},{8,12},{10,14},{12,8},{14,10},{1,5},{3,7},... | collective-permute-start | bytes 245768 | tf_op jit(solution)/shard_map/ppermute | solution.py:514
  5.7 0.7 %collective-permute-start.4 = (f32[40,512]{1,0:T(8,128)S(1)}, f32[40,512]{1,0:T(8,128)S(1)}, u32[]{:S(2)}, u32[]{:S(2)}) collective-permute-start(f32[40,512]{1,0:T(8,128)S(1)} %get-tuple-element.45), channel_id=1, source_target_pairs={{0,0},{2,2},{4,8},{6,10},{8,4},{10,6},{12,12},{14,14},{1,1},{3,3},... | collective-permute-start | bytes 245768 | tf_op jit(solution)/shard_map/ppermute | solution.py:514
  6.3 1.6 %collective-permute-start.1 = (f32[64,128]{1,0:T(8,128)S(1)}, f32[64,128]{1,0:T(8,128)S(1)}, u32[]{:S(2)}, u32[]{:S(2)}) collective-permute-start(f32[64,128]{1,0:T(8,128)S(1)} %get-tuple-element.42.refs_0_), channel_id=1, source_target_pairs={{0,2},{2,0},{4,6},{6,4},{8,10},{10,8},{12,14},{14,12},{1,3},{3,1},... | collective-permute-start | bytes 98312 | tf_op jit(solution)/shard_map/ppermute | solution.py:514
  7.9 4.4 %collective-permute-start.3 = (f32[40,128]{1,0:T(8,128)S(1)}, f32[40,128]{1,0:T(8,128)S(1)}, u32[]{:S(2)}, u32[]{:S(2)}) collective-permute-start(f32[40,128]{1,0:T(8,128)S(1)} %get-tuple-element.44), channel_id=1, source_target_pairs={{0,6},{2,4},{4,2},{6,0},{8,14},{10,12},{12,10},{14,8},{1,7},{3,5},... | collective-permute-start | bytes 61448 | tf_op jit(solution)/shard_map/ppermute | solution.py:514
  12.2 1.5 %collective-permute-start.5 = (f32[40,128]{1,0:T(8,128)S(1)}, f32[40,128]{1,0:T(8,128)S(1)}, u32[]{:S(2)}, u32[]{:S(2)}) collective-permute-start(f32[40,128]{1,0:T(8,128)S(1)} %get-tuple-element.46), channel_id=1, source_target_pairs={{0,2},{2,0},{4,10},{6,8},{8,6},{10,4},{12,14},{14,12},{1,3},{3,1},... | collective-permute-start | bytes 61448 | tf_op jit(solution)/shard_map/ppermute | solution.py:514
  14.6 1.4 %collective-permute-done.5.refs_5_.diag_2 = f32[40,128]{1,0:T(8,128)S(1)} collective-permute-done((f32[40,128]{1,0:T(8,128)S(1)}, f32[40,128]{1,0:T(8,128)S(1)}, u32[]{:S(2)}, u32[]{:S(2)}) %collective-permute-start.5) | collective-permute-done | bytes 20512 | tf_op jit(solution)/shard_map/ppermute | solution.py:514
  16.0 2.3 %shard_map.154 = (f32[8,8,128]{2,1,0:T(8,128)S(1)}, f32[2,64,640]{2,1,0:T(8,128)S(1)}, f32[2,64,640]{2,1,0:T(8,128)S(1)}, f32[2,64,640]{2,1,0:T(8,128)S(1)}, f32...) custom-call(s32[1,128]{1,0:T(1,128)S(1)} %get-tuple-element.47.place, ...), custom_call_target="tpu_custom_call", output_to_operand_aliasing={{1}: (3, {}), {2}: (4, {}), {3}: (5, {}), {4}: (6, {}), {5}... | custom-call | flops 1048576 | bytes 1048576 | tf_op jit(solution)/shard_map/pallas_call | solution.py:575
  18.4 9.6 %all_to_all.15.arrived = f32[8,8,128]{2,1,0:T(8,128)S(1)} all-to-all(f32[8,8,128]{2,1,0:T(8,128)S(1)} %get-tuple-element.61), channel_id=1, replica_groups=mesh['member'=2,'lat'=4,'lon'=2,'lev'=2] {'lat','lon'}, dimensions={0} | all-to-all | bytes 65536 | tf_op jit(solution)/shard_map/all_to_all | solution.py:592
  28.0 0.3 shard_map.155
  28.2 9.1 %all_to_all.16.returned = f32[8,8,128]{2,1,0:T(8,128)S(1)} all-to-all(f32[8,8,128]{2,1,0:T(8,128)S(1)} %shard_map.155), channel_id=1, replica_groups=mesh['member'=2,'lat'=4,'lon'=2,'lev'=2] {'lat','lon'}, dimensions={0} | all-to-all | bytes 65536 | tf_op jit(solution)/shard_map/all_to_all | solution.py:599
  37.3 0.3 shard_map.156.refs_1_
  37.6 0.5 collective-permute-start.6
  38.1 3.2 %collective-permute-done.6.refs_2_ = f32[16,128]{1,0:T(8,128)S(1)} collective-permute-done((f32[16,128]{1,0:T(8,128)S(1)}, f32[16,128]{1,0:T(8,128)S(1)}, u32[]{:S(2)}, u32[]{:S(2)}) %collective-permute-start.6) | collective-permute-done | bytes 8224 | tf_op jit(solution)/shard_map/ppermute | solution.py:514
  41.3 0.4 collective-permute-start.7
  41.7 0.7 %collective-permute-start.8 = (f32[32,128]{1,0:T(8,128)S(1)}, f32[32,128]{1,0:T(8,128)S(1)}, u32[]{:S(2)}, u32[]{:S(2)}) collective-permute-start(f32[32,128]{1,0:T(8,128)S(1)} %pad_maximum_fusion), channel_id=1, source_target_pairs={{0,0},{2,2},{4,8},{6,10},{8,4},{10,6},{12,12},{14,14},{1,1},{3,3},... | collective-permute-start | bytes 49160 | tf_op jit(solution)/shard_map/ppermute | solution.py:514
  42.4 0.2 shard_map.151.refs_0_
  42.6 2.5 %collective-permute-done.7.refs_3_ = f32[32,128]{1,0:T(8,128)S(1)} collective-permute-done((f32[32,128]{1,0:T(8,128)S(1)}, f32[32,128]{1,0:T(8,128)S(1)}, u32[]{:S(2)}, u32[]{:S(2)}) %collective-permute-start.7) | collective-permute-done | bytes 16416 | tf_op jit(solution)/shard_map/ppermute | solution.py:514
  45.0 1.2 %shard_map.157.refs_2_ = f32[2,56,512]{2,1,0:T(8,128)S(1)} custom-call(bf16[768,256]{1,0:T(8,128)(2,1)S(1)} %shard_map.151.refs_0_, f32[16,128]{1,0:T(8,128)S(1)} %shard_map.156.refs_1_, f32[16,128]{1,0:T(8,128)S(1)} %collective-permute-done.6.refs_2_, f32[32,128]{1,0:T(8,128)S(1)} %collective-permute-done.7.refs_3_, ...), custom_call_target="tpu_custom_call" | custom-call | flops 1048576 | bytes 1048576 | tf_op jit(solution)/shard_map/pallas_call | solution.py:625
  46.3 1.5 %collective-permute-done.9.refs_3_ = f32[2,56,512]{2,1,0:T(8,128)S(1)} collective-permute-done((f32[2,56,512]{2,1,0:T(8,128)S(1)}, f32[2,56,512]{2,1,0:T(8,128)S(1)}, u32[]{:S(2)}, u32[]{:S(2)}) %collective-permute-start.9) | collective-permute-done | bytes 229408 | tf_op jit(solution)/shard_map/ppermute | solution.py:501
  47.8 0.2 shard_map.158
  47.9 11.5 %all_to_all.17.sums = f32[16,1,128]{2,1,0:T(1,128)S(1)} all-to-all(f32[16,1,128]{2,1,0:T(1,128)S(1)} %get-tuple-element.67), channel_id=1, replica_groups=mesh['member'=2,'lat'=4,'lon'=2,'lev'=2] {'lat','lon','lev'}, dimensions={0} | all-to-all | bytes 16384 | tf_op jit(solution)/shard_map/all_to_all | solution.py:640
  59.4 0.8 %shard_map.159 = (f32[2,56,512]{2,1,0:T(8,128)}, f32[2,56,512]{2,1,0:T(8,128)}) custom-call(f32[2,56,512]{2,1,0:T(8,128)S(1)} %get-tuple-element.66.gradient_in, f32[16,1,128]{2,1,0:T(1,128)S(1)} %all_to_all.17.sums, f32[2,56,512]{2,1,0:T(8,128)S(1)} %get-tuple-element.68.previous, f32[1,128]{1,0:T(1,128)S(1)} %get-tuple-element.69.previous_square), custom_call_target="tpu_custom_call" | custom-call | flops 1048576 | bytes 1048576 | tf_op jit(solution)/shard_map/pallas_call | solution.py:641
  (15 shorter events, 0.5 us)
Async XLA Ops:
  0.6 13.7 %copy-start = (f32[1,1,1,8,2,128,128]{6,5,4,3,2,1,0:T(8,128)S(1)}, f32[1,1,1,8,2,128,128]{6,5,4,3,2,1,0:T(8,128)}, u32[]{:S(2)}) copy-start(f32[1,1,1,8,2,128,128]{6,5,4,3,2,1,0:T(8,128)} %param.23) | copy-start | bytes 3145732
  0.6 2.1 %collective-permute-start = (f32[2,56,512]{2,1,0:T(8,128)}, f32[2,56,512]{2,1,0:T(8,128)S(1)}, u32[]{:S(2)}, u32[]{:S(2)}) collective-permute-start(f32[2,56,512]{2,1,0:T(8,128)} %control.1), channel_id=1, source_target_pairs={{0,1},{1,0},{2,3},{3,2},{4,5},{5,4},{6,7},{7,6},{8,9},{9,8},{10,11... | collective-permute-start | bytes 688136 | tf_op jit(solution)/shard_map/ppermute | solution.py:501
  2.9 13.1 %collective-permute-start.2 = (f32[40,512]{1,0:T(8,128)S(1)}, f32[40,512]{1,0:T(8,128)S(1)}, u32[]{:S(2)}, u32[]{:S(2)}) collective-permute-start(f32[40,512]{1,0:T(8,128)S(1)} %get-tuple-element.43), channel_id=1, source_target_pairs={{0,4},{2,6},{4,0},{6,2},{8,12},{10,14},{12,8},{14,10},{1,5},{3,7},... | collective-permute-start | bytes 245768 | tf_op jit(solution)/shard_map/ppermute | solution.py:514
  5.7 10.4 %collective-permute-start.4 = (f32[40,512]{1,0:T(8,128)S(1)}, f32[40,512]{1,0:T(8,128)S(1)}, u32[]{:S(2)}, u32[]{:S(2)}) collective-permute-start(f32[40,512]{1,0:T(8,128)S(1)} %get-tuple-element.45), channel_id=1, source_target_pairs={{0,0},{2,2},{4,8},{6,10},{8,4},{10,6},{12,12},{14,14},{1,1},{3,3},... | collective-permute-start | bytes 245768 | tf_op jit(solution)/shard_map/ppermute | solution.py:514
  6.3 9.7 %collective-permute-start.1 = (f32[64,128]{1,0:T(8,128)S(1)}, f32[64,128]{1,0:T(8,128)S(1)}, u32[]{:S(2)}, u32[]{:S(2)}) collective-permute-start(f32[64,128]{1,0:T(8,128)S(1)} %get-tuple-element.42.refs_0_), channel_id=1, source_target_pairs={{0,2},{2,0},{4,6},{6,4},{8,10},{10,8},{12,14},{14,12},{1,3},{3,1},... | collective-permute-start | bytes 98312 | tf_op jit(solution)/shard_map/ppermute | solution.py:514
  7.9 6.7 %collective-permute-start.3 = (f32[40,128]{1,0:T(8,128)S(1)}, f32[40,128]{1,0:T(8,128)S(1)}, u32[]{:S(2)}, u32[]{:S(2)}) collective-permute-start(f32[40,128]{1,0:T(8,128)S(1)} %get-tuple-element.44), channel_id=1, source_target_pairs={{0,6},{2,4},{4,2},{6,0},{8,14},{10,12},{12,10},{14,8},{1,7},{3,5},... | collective-permute-start | bytes 61448 | tf_op jit(solution)/shard_map/ppermute | solution.py:514
  12.2 3.8 %collective-permute-start.5 = (f32[40,128]{1,0:T(8,128)S(1)}, f32[40,128]{1,0:T(8,128)S(1)}, u32[]{:S(2)}, u32[]{:S(2)}) collective-permute-start(f32[40,128]{1,0:T(8,128)S(1)} %get-tuple-element.46), channel_id=1, source_target_pairs={{0,2},{2,0},{4,10},{6,8},{8,6},{10,4},{12,14},{14,12},{1,3},{3,1},... | collective-permute-start | bytes 61448 | tf_op jit(solution)/shard_map/ppermute | solution.py:514
  16.0 11.9 %copy-start.1 = (f32[1,1,8,128,128]{4,3,2,1,0:T(8,128)S(1)}, f32[1,1,8,128,128]{4,3,2,1,0:T(8,128)}, u32[]{:S(2)}) copy-start(f32[1,1,8,128,128]{4,3,2,1,0:T(8,128)} %param.25) | copy-start | bytes 1572868
  37.6 3.7 %collective-permute-start.6 = (f32[16,128]{1,0:T(8,128)S(1)}, f32[16,128]{1,0:T(8,128)S(1)}, u32[]{:S(2)}, u32[]{:S(2)}) collective-permute-start(f32[16,128]{1,0:T(8,128)S(1)} %shard_map.156.refs_1_), channel_id=1, source_target_pairs={{0,2},{2,0},{4,6},{6,4},{8,10},{10,8},{12,14},{14,12},{1,3},{3,1},... | collective-permute-start | bytes 24584 | tf_op jit(solution)/shard_map/ppermute | solution.py:514
  41.3 3.7 %collective-permute-start.7 = (f32[32,128]{1,0:T(8,128)S(1)}, f32[32,128]{1,0:T(8,128)S(1)}, u32[]{:S(2)}, u32[]{:S(2)}) collective-permute-start(f32[32,128]{1,0:T(8,128)S(1)} %pad_maximum_fusion), channel_id=1, source_target_pairs={{0,4},{2,6},{4,0},{6,2},{8,12},{10,14},{12,8},{14,10},{1,5},{3,7},... | collective-permute-start | bytes 49160 | tf_op jit(solution)/shard_map/ppermute | solution.py:514
  41.7 3.4 %collective-permute-start.8 = (f32[32,128]{1,0:T(8,128)S(1)}, f32[32,128]{1,0:T(8,128)S(1)}, u32[]{:S(2)}, u32[]{:S(2)}) collective-permute-start(f32[32,128]{1,0:T(8,128)S(1)} %pad_maximum_fusion), channel_id=1, source_target_pairs={{0,0},{2,2},{4,8},{6,10},{8,4},{10,6},{12,12},{14,14},{1,1},{3,3},... | collective-permute-start | bytes 49160 | tf_op jit(solution)/shard_map/ppermute | solution.py:514
  46.2 1.6 %collective-permute-start.9 = (f32[2,56,512]{2,1,0:T(8,128)S(1)}, f32[2,56,512]{2,1,0:T(8,128)S(1)}, u32[]{:S(2)}, u32[]{:S(2)}) collective-permute-start(f32[2,56,512]{2,1,0:T(8,128)S(1)} %shard_map.157.refs_2_), channel_id=1, source_target_pairs={{0,1},{1,0},{2,3},{3,2},{4,5},{5,4},{6,7},{7,6},{8,9},{9,8},{10,11... | collective-permute-start | bytes 688136 | tf_op jit(solution)/shard_map/ppermute | solution.py:501

commit v7 on v6

--- a/solution.py
+++ b/solution.py
@@ -319,28 +319,25 @@
         return total + dot(left, interp[b], 1)
 
     departure = for_each(count, body, jnp.zeros((count, width), f32)) - innovation[...]
-    half = sent.shape[1] // 2
-    sent[...] = jnp.zeros(sent.shape, f32)
     for o in range(owners):
         for s in range(slots):
             live = jnp.full((1, width), counts_s[0, o], jnp.int32) > s
             b = o * slots + s
             sent[o, s : s + 1, :] = jnp.where(live, departure[b : b + 1, :], 0.0)
-            sent[o, half + s : half + s + 1, :] = jnp.full((1, width), platforms_s[s, o].astype(f32), f32)
+            sent[o, slots + s : slots + s + 1, :] = jnp.full((1, width), platforms_s[s, o].astype(f32), f32)
 
 
 def weigh_kernel(slots, arrived, matrices, out, values, platform):
-    tiles, height, width = arrived.shape
+    tiles = arrived.shape[0]
     for t in range(tiles):
         for s in range(slots):
             at = s * tiles + t
             values[at : at + 1, :] = arrived[t, s : s + 1, :]
-            platform[at : at + 1, :] = arrived[t, height // 2 + s : height // 2 + s + 1, :]
+            platform[at : at + 1, :] = arrived[t, slots + s : slots + s + 1, :]
     x, where = values[...], platform[...]
     total = jnp.zeros(x.shape, f32)
     for p in range(matrices.shape[0]):
         total = total + dot(jnp.where(where == float(p), x, 0.0), jnp.concatenate(split(matrices[p]), axis=0), 1)
-    out[...] = jnp.zeros(out.shape, f32)
     for t in range(tiles):
         for s in range(slots):
             at = s * tiles + t
@@ -565,7 +562,6 @@
             phase: jnp.where(lane < LANES // 2, diag_raw[phase, 1], diag_raw[phase, -1]) for phase in (1, 2)
         }
 
-    half = -(-slots // 4) * 4
     ext = held(layers, ext_rows, ext_cols)
     *exts, square_v = call(extend_kernel, [ext] * 5 + [held(1, LANES)], [SMEM] + [VMEM] * 5)(
         previous_square, blended, spread_v, wind_e_v, wind_n_v, scale_v
@@ -574,7 +570,7 @@
     weights = call(parts_kernel, held(count, 2 * width, width, dtype=bf16), [VMEM], (), limit)(weights)
     sent, _, ext_spread, ext_e, ext_n, ext_scale = call(
         forward_kernel,
-        [held(owners, 2 * half, width)] + [ext] * 5,
+        [held(owners, 2 * slots, width)] + [ext] * 5,
         [VMEM] * 15,
         [
             pltpu.VMEM((layers * ext_rows * per, LANES), f32),
@@ -592,7 +588,7 @@
     arrived = lax.all_to_all(sent, ("lat", "lon"), split_axis=0, concat_axis=0, tiled=True)
     result = call(
         functools.partial(weigh_kernel, slots),
-        held(owners, 2 * half, width),
+        held(owners, slots, width),
         [VMEM] * 2,
         [pltpu.VMEM((count, width), f32)] * 2,
     )(arrived, matrices)

time: 60.6 us -> 60.3 us (level)
  no operation moved by 1% of the time
where the time goes in v7:
time: 60.3 us; the launch traced here: 60 us
  blocking collectives  29.9 us (50%)
  starting transfers between devices  13.2 us (22%)
  waiting for transfers between devices  8.35 us (14%)
  Pallas kernels  7.17 us (12%)
  between operations  1.41 us (2%)
    ppermute x8, starting transfers between devices, exchange(): return lax.ppermute(field, ('lat', 'lon'), pairs)  12.6 us
    all_to_all x1, blocking collectives, local(): lax.all_to_all(partial, ('lat', 'lon', 'lev'), split_axis=0, concat_axis=...  11.5 us
    all_to_all x1, blocking collectives, local(): lax.all_to_all(sent, ('lat', 'lon'), split_axis=0, concat_axis=0, tiled=T...  9.49 us
    all_to_all x1, blocking collectives, local(): lax.all_to_all(result, ('lat', 'lon'), split_axis=0, concat_axis=0, tiled...  8.89 us
    ppermute x8, waiting for transfers between devices, exchange(): return lax.ppermute(field, ('lat', 'lon'), pairs)  6.87 us
    pallas_call x1, Pallas kernels, local(): call(forward_kernel, [held(owners, 2 * slots, width)] + [ext] * 5, [VMEM]...  2.32 us
    pallas_call x1, Pallas kernels, local(): call(load_kernel, [mix, mix] + [field] * 6 + [held(count, width)] + [held...  1.57 us
    ppermute x2, waiting for transfers between devices, from_levs(): lax.ppermute(field, 'lev', [(i, (i + k) % n_lev) for i in range(n_lev)])  1.48 us
  transfers between devices with their start and end apart: 10, of which 4 were waited for; matrix products, arithmetic and copies ran while one was open for 0% of the time, Pallas kernels for 3%

profile of v7, /device:TPU:0, one launch (start us, length us, event | category | flops | bytes accessed | tf_op | source)
XLA Modules:
  0.0 60.0 jit_solution(3798680869519760834)
XLA Ops:
  0.6 0.5 collective-permute-start
  1.2 1.6 %shard_map.149 = (f32[8,128]{1,0:T(8,128)S(1)}, f32[8,128]{1,0:T(8,128)S(1)}, f32[2,56,512]{2,1,0:T(8,128)S(1)}, f32[2,56,512]{2,1,0:T(8,128)S(1)}, f32[2,56,512...) custom-call(f32[4,4]{1,0:T(4,128)} %vertical.1, ...), custom_call_target="tpu_custom_call" | custom-call | flops 1048576 | bytes 1048576 | tf_op jit(solution)/shard_map/pallas_call | solution.py:525
  2.9 2.7 %collective-permute-start.2 = (f32[40,512]{1,0:T(8,128)S(1)}, f32[40,512]{1,0:T(8,128)S(1)}, u32[]{:S(2)}, u32[]{:S(2)}) collective-permute-start(f32[40,512]{1,0:T(8,128)S(1)} %get-tuple-element.43), channel_id=1, source_target_pairs={{0,4},{2,6},{4,0},{6,2},{8,12},{10,14},{12,8},{14,10},{1,5},{3,7},... | collective-permute-start | bytes 245768 | tf_op jit(solution)/shard_map/ppermute | solution.py:511
  5.7 0.7 %collective-permute-start.4 = (f32[40,512]{1,0:T(8,128)S(1)}, f32[40,512]{1,0:T(8,128)S(1)}, u32[]{:S(2)}, u32[]{:S(2)}) collective-permute-start(f32[40,512]{1,0:T(8,128)S(1)} %get-tuple-element.45), channel_id=1, source_target_pairs={{0,0},{2,2},{4,8},{6,10},{8,4},{10,6},{12,12},{14,14},{1,1},{3,3},... | collective-permute-start | bytes 245768 | tf_op jit(solution)/shard_map/ppermute | solution.py:511
  6.3 1.6 %collective-permute-start.1 = (f32[64,128]{1,0:T(8,128)S(1)}, f32[64,128]{1,0:T(8,128)S(1)}, u32[]{:S(2)}, u32[]{:S(2)}) collective-permute-start(f32[64,128]{1,0:T(8,128)S(1)} %get-tuple-element.42.refs_0_), channel_id=1, source_target_pairs={{0,2},{2,0},{4,6},{6,4},{8,10},{10,8},{12,14},{14,12},{1,3},{3,1},... | collective-permute-start | bytes 98312 | tf_op jit(solution)/shard_map/ppermute | solution.py:511
  7.9 4.4 %collective-permute-start.3 = (f32[40,128]{1,0:T(8,128)S(1)}, f32[40,128]{1,0:T(8,128)S(1)}, u32[]{:S(2)}, u32[]{:S(2)}) collective-permute-start(f32[40,128]{1,0:T(8,128)S(1)} %get-tuple-element.44), channel_id=1, source_target_pairs={{0,6},{2,4},{4,2},{6,0},{8,14},{10,12},{12,10},{14,8},{1,7},{3,5},... | collective-permute-start | bytes 61448 | tf_op jit(solution)/shard_map/ppermute | solution.py:511
  12.2 1.5 %collective-permute-start.5 = (f32[40,128]{1,0:T(8,128)S(1)}, f32[40,128]{1,0:T(8,128)S(1)}, u32[]{:S(2)}, u32[]{:S(2)}) collective-permute-start(f32[40,128]{1,0:T(8,128)S(1)} %get-tuple-element.46), channel_id=1, source_target_pairs={{0,2},{2,0},{4,10},{6,8},{8,6},{10,4},{12,14},{14,12},{1,3},{3,1},... | collective-permute-start | bytes 61448 | tf_op jit(solution)/shard_map/ppermute | solution.py:511
  14.6 1.4 %collective-permute-done.5.refs_5_.diag_2 = f32[40,128]{1,0:T(8,128)S(1)} collective-permute-done((f32[40,128]{1,0:T(8,128)S(1)}, f32[40,128]{1,0:T(8,128)S(1)}, u32[]{:S(2)}, u32[]{:S(2)}) %collective-permute-start.5) | collective-permute-done | bytes 20512 | tf_op jit(solution)/shard_map/ppermute | solution.py:511
  16.0 2.3 %shard_map.154 = (f32[8,4,128]{2,1,0:T(4,128)S(1)}, f32[2,64,640]{2,1,0:T(8,128)S(1)}, f32[2,64,640]{2,1,0:T(8,128)S(1)}, f32[2,64,640]{2,1,0:T(8,128)S(1)}, f32...) custom-call(s32[1,128]{1,0:T(1,128)S(1)} %get-tuple-element.47.place, ...), custom_call_target="tpu_custom_call", output_to_operand_aliasing={{1}: (3, {}), {2}: (4, {}), {3}: (5, {}), {4}: (6, {}), {5}... | custom-call | flops 1048576 | bytes 1048576 | tf_op jit(solution)/shard_map/pallas_call | solution.py:571
  18.4 9.5 %all_to_all.15.arrived = f32[8,4,128]{2,1,0:T(4,128)S(1)} all-to-all(f32[8,4,128]{2,1,0:T(4,128)S(1)} %get-tuple-element.61), channel_id=1, replica_groups=mesh['member'=2,'lat'=4,'lon'=2,'lev'=2] {'lat','lon'}, dimensions={0} | all-to-all | bytes 32768 | tf_op jit(solution)/shard_map/all_to_all | solution.py:588
  27.9 0.3 shard_map.155
  28.1 8.9 %all_to_all.16.returned = f32[8,2,128]{2,1,0:T(2,128)S(1)} all-to-all(f32[8,2,128]{2,1,0:T(2,128)S(1)} %shard_map.155), channel_id=1, replica_groups=mesh['member'=2,'lat'=4,'lon'=2,'lev'=2] {'lat','lon'}, dimensions={0} | all-to-all | bytes 16384 | tf_op jit(solution)/shard_map/all_to_all | solution.py:595
  37.0 0.3 shard_map.156.refs_1_
  37.3 0.6 %collective-permute-start.6 = (f32[16,128]{1,0:T(8,128)S(1)}, f32[16,128]{1,0:T(8,128)S(1)}, u32[]{:S(2)}, u32[]{:S(2)}) collective-permute-start(f32[16,128]{1,0:T(8,128)S(1)} %shard_map.156.refs_1_), channel_id=1, source_target_pairs={{0,2},{2,0},{4,6},{6,4},{8,10},{10,8},{12,14},{14,12},{1,3},{3,1},... | collective-permute-start | bytes 24584 | tf_op jit(solution)/shard_map/ppermute | solution.py:511
  37.9 3.1 %collective-permute-done.6.refs_2_ = f32[16,128]{1,0:T(8,128)S(1)} collective-permute-done((f32[16,128]{1,0:T(8,128)S(1)}, f32[16,128]{1,0:T(8,128)S(1)}, u32[]{:S(2)}, u32[]{:S(2)}) %collective-permute-start.6) | collective-permute-done | bytes 8224 | tf_op jit(solution)/shard_map/ppermute | solution.py:511
  41.0 0.5 collective-permute-start.7
  41.5 0.7 %collective-permute-start.8 = (f32[32,128]{1,0:T(8,128)S(1)}, f32[32,128]{1,0:T(8,128)S(1)}, u32[]{:S(2)}, u32[]{:S(2)}) collective-permute-start(f32[32,128]{1,0:T(8,128)S(1)} %pad_maximum_fusion), channel_id=1, source_target_pairs={{0,0},{2,2},{4,8},{6,10},{8,4},{10,6},{12,12},{14,14},{1,1},{3,3},... | collective-permute-start | bytes 49160 | tf_op jit(solution)/shard_map/ppermute | solution.py:511
  42.2 0.2 shard_map.151.refs_0_
  42.4 2.3 %collective-permute-done.7.refs_3_ = f32[32,128]{1,0:T(8,128)S(1)} collective-permute-done((f32[32,128]{1,0:T(8,128)S(1)}, f32[32,128]{1,0:T(8,128)S(1)}, u32[]{:S(2)}, u32[]{:S(2)}) %collective-permute-start.7) | collective-permute-done | bytes 16416 | tf_op jit(solution)/shard_map/ppermute | solution.py:511
  44.8 1.2 %shard_map.157.refs_2_ = f32[2,56,512]{2,1,0:T(8,128)S(1)} custom-call(bf16[768,256]{1,0:T(8,128)(2,1)S(1)} %shard_map.151.refs_0_, f32[16,128]{1,0:T(8,128)S(1)} %shard_map.156.refs_1_, f32[16,128]{1,0:T(8,128)S(1)} %collective-permute-done.6.refs_2_, f32[32,128]{1,0:T(8,128)S(1)} %collective-permute-done.7.refs_3_, ...), custom_call_target="tpu_custom_call" | custom-call | flops 1048576 | bytes 1048576 | tf_op jit(solution)/shard_map/pallas_call | solution.py:621
  46.0 1.5 %collective-permute-done.9.refs_3_ = f32[2,56,512]{2,1,0:T(8,128)S(1)} collective-permute-done((f32[2,56,512]{2,1,0:T(8,128)S(1)}, f32[2,56,512]{2,1,0:T(8,128)S(1)}, u32[]{:S(2)}, u32[]{:S(2)}) %collective-permute-start.9) | collective-permute-done | bytes 229408 | tf_op jit(solution)/shard_map/ppermute | solution.py:498
  47.5 0.2 shard_map.158
  47.7 11.5 %all_to_all.17.sums = f32[16,1,128]{2,1,0:T(1,128)S(1)} all-to-all(f32[16,1,128]{2,1,0:T(1,128)S(1)} %get-tuple-element.67), channel_id=1, replica_groups=mesh['member'=2,'lat'=4,'lon'=2,'lev'=2] {'lat','lon','lev'}, dimensions={0} | all-to-all | bytes 16384 | tf_op jit(solution)/shard_map/all_to_all | solution.py:636
  59.2 0.8 %shard_map.159 = (f32[2,56,512]{2,1,0:T(8,128)}, f32[2,56,512]{2,1,0:T(8,128)}) custom-call(f32[2,56,512]{2,1,0:T(8,128)S(1)} %get-tuple-element.66.gradient_in, f32[16,1,128]{2,1,0:T(1,128)S(1)} %all_to_all.17.sums, f32[2,56,512]{2,1,0:T(8,128)S(1)} %get-tuple-element.68.previous, f32[1,128]{1,0:T(1,128)S(1)} %get-tuple-element.69.previous_square), custom_call_target="tpu_custom_call" | custom-call | flops 1048576 | bytes 1048576 | tf_op jit(solution)/shard_map/pallas_call | solution.py:637
  (15 shorter events, 0.5 us)
Async XLA Ops:
  0.6 13.7 %copy-start = (f32[1,1,1,8,2,128,128]{6,5,4,3,2,1,0:T(8,128)S(1)}, f32[1,1,1,8,2,128,128]{6,5,4,3,2,1,0:T(8,128)}, u32[]{:S(2)}) copy-start(f32[1,1,1,8,2,128,128]{6,5,4,3,2,1,0:T(8,128)} %param.23) | copy-start | bytes 3145732
  0.6 2.1 %collective-permute-start = (f32[2,56,512]{2,1,0:T(8,128)}, f32[2,56,512]{2,1,0:T(8,128)S(1)}, u32[]{:S(2)}, u32[]{:S(2)}) collective-permute-start(f32[2,56,512]{2,1,0:T(8,128)} %control.1), channel_id=1, source_target_pairs={{0,1},{1,0},{2,3},{3,2},{4,5},{5,4},{6,7},{7,6},{8,9},{9,8},{10,11... | collective-permute-start | bytes 688136 | tf_op jit(solution)/shard_map/ppermute | solution.py:498
  2.9 13.1 %collective-permute-start.2 = (f32[40,512]{1,0:T(8,128)S(1)}, f32[40,512]{1,0:T(8,128)S(1)}, u32[]{:S(2)}, u32[]{:S(2)}) collective-permute-start(f32[40,512]{1,0:T(8,128)S(1)} %get-tuple-element.43), channel_id=1, source_target_pairs={{0,4},{2,6},{4,0},{6,2},{8,12},{10,14},{12,8},{14,10},{1,5},{3,7},... | collective-permute-start | bytes 245768 | tf_op jit(solution)/shard_map/ppermute | solution.py:511
  5.7 10.4 %collective-permute-start.4 = (f32[40,512]{1,0:T(8,128)S(1)}, f32[40,512]{1,0:T(8,128)S(1)}, u32[]{:S(2)}, u32[]{:S(2)}) collective-permute-start(f32[40,512]{1,0:T(8,128)S(1)} %get-tuple-element.45), channel_id=1, source_target_pairs={{0,0},{2,2},{4,8},{6,10},{8,4},{10,6},{12,12},{14,14},{1,1},{3,3},... | collective-permute-start | bytes 245768 | tf_op jit(solution)/shard_map/ppermute | solution.py:511
  6.3 9.7 %collective-permute-start.1 = (f32[64,128]{1,0:T(8,128)S(1)}, f32[64,128]{1,0:T(8,128)S(1)}, u32[]{:S(2)}, u32[]{:S(2)}) collective-permute-start(f32[64,128]{1,0:T(8,128)S(1)} %get-tuple-element.42.refs_0_), channel_id=1, source_target_pairs={{0,2},{2,0},{4,6},{6,4},{8,10},{10,8},{12,14},{14,12},{1,3},{3,1},... | collective-permute-start | bytes 98312 | tf_op jit(solution)/shard_map/ppermute | solution.py:511
  7.9 6.7 %collective-permute-start.3 = (f32[40,128]{1,0:T(8,128)S(1)}, f32[40,128]{1,0:T(8,128)S(1)}, u32[]{:S(2)}, u32[]{:S(2)}) collective-permute-start(f32[40,128]{1,0:T(8,128)S(1)} %get-tuple-element.44), channel_id=1, source_target_pairs={{0,6},{2,4},{4,2},{6,0},{8,14},{10,12},{12,10},{14,8},{1,7},{3,5},... | collective-permute-start | bytes 61448 | tf_op jit(solution)/shard_map/ppermute | solution.py:511
  12.2 3.8 %collective-permute-start.5 = (f32[40,128]{1,0:T(8,128)S(1)}, f32[40,128]{1,0:T(8,128)S(1)}, u32[]{:S(2)}, u32[]{:S(2)}) collective-permute-start(f32[40,128]{1,0:T(8,128)S(1)} %get-tuple-element.46), channel_id=1, source_target_pairs={{0,2},{2,0},{4,10},{6,8},{8,6},{10,4},{12,14},{14,12},{1,3},{3,1},... | collective-permute-start | bytes 61448 | tf_op jit(solution)/shard_map/ppermute | solution.py:511
  16.0 11.8 %copy-start.1 = (f32[1,1,8,128,128]{4,3,2,1,0:T(8,128)S(1)}, f32[1,1,8,128,128]{4,3,2,1,0:T(8,128)}, u32[]{:S(2)}) copy-start(f32[1,1,8,128,128]{4,3,2,1,0:T(8,128)} %param.25) | copy-start | bytes 1572868
  37.3 3.7 %collective-permute-start.6 = (f32[16,128]{1,0:T(8,128)S(1)}, f32[16,128]{1,0:T(8,128)S(1)}, u32[]{:S(2)}, u32[]{:S(2)}) collective-permute-start(f32[16,128]{1,0:T(8,128)S(1)} %shard_map.156.refs_1_), channel_id=1, source_target_pairs={{0,2},{2,0},{4,6},{6,4},{8,10},{10,8},{12,14},{14,12},{1,3},{3,1},... | collective-permute-start | bytes 24584 | tf_op jit(solution)/shard_map/ppermute | solution.py:511
  41.0 3.7 %collective-permute-start.7 = (f32[32,128]{1,0:T(8,128)S(1)}, f32[32,128]{1,0:T(8,128)S(1)}, u32[]{:S(2)}, u32[]{:S(2)}) collective-permute-start(f32[32,128]{1,0:T(8,128)S(1)} %pad_maximum_fusion), channel_id=1, source_target_pairs={{0,4},{2,6},{4,0},{6,2},{8,12},{10,14},{12,8},{14,10},{1,5},{3,7},... | collective-permute-start | bytes 49160 | tf_op jit(solution)/shard_map/ppermute | solution.py:511
  41.5 3.2 %collective-permute-start.8 = (f32[32,128]{1,0:T(8,128)S(1)}, f32[32,128]{1,0:T(8,128)S(1)}, u32[]{:S(2)}, u32[]{:S(2)}) collective-permute-start(f32[32,128]{1,0:T(8,128)S(1)} %pad_maximum_fusion), channel_id=1, source_target_pairs={{0,0},{2,2},{4,8},{6,10},{8,4},{10,6},{12,12},{14,14},{1,1},{3,3},... | collective-permute-start | bytes 49160 | tf_op jit(solution)/shard_map/ppermute | solution.py:511
  46.0 1.6 %collective-permute-start.9 = (f32[2,56,512]{2,1,0:T(8,128)S(1)}, f32[2,56,512]{2,1,0:T(8,128)S(1)}, u32[]{:S(2)}, u32[]{:S(2)}) collective-permute-start(f32[2,56,512]{2,1,0:T(8,128)S(1)} %shard_map.157.refs_2_), channel_id=1, source_target_pairs={{0,1},{1,0},{2,3},{3,2},{4,5},{5,4},{6,7},{7,6},{8,9},{9,8},{10,11... | collective-permute-start | bytes 688136 | tf_op jit(solution)/shard_map/ppermute | solution.py:498

commit v8 on v7

--- a/solution.py
+++ b/solution.py
@@ -297,13 +297,8 @@
         for step in range(STEPS):
             if step:
                 x = x * mask
-            x = (
-                (1.0 - 4.0 * diffusion) * x
-                + (diffusion - u) * east(x)
-                + (diffusion + u) * west(x)
-                + (diffusion - v) * north(x)
-                + (diffusion + v) * south(x)
-            )
+            e, w, n, t = east(x), west(x), north(x), south(x)
+            x = (1.0 - 4.0 * diffusion) * x + diffusion * ((e + w) + (n + t)) + (u * (w - e) + v * (t - n))
         for c in range(per):
             begin = (l * per + c) * ext_rows
             field[begin : begin + ext_rows, :] = x[:, c * LANES : (c + 1) * LANES]

time: 60.3 us -> 60.3 us (level)
  no operation moved by 1% of the time
where the time goes in v8:
time: 60.3 us; the launch traced here: 60 us
  blocking collectives  29.9 us (50%)
  starting transfers between devices  13.2 us (22%)
  waiting for transfers between devices  8.35 us (14%)
  Pallas kernels  7.15 us (12%)
  between operations  1.41 us (2%)
    ppermute x8, starting transfers between devices, exchange(): return lax.ppermute(field, ('lat', 'lon'), pairs)  12.6 us
    all_to_all x1, blocking collectives, local(): lax.all_to_all(partial, ('lat', 'lon', 'lev'), split_axis=0, concat_axis=...  11.5 us
    all_to_all x1, blocking collectives, local(): lax.all_to_all(sent, ('lat', 'lon'), split_axis=0, concat_axis=0, tiled=T...  9.49 us
    all_to_all x1, blocking collectives, local(): lax.all_to_all(result, ('lat', 'lon'), split_axis=0, concat_axis=0, tiled...  8.89 us
    ppermute x8, waiting for transfers between devices, exchange(): return lax.ppermute(field, ('lat', 'lon'), pairs)  6.87 us
    pallas_call x1, Pallas kernels, local(): call(forward_kernel, [held(owners, 2 * slots, width)] + [ext] * 5, [VMEM]...  2.31 us
    pallas_call x1, Pallas kernels, local(): call(load_kernel, [mix, mix] + [field] * 6 + [held(count, width)] + [held...  1.57 us
    ppermute x2, waiting for transfers between devices, from_levs(): lax.ppermute(field, 'lev', [(i, (i + k) % n_lev) for i in range(n_lev)])  1.48 us
  transfers between devices with their start and end apart: 10, of which 4 were waited for; matrix products, arithmetic and copies ran while one was open for 0% of the time, Pallas kernels for 3%

profile of v8, /device:TPU:0, one launch (start us, length us, event | category | flops | bytes accessed | tf_op | source)
XLA Modules:
  0.0 60.0 jit_solution(15980004361186788757)
XLA Ops:
  0.6 0.5 collective-permute-start
  1.2 1.6 %shard_map.149 = (f32[8,128]{1,0:T(8,128)S(1)}, f32[8,128]{1,0:T(8,128)S(1)}, f32[2,56,512]{2,1,0:T(8,128)S(1)}, f32[2,56,512]{2,1,0:T(8,128)S(1)}, f32[2,56,512...) custom-call(f32[4,4]{1,0:T(4,128)} %vertical.1, ...), custom_call_target="tpu_custom_call" | custom-call | flops 1048576 | bytes 1048576 | tf_op jit(solution)/shard_map/pallas_call | solution.py:520
  2.9 2.7 %collective-permute-start.2 = (f32[40,512]{1,0:T(8,128)S(1)}, f32[40,512]{1,0:T(8,128)S(1)}, u32[]{:S(2)}, u32[]{:S(2)}) collective-permute-start(f32[40,512]{1,0:T(8,128)S(1)} %get-tuple-element.43), channel_id=1, source_target_pairs={{0,4},{2,6},{4,0},{6,2},{8,12},{10,14},{12,8},{14,10},{1,5},{3,7},... | collective-permute-start | bytes 245768 | tf_op jit(solution)/shard_map/ppermute | solution.py:506
  5.7 0.7 %collective-permute-start.4 = (f32[40,512]{1,0:T(8,128)S(1)}, f32[40,512]{1,0:T(8,128)S(1)}, u32[]{:S(2)}, u32[]{:S(2)}) collective-permute-start(f32[40,512]{1,0:T(8,128)S(1)} %get-tuple-element.45), channel_id=1, source_target_pairs={{0,0},{2,2},{4,8},{6,10},{8,4},{10,6},{12,12},{14,14},{1,1},{3,3},... | collective-permute-start | bytes 245768 | tf_op jit(solution)/shard_map/ppermute | solution.py:506
  6.3 1.6 %collective-permute-start.1 = (f32[64,128]{1,0:T(8,128)S(1)}, f32[64,128]{1,0:T(8,128)S(1)}, u32[]{:S(2)}, u32[]{:S(2)}) collective-permute-start(f32[64,128]{1,0:T(8,128)S(1)} %get-tuple-element.42.refs_0_), channel_id=1, source_target_pairs={{0,2},{2,0},{4,6},{6,4},{8,10},{10,8},{12,14},{14,12},{1,3},{3,1},... | collective-permute-start | bytes 98312 | tf_op jit(solution)/shard_map/ppermute | solution.py:506
  7.9 4.4 %collective-permute-start.3 = (f32[40,128]{1,0:T(8,128)S(1)}, f32[40,128]{1,0:T(8,128)S(1)}, u32[]{:S(2)}, u32[]{:S(2)}) collective-permute-start(f32[40,128]{1,0:T(8,128)S(1)} %get-tuple-element.44), channel_id=1, source_target_pairs={{0,6},{2,4},{4,2},{6,0},{8,14},{10,12},{12,10},{14,8},{1,7},{3,5},... | collective-permute-start | bytes 61448 | tf_op jit(solution)/shard_map/ppermute | solution.py:506
  12.2 1.5 %collective-permute-start.5 = (f32[40,128]{1,0:T(8,128)S(1)}, f32[40,128]{1,0:T(8,128)S(1)}, u32[]{:S(2)}, u32[]{:S(2)}) collective-permute-start(f32[40,128]{1,0:T(8,128)S(1)} %get-tuple-element.46), channel_id=1, source_target_pairs={{0,2},{2,0},{4,10},{6,8},{8,6},{10,4},{12,14},{14,12},{1,3},{3,1},... | collective-permute-start | bytes 61448 | tf_op jit(solution)/shard_map/ppermute | solution.py:506
  14.6 1.4 %collective-permute-done.5.refs_5_.diag_2 = f32[40,128]{1,0:T(8,128)S(1)} collective-permute-done((f32[40,128]{1,0:T(8,128)S(1)}, f32[40,128]{1,0:T(8,128)S(1)}, u32[]{:S(2)}, u32[]{:S(2)}) %collective-permute-start.5) | collective-permute-done | bytes 20512 | tf_op jit(solution)/shard_map/ppermute | solution.py:506
  16.0 2.3 %shard_map.154 = (f32[8,4,128]{2,1,0:T(4,128)S(1)}, f32[2,64,640]{2,1,0:T(8,128)S(1)}, f32[2,64,640]{2,1,0:T(8,128)S(1)}, f32[2,64,640]{2,1,0:T(8,128)S(1)}, f32...) custom-call(s32[1,128]{1,0:T(1,128)S(1)} %get-tuple-element.47.place, ...), custom_call_target="tpu_custom_call", output_to_operand_aliasing={{1}: (3, {}), {2}: (4, {}), {3}: (5, {}), {4}: (6, {}), {5}... | custom-call | flops 1048576 | bytes 1048576 | tf_op jit(solution)/shard_map/pallas_call | solution.py:566
  18.4 9.5 %all_to_all.15.arrived = f32[8,4,128]{2,1,0:T(4,128)S(1)} all-to-all(f32[8,4,128]{2,1,0:T(4,128)S(1)} %get-tuple-element.61), channel_id=1, replica_groups=mesh['member'=2,'lat'=4,'lon'=2,'lev'=2] {'lat','lon'}, dimensions={0} | all-to-all | bytes 32768 | tf_op jit(solution)/shard_map/all_to_all | solution.py:583
  27.8 0.3 shard_map.155
  28.1 8.9 %all_to_all.16.returned = f32[8,2,128]{2,1,0:T(2,128)S(1)} all-to-all(f32[8,2,128]{2,1,0:T(2,128)S(1)} %shard_map.155), channel_id=1, replica_groups=mesh['member'=2,'lat'=4,'lon'=2,'lev'=2] {'lat','lon'}, dimensions={0} | all-to-all | bytes 16384 | tf_op jit(solution)/shard_map/all_to_all | solution.py:590
  37.0 0.3 shard_map.156.refs_1_
  37.3 0.6 %collective-permute-start.6 = (f32[16,128]{1,0:T(8,128)S(1)}, f32[16,128]{1,0:T(8,128)S(1)}, u32[]{:S(2)}, u32[]{:S(2)}) collective-permute-start(f32[16,128]{1,0:T(8,128)S(1)} %shard_map.156.refs_1_), channel_id=1, source_target_pairs={{0,2},{2,0},{4,6},{6,4},{8,10},{10,8},{12,14},{14,12},{1,3},{3,1},... | collective-permute-start | bytes 24584 | tf_op jit(solution)/shard_map/ppermute | solution.py:506
  37.9 3.1 %collective-permute-done.6.refs_2_ = f32[16,128]{1,0:T(8,128)S(1)} collective-permute-done((f32[16,128]{1,0:T(8,128)S(1)}, f32[16,128]{1,0:T(8,128)S(1)}, u32[]{:S(2)}, u32[]{:S(2)}) %collective-permute-start.6) | collective-permute-done | bytes 8224 | tf_op jit(solution)/shard_map/ppermute | solution.py:506
  41.0 0.5 collective-permute-start.7
  41.5 0.7 %collective-permute-start.8 = (f32[32,128]{1,0:T(8,128)S(1)}, f32[32,128]{1,0:T(8,128)S(1)}, u32[]{:S(2)}, u32[]{:S(2)}) collective-permute-start(f32[32,128]{1,0:T(8,128)S(1)} %pad_maximum_fusion), channel_id=1, source_target_pairs={{0,0},{2,2},{4,8},{6,10},{8,4},{10,6},{12,12},{14,14},{1,1},{3,3},... | collective-permute-start | bytes 49160 | tf_op jit(solution)/shard_map/ppermute | solution.py:506
  42.2 0.2 shard_map.151.refs_0_
  42.4 2.3 %collective-permute-done.7.refs_3_ = f32[32,128]{1,0:T(8,128)S(1)} collective-permute-done((f32[32,128]{1,0:T(8,128)S(1)}, f32[32,128]{1,0:T(8,128)S(1)}, u32[]{:S(2)}, u32[]{:S(2)}) %collective-permute-start.7) | collective-permute-done | bytes 16416 | tf_op jit(solution)/shard_map/ppermute | solution.py:506
  44.7 1.2 %shard_map.157.refs_2_ = f32[2,56,512]{2,1,0:T(8,128)S(1)} custom-call(bf16[768,256]{1,0:T(8,128)(2,1)S(1)} %shard_map.151.refs_0_, f32[16,128]{1,0:T(8,128)S(1)} %shard_map.156.refs_1_, f32[16,128]{1,0:T(8,128)S(1)} %collective-permute-done.6.refs_2_, f32[32,128]{1,0:T(8,128)S(1)} %collective-permute-done.7.refs_3_, ...), custom_call_target="tpu_custom_call" | custom-call | flops 1048576 | bytes 1048576 | tf_op jit(solution)/shard_map/pallas_call | solution.py:616
  46.0 1.5 %collective-permute-done.9.refs_3_ = f32[2,56,512]{2,1,0:T(8,128)S(1)} collective-permute-done((f32[2,56,512]{2,1,0:T(8,128)S(1)}, f32[2,56,512]{2,1,0:T(8,128)S(1)}, u32[]{:S(2)}, u32[]{:S(2)}) %collective-permute-start.9) | collective-permute-done | bytes 229408 | tf_op jit(solution)/shard_map/ppermute | solution.py:493
  47.5 0.2 shard_map.158
  47.6 11.5 %all_to_all.17.sums = f32[16,1,128]{2,1,0:T(1,128)S(1)} all-to-all(f32[16,1,128]{2,1,0:T(1,128)S(1)} %get-tuple-element.67), channel_id=1, replica_groups=mesh['member'=2,'lat'=4,'lon'=2,'lev'=2] {'lat','lon','lev'}, dimensions={0} | all-to-all | bytes 16384 | tf_op jit(solution)/shard_map/all_to_all | solution.py:631
  59.1 0.8 %shard_map.159 = (f32[2,56,512]{2,1,0:T(8,128)}, f32[2,56,512]{2,1,0:T(8,128)}) custom-call(f32[2,56,512]{2,1,0:T(8,128)S(1)} %get-tuple-element.66.gradient_in, f32[16,1,128]{2,1,0:T(1,128)S(1)} %all_to_all.17.sums, f32[2,56,512]{2,1,0:T(8,128)S(1)} %get-tuple-element.68.previous, f32[1,128]{1,0:T(1,128)S(1)} %get-tuple-element.69.previous_square), custom_call_target="tpu_custom_call" | custom-call | flops 1048576 | bytes 1048576 | tf_op jit(solution)/shard_map/pallas_call | solution.py:632
  (15 shorter events, 0.5 us)
Async XLA Ops:
  0.6 13.7 %copy-start = (f32[1,1,1,8,2,128,128]{6,5,4,3,2,1,0:T(8,128)S(1)}, f32[1,1,1,8,2,128,128]{6,5,4,3,2,1,0:T(8,128)}, u32[]{:S(2)}) copy-start(f32[1,1,1,8,2,128,128]{6,5,4,3,2,1,0:T(8,128)} %param.23) | copy-start | bytes 3145732
  0.6 2.1 %collective-permute-start = (f32[2,56,512]{2,1,0:T(8,128)}, f32[2,56,512]{2,1,0:T(8,128)S(1)}, u32[]{:S(2)}, u32[]{:S(2)}) collective-permute-start(f32[2,56,512]{2,1,0:T(8,128)} %control.1), channel_id=1, source_target_pairs={{0,1},{1,0},{2,3},{3,2},{4,5},{5,4},{6,7},{7,6},{8,9},{9,8},{10,11... | collective-permute-start | bytes 688136 | tf_op jit(solution)/shard_map/ppermute | solution.py:493
  2.9 13.1 %collective-permute-start.2 = (f32[40,512]{1,0:T(8,128)S(1)}, f32[40,512]{1,0:T(8,128)S(1)}, u32[]{:S(2)}, u32[]{:S(2)}) collective-permute-start(f32[40,512]{1,0:T(8,128)S(1)} %get-tuple-element.43), channel_id=1, source_target_pairs={{0,4},{2,6},{4,0},{6,2},{8,12},{10,14},{12,8},{14,10},{1,5},{3,7},... | collective-permute-start | bytes 245768 | tf_op jit(solution)/shard_map/ppermute | solution.py:506
  5.7 10.4 %collective-permute-start.4 = (f32[40,512]{1,0:T(8,128)S(1)}, f32[40,512]{1,0:T(8,128)S(1)}, u32[]{:S(2)}, u32[]{:S(2)}) collective-permute-start(f32[40,512]{1,0:T(8,128)S(1)} %get-tuple-element.45), channel_id=1, source_target_pairs={{0,0},{2,2},{4,8},{6,10},{8,4},{10,6},{12,12},{14,14},{1,1},{3,3},... | collective-permute-start | bytes 245768 | tf_op jit(solution)/shard_map/ppermute | solution.py:506
  6.3 9.7 %collective-permute-start.1 = (f32[64,128]{1,0:T(8,128)S(1)}, f32[64,128]{1,0:T(8,128)S(1)}, u32[]{:S(2)}, u32[]{:S(2)}) collective-permute-start(f32[64,128]{1,0:T(8,128)S(1)} %get-tuple-element.42.refs_0_), channel_id=1, source_target_pairs={{0,2},{2,0},{4,6},{6,4},{8,10},{10,8},{12,14},{14,12},{1,3},{3,1},... | collective-permute-start | bytes 98312 | tf_op jit(solution)/shard_map/ppermute | solution.py:506
  7.9 6.7 %collective-permute-start.3 = (f32[40,128]{1,0:T(8,128)S(1)}, f32[40,128]{1,0:T(8,128)S(1)}, u32[]{:S(2)}, u32[]{:S(2)}) collective-permute-start(f32[40,128]{1,0:T(8,128)S(1)} %get-tuple-element.44), channel_id=1, source_target_pairs={{0,6},{2,4},{4,2},{6,0},{8,14},{10,12},{12,10},{14,8},{1,7},{3,5},... | collective-permute-start | bytes 61448 | tf_op jit(solution)/shard_map/ppermute | solution.py:506
  12.2 3.8 %collective-permute-start.5 = (f32[40,128]{1,0:T(8,128)S(1)}, f32[40,128]{1,0:T(8,128)S(1)}, u32[]{:S(2)}, u32[]{:S(2)}) collective-permute-start(f32[40,128]{1,0:T(8,128)S(1)} %get-tuple-element.46), channel_id=1, source_target_pairs={{0,2},{2,0},{4,10},{6,8},{8,6},{10,4},{12,14},{14,12},{1,3},{3,1},... | collective-permute-start | bytes 61448 | tf_op jit(solution)/shard_map/ppermute | solution.py:506
  16.0 11.8 %copy-start.1 = (f32[1,1,8,128,128]{4,3,2,1,0:T(8,128)S(1)}, f32[1,1,8,128,128]{4,3,2,1,0:T(8,128)}, u32[]{:S(2)}) copy-start(f32[1,1,8,128,128]{4,3,2,1,0:T(8,128)} %param.25) | copy-start | bytes 1572868
  37.3 3.7 %collective-permute-start.6 = (f32[16,128]{1,0:T(8,128)S(1)}, f32[16,128]{1,0:T(8,128)S(1)}, u32[]{:S(2)}, u32[]{:S(2)}) collective-permute-start(f32[16,128]{1,0:T(8,128)S(1)} %shard_map.156.refs_1_), channel_id=1, source_target_pairs={{0,2},{2,0},{4,6},{6,4},{8,10},{10,8},{12,14},{14,12},{1,3},{3,1},... | collective-permute-start | bytes 24584 | tf_op jit(solution)/shard_map/ppermute | solution.py:506
  41.0 3.7 %collective-permute-start.7 = (f32[32,128]{1,0:T(8,128)S(1)}, f32[32,128]{1,0:T(8,128)S(1)}, u32[]{:S(2)}, u32[]{:S(2)}) collective-permute-start(f32[32,128]{1,0:T(8,128)S(1)} %pad_maximum_fusion), channel_id=1, source_target_pairs={{0,4},{2,6},{4,0},{6,2},{8,12},{10,14},{12,8},{14,10},{1,5},{3,7},... | collective-permute-start | bytes 49160 | tf_op jit(solution)/shard_map/ppermute | solution.py:506
  41.5 3.2 %collective-permute-start.8 = (f32[32,128]{1,0:T(8,128)S(1)}, f32[32,128]{1,0:T(8,128)S(1)}, u32[]{:S(2)}, u32[]{:S(2)}) collective-permute-start(f32[32,128]{1,0:T(8,128)S(1)} %pad_maximum_fusion), channel_id=1, source_target_pairs={{0,0},{2,2},{4,8},{6,10},{8,4},{10,6},{12,12},{14,14},{1,1},{3,3},... | collective-permute-start | bytes 49160 | tf_op jit(solution)/shard_map/ppermute | solution.py:506
  45.9 1.6 %collective-permute-start.9 = (f32[2,56,512]{2,1,0:T(8,128)S(1)}, f32[2,56,512]{2,1,0:T(8,128)S(1)}, u32[]{:S(2)}, u32[]{:S(2)}) collective-permute-start(f32[2,56,512]{2,1,0:T(8,128)S(1)} %shard_map.157.refs_2_), channel_id=1, source_target_pairs={{0,1},{1,0},{2,3},{3,2},{4,5},{5,4},{6,7},{7,6},{8,9},{9,8},{10,11... | collective-permute-start | bytes 688136 | tf_op jit(solution)/shard_map/ppermute | solution.py:493
